TPU v7x, 256 devices: a whole 4x4x8 slice. The times are simulated.
256 devices in a mesh: shot: 16 (over x_hi, z), lag: 16 (over x_lo, y, core).
Axes of the slice: x: 4 (x_hi: 2, x_lo: 2; x = x_hi * 2 + x_lo), y: 4, z: 8, core: 2. Of those that a mesh axis runs over, the one named last changes fastest.
Arguments:
- traces: bfloat16 [96, 256, 8192], P('shot', 'lag'), may hold values from -64 to 64, as said below
- live_mask: int32 [96, 256], P('shot', 'lag'), may hold values 0 or 1
- gap_samples: int32 [1], replicated, may hold values from 1 to 32
Outputs:
- residual_traces: bfloat16 [96, 256, 8192], P('shot', 'lag')
Inputs may be any that keep to these rules, and one draw needn't show every extreme that they name: `traces`: recorded samples.
All inputs are finite; a program needn't handle non-finite values. No bound on the sum of `live_mask` on one device may be relied on, other than what follows from the above.
Results may differ from a plain program's by a relative error of at most 0.015.
The roundings to bfloat16 on the way count: a program that leaves them out, or rounds other values in their place, can miss the bound.
Values may be sent and summed in bfloat16 or wider, within the bound.
No kernel may reach another device: no remote copies, remote signals or barrier semaphores. Data moves between devices by JAX's collectives and lax.ppermute only.
A program may use at most 128 MiB of HBM per device.

v0:
```python
import jax
import jax.numpy as jnp
from jax import lax
from jax.sharding import PartitionSpec as P

LAGS = 4


def spread(x, axis, root):
    mine = lax.axis_index(axis) == root
    return lax.psum(jnp.where(mine, x, jnp.zeros_like(x)), axis)


def dft_table(first_row, row_count, samples, band_size):
    times_idx = jnp.arange(row_count, dtype=jnp.int32) + first_row
    harmonic = jnp.arange(1, band_size + 1, dtype=jnp.int32)
    phase = times_idx[:, None] * harmonic[None, :] % (2 * samples)
    angle = phase.astype(jnp.float32) * (jnp.pi / samples)
    return jnp.concatenate([jnp.cos(angle), jnp.sin(angle)], axis=1).astype(jnp.bfloat16)


def delay_tables(delays, samples, band_size):
    harmonic = jnp.arange(1, band_size + 1, dtype=jnp.int32)
    phase = delays[:, None] * harmonic[None, :] % (2 * samples)
    angle = phase.astype(jnp.float32) * (jnp.pi / samples)
    return (jnp.cos(angle), jnp.sin(angle))


def delay_apply(spectrum, cosine, sine):
    band_size = cosine.shape[-1]
    real_part = spectrum[..., :band_size]
    imag_part = spectrum[..., band_size:]
    return jnp.concatenate(
        [real_part * cosine - imag_part * sine, imag_part * cosine + real_part * sine], axis=-1
    )


def shards(traces, live_mask, gap_samples):
    shot_count, local_chan, samples = traces.shape
    band_size = samples // 16
    block_len = min(1024, samples)
    live_bf = live_mask.astype(jnp.bfloat16)
    masked = traces * live_bf[:, :, None]
    running = jnp.zeros((shot_count, local_chan, 2 * band_size), jnp.float32)
    for offset in range(0, samples, block_len):
        table = dft_table(offset, block_len, samples, band_size)
        running = running + jnp.einsum(
            "sct,tw->scw",
            masked[:, :, offset : offset + block_len],
            table,
            preferred_element_type=jnp.float32,
        )
    own_spec = running.astype(jnp.bfloat16)
    all_spec = lax.all_gather(own_spec, "lag", axis=1, tiled=True)
    spacing = samples // (2 * band_size)
    tap_delays = jnp.arange(LAGS, dtype=jnp.int32) * spacing
    lag_list = jnp.concatenate([tap_delays, gap_samples[0] + tap_delays])
    cosine, sine = delay_tables(lag_list, samples, band_size)
    rotated = delay_apply(
        own_spec.astype(jnp.float32)[None], cosine[:, None, None, :], sine[:, None, None, :]
    ).astype(jnp.bfloat16)
    partial_value = jnp.einsum(
        "ksaf,sbf->kab", rotated, all_spec, preferred_element_type=jnp.float32
    )
    summed = lax.psum(partial_value, "shot")
    total_shots = shot_count * lax.axis_size("shot")
    gathered = lax.all_gather(summed, "lag", axis=1, tiled=True)
    correlation = gathered * (1.0 / samples) * (1.0 / (samples * total_shots))
    channels = correlation.shape[1]
    whiten = 0.1 * jnp.mean(jnp.diagonal(correlation[0])) + 1e-06
    zero_lag = correlation[0] + whiten * jnp.eye(channels, dtype=jnp.float32)
    weighted = jnp.concatenate([zero_lag[None], correlation[1:]], axis=0)
    lag_index = lax.axis_index("lag")
    first_out = lag_index * local_chan
    rhs = jnp.concatenate(
        [
            lax.dynamic_slice(weighted[LAGS + row_block], (0, first_out), (channels, local_chan))
            for row_block in range(LAGS)
        ],
        axis=0,
    )
    lag_devices = lax.axis_size("lag")
    per_dev = LAGS * channels // lag_devices
    groups = lag_devices // LAGS
    first_col = lag_index * per_dev
    col_block = first_col // channels
    col_offset = first_col % channels
    slabs = []
    for row_block in range(LAGS):
        distance = row_block - col_block
        magnitude = jnp.abs(distance)
        below = lax.dynamic_slice(weighted, (magnitude, 0, col_offset), (1, channels, per_dev))[0]
        above = lax.dynamic_slice(weighted, (magnitude, col_offset, 0), (1, per_dev, channels))[0].T
        slabs.append(jnp.where(distance >= 0, below, above))
    matrix = jnp.concatenate([jnp.concatenate(slabs, axis=0), rhs], axis=1)
    for col_section in range(LAGS):
        pieces = [
            spread(matrix[:, :per_dev], "lag", col_section * groups + sender)
            for sender in range(groups)
        ]
        column = jnp.concatenate(pieces, axis=1)
        top_row = col_section * channels
        pivot_block = column[top_row : top_row + channels]
        lower_factor = jnp.linalg.cholesky(pivot_block)
        solved = jax.scipy.linalg.cho_solve(
            (lower_factor, True), matrix[top_row : top_row + channels]
        )
        matrix = matrix - jnp.dot(column, solved, precision=lax.Precision.HIGHEST)
        matrix = lax.dynamic_update_slice(matrix, solved, (top_row, 0))
    filter_own = matrix[:, per_dev:]
    filter_bf = filter_own.astype(jnp.bfloat16).reshape(LAGS, channels, local_chan)
    mixed = jnp.einsum("jab,saf->jsbf", filter_bf, all_spec, preferred_element_type=jnp.float32)
    shifted = delay_apply(mixed, cosine[LAGS:, None, None, :], sine[LAGS:, None, None, :])
    predicted = jnp.sum(shifted, axis=0)
    error = (own_spec.astype(jnp.float32) - predicted).astype(jnp.bfloat16)
    live_float = live_bf.astype(jnp.float32)[:, :, None]
    outputs = []
    for offset in range(0, samples, block_len):
        table = dft_table(offset, block_len, samples, band_size)
        restored = jnp.einsum("scw,tw->sct", error, table, preferred_element_type=jnp.float32)
        outputs.append((restored * (1.0 / samples) * live_float).astype(jnp.bfloat16))
    return jnp.concatenate(outputs, axis=2)


def solution(mesh):
    placed = (P("shot", "lag", None), P("shot", "lag"), P())
    return jax.shard_map(
        shards, mesh=mesh, in_specs=placed, out_specs=P("shot", "lag", None), check_vma=False
    )
```

profile of v0, /device:TPU:1, one launch (start us, length us, event | category | flops | bytes accessed | tf_op | source)
XLA Modules:
  0.0 1142.9 jit_solution(256592052149196447)
XLA Ops:
  9.4 67.7 %cosine_convert_fusion = (bf16[1024,512]{1,0:T(8,128)(2,1)S(1)}, bf16[1024,512]{1,0:T(8,128)(2,1)S(1)}, bf16[1024,512]{1,0:T(8,128)(2,1)S(1)}, bf16[1024,512]{1,...) fusion(s32[512]{0:T(512)S(1)} %iota_add_fusion.7, ...), kind=kLoop, calls=%fused_computation.100 | loop fusion | flops 67108864 | bytes 16807936 | tf_op jit(solution)/shard_map/convert.3
  86.7 40.3 %all-gather.3.cloned.1.call-done = bf16[6,256,1024]{2,1,0:T(8,128)(2,1)} async-done(((bf16[6,16,1024]{2,1,0:T(8,128)(2,1)}), bf16[6,256,1024]{2,1,0:T(8,128)(2,1)}) %all-gather.3.cloned.1.call-update) | async-done | bytes 3145744 | tf_op jit(solution)/shard_map/all_gather | solution.py:54
  127.0 3.7 fusion.85
  130.8 144.3 %all-reduce.11.cloned.1.call-done = f32[8,16,256]{2,1,0:T(8,128)} async-done(((f32[8,16,256]{2,1,0:T(8,128)}), f32[8,16,256]{2,1,0:T(8,128)}) %all-reduce.11.cloned.1.call-update) | async-done | bytes 131088 | tf_op jit(solution)/shard_map/psum | solution.py:65
  275.3 45.7 %all-gather.5.cloned.1.call-done = f32[8,256,256]{2,1,0:T(8,128)} async-done(((f32[8,16,256]{2,1,0:T(8,128)}), f32[8,256,256]{2,1,0:T(8,128)}) %all-gather.5.cloned.1.call-update) | async-done | bytes 2097168 | tf_op jit(solution)/shard_map/all_gather | solution.py:67
  324.1 2.3 gather_fusion
  336.7 123.6 %all-reduce.19.cloned.1.call-done = (f32[1024,64]{0,1:T(8,128)}, f32[1024,64]{0,1:T(8,128)}, f32[1024,64]{0,1:T(8,128)}, f32[1024,64]{0,1:T(8,128)}) async-done(((f32[1024,64]{0,1:T(8,128)}, f32[1024,64]{0,1:T(8,128)}, f32[1024,64]{0,1:T(8,128)}, f32[1024,64]{0,1:T(8,128)}), (f32[1024,64]{0,1:T(8,128)}, f32[1024,64]{0,1:T(8,128)}, f32[1024,64]{0,1:T(8,128)}, ...) | async-done | bytes 1048592 | tf_op jit(solution)/shard_map/psum | solution.py:11
  464.4 11.7 %cholesky.214 = f32[128,128]{1,0:T(8,128)S(1)} custom-call(f32[128,128]{1,0:T(8,128)S(1)} %cholesky.346), custom_call_target="Cholesky" | custom-call | tf_op jit(solution)/shard_map/jit(cholesky)/cholesky | solution.py:104
  476.2 9.8 custom-call.21
  486.4 11.7 %cholesky.231 = f32[128,128]{1,0:T(8,128)S(1)} custom-call(f32[128,128]{1,0:T(8,128)S(1)} %convolution_subtract_fusion.7), custom_call_target="Cholesky" | custom-call | tf_op jit(solution)/shard_map/jit(cholesky)/cholesky | solution.py:104
  500.8 4.2 while.8
  505.1 19.7 %custom-call.22 = f32[2,128,128]{1,2,0:T(8,128)S(1)} custom-call(f32[2,128,128]{2,1,0:T(8,128)S(1)} %get-tuple-element.33), custom_call_target="InvertDiagBlocksLowerTriangular" | custom-call | tf_op jit(solution)/shard_map/jit(_cho_solve)/triangular_solve | solution.py:105
  528.1 126.0 %all-reduce.17.cloned.1.call-done = (f32[1024,64]{0,1:T(8,128)}, f32[1024,64]{0,1:T(8,128)}, f32[1024,64]{0,1:T(8,128)}, f32[1024,64]{0,1:T(8,128)}) async-done(((f32[1024,64]{0,1:T(8,128)}, f32[1024,64]{0,1:T(8,128)}, f32[1024,64]{0,1:T(8,128)}, f32[1024,64]{0,1:T(8,128)}), (f32[1024,64]{0,1:T(8,128)}, f32[1024,64]{0,1:T(8,128)}, f32[1024,64]{0,1:T(8,128)}, ...) | async-done | bytes 1048592 | tf_op jit(solution)/shard_map/psum | solution.py:11
  658.2 11.7 %cholesky.248 = f32[128,128]{1,0:T(8,128)S(1)} custom-call(f32[128,128]{1,0:T(8,128)S(1)} %cholesky.349), custom_call_target="Cholesky" | custom-call | tf_op jit(solution)/shard_map/jit(cholesky)/cholesky | solution.py:104
  670.0 9.8 custom-call.23
  680.3 11.7 %cholesky.265 = f32[128,128]{1,0:T(8,128)S(1)} custom-call(f32[128,128]{1,0:T(8,128)S(1)} %convolution_subtract_fusion.6), custom_call_target="Cholesky" | custom-call | tf_op jit(solution)/shard_map/jit(cholesky)/cholesky | solution.py:104
  694.6 4.0 while.9
  698.6 19.7 %custom-call.24 = f32[2,128,128]{1,2,0:T(8,128)S(1)} custom-call(f32[2,128,128]{2,1,0:T(8,128)S(1)} %get-tuple-element.34), custom_call_target="InvertDiagBlocksLowerTriangular" | custom-call | tf_op jit(solution)/shard_map/jit(_cho_solve)/triangular_solve | solution.py:105
  721.7 126.2 %all-reduce.15.cloned.1.call-done = (f32[1024,64]{0,1:T(8,128)}, f32[1024,64]{0,1:T(8,128)}, f32[1024,64]{0,1:T(8,128)}, f32[1024,64]{0,1:T(8,128)}) async-done(((f32[1024,64]{0,1:T(8,128)}, f32[1024,64]{0,1:T(8,128)}, f32[1024,64]{0,1:T(8,128)}, f32[1024,64]{0,1:T(8,128)}), (f32[1024,64]{0,1:T(8,128)}, f32[1024,64]{0,1:T(8,128)}, f32[1024,64]{0,1:T(8,128)}, ...) | async-done | bytes 1048592 | tf_op jit(solution)/shard_map/psum | solution.py:11
  851.9 11.7 %cholesky.282 = f32[128,128]{1,0:T(8,128)S(1)} custom-call(f32[128,128]{1,0:T(8,128)S(1)} %cholesky.352), custom_call_target="Cholesky" | custom-call | tf_op jit(solution)/shard_map/jit(cholesky)/cholesky | solution.py:104
  863.7 9.8 custom-call.25
  874.0 11.7 %cholesky.299 = f32[128,128]{1,0:T(8,128)S(1)} custom-call(f32[128,128]{1,0:T(8,128)S(1)} %convolution_subtract_fusion.5), custom_call_target="Cholesky" | custom-call | tf_op jit(solution)/shard_map/jit(cholesky)/cholesky | solution.py:104
  888.3 3.8 while.10
  892.1 20.1 %custom-call.26 = f32[2,128,128]{1,2,0:T(8,128)S(1)} custom-call(f32[2,128,128]{2,1,0:T(8,128)S(1)} %get-tuple-element.35), custom_call_target="InvertDiagBlocksLowerTriangular" | custom-call | tf_op jit(solution)/shard_map/jit(_cho_solve)/triangular_solve | solution.py:105
  915.6 126.0 %all-reduce.13.cloned.1.call-done = (f32[1024,64]{0,1:T(8,128)}, f32[1024,64]{0,1:T(8,128)}, f32[1024,64]{0,1:T(8,128)}, f32[1024,64]{0,1:T(8,128)}) async-done(((f32[1024,64]{0,1:T(8,128)}, f32[1024,64]{0,1:T(8,128)}, f32[1024,64]{0,1:T(8,128)}, f32[1024,64]{0,1:T(8,128)}), (f32[1024,64]{0,1:T(8,128)}, f32[1024,64]{0,1:T(8,128)}, f32[1024,64]{0,1:T(8,128)}, ...) | async-done | bytes 1048592 | tf_op jit(solution)/shard_map/psum | solution.py:11
  1045.7 11.7 %cholesky.316 = f32[128,128]{1,0:T(8,128)S(1)} custom-call(f32[128,128]{1,0:T(8,128)S(1)} %cholesky.355), custom_call_target="Cholesky" | custom-call | tf_op jit(solution)/shard_map/jit(cholesky)/cholesky | solution.py:104
  1057.5 9.8 custom-call.27
  1067.8 11.7 %cholesky.333 = f32[128,128]{1,0:T(8,128)S(1)} custom-call(f32[128,128]{1,0:T(8,128)S(1)} %convolution_subtract_fusion.4), custom_call_target="Cholesky" | custom-call | tf_op jit(solution)/shard_map/jit(cholesky)/cholesky | solution.py:104
  1084.6 7.0 while.11
  1085.3 2.8 bitcast_dynamic-update-slice_fusion.11
  1088.8 2.8 bitcast_dynamic-update-slice_fusion.11
  1091.5 21.1 %custom-call.28 = f32[2,128,128]{1,2,0:T(8,128)} custom-call(f32[2,128,128]{2,1,0:T(8,128)} %get-tuple-element.36), custom_call_target="InvertDiagBlocksLowerTriangular" | custom-call | tf_op jit(solution)/shard_map/jit(_cho_solve)/triangular_solve | solution.py:105
  (287 shorter events, 96.0 us)
Async XLA Ops:
  6.5 120.5 %all-gather.3.cloned.1.call-start = ((), (), s32[]{:S(2)}) async-start(), calls=%async_computation | async-start | bytes 3342336 | tf_op jit(solution)/shard_map/all_gather | solution.py:54
  77.2 1.6 copy-start.21
  77.2 2.1 copy-start.25
  77.2 2.1 copy-start.27
  77.2 2.3 copy-start.29
  77.2 2.6 copy-start.31
  77.2 3.0 copy-start.33
  77.2 3.3 copy-start.35
  77.3 3.6 copy-start.17
  77.3 3.9 copy-start.19
  77.3 4.3 copy-start.13
  77.3 4.5 copy-start.15
  77.3 4.9 copy-start.9
  77.3 5.0 copy-start.11
  77.3 5.5 copy-start.5
  77.3 5.7 copy-start.7
  84.2 191.0 %all-reduce.11.cloned.1.call-start = ((), (), s32[]{:S(2)}) async-start(), calls=%async_computation.1 | async-start | bytes 262144 | tf_op jit(solution)/shard_map/psum | solution.py:65
  85.3 45.4 %copy-start.39 = (f32[8,512]{1,0:T(8,128)}, f32[8,512]{1,0:T(8,128)S(1)}, u32[]{:S(2)}) copy-start(f32[8,512]{1,0:T(8,128)S(1)} %get-tuple-element.158) | copy-start | bytes 49156
  130.8 190.2 %all-gather.5.cloned.1.call-start = ((), (), s32[]{:S(2)}) async-start(), calls=%async_computation.2 | async-start | bytes 2228224 | tf_op jit(solution)/shard_map/all_gather | solution.py:67
  275.2 185.1 %all-reduce.19.cloned.1.call-start = ((), (), s32[]{:S(2)}) async-start(), calls=%async_computation.6 | async-start | bytes 2097152 | tf_op jit(solution)/shard_map/psum | solution.py:11
  332.4 1.7 copy-start.37
  335.9 318.2 %all-reduce.17.cloned.1.call-start = ((), (), s32[]{:S(2)}) async-start(), calls=%async_computation.5 | async-start | bytes 2097152 | tf_op jit(solution)/shard_map/psum | solution.py:11
  528.1 319.7 %all-reduce.15.cloned.1.call-start = ((), (), s32[]{:S(2)}) async-start(), calls=%async_computation.4 | async-start | bytes 2097152 | tf_op jit(solution)/shard_map/psum | solution.py:11
  721.6 320.0 %all-reduce.13.cloned.1.call-start = ((), (), s32[]{:S(2)}) async-start(), calls=%async_computation.3 | async-start | bytes 2097152 | tf_op jit(solution)/shard_map/psum | solution.py:11
  913.7 1.9 copy-start.40
  1045.5 36.6 %copy-start.2 = (f32[1024,256]{0,1:T(8,128)}, f32[1024,256]{0,1:T(8,128)S(1)}, u32[]{:S(2)}) copy-start(f32[1024,256]{0,1:T(8,128)S(1)} %constant_dynamic-update-slice_fusion.12) | copy-start | bytes 3145732
  1079.5 2.5 copy-start.4
  1082.1 39.1 %copy-start.1 = (bf16[6,256,1024]{2,1,0:T(8,128)(2,1)S(1)}, bf16[6,256,1024]{2,1,0:T(8,128)(2,1)}, u32[]{:S(2)}) copy-start(bf16[6,256,1024]{2,1,0:T(8,128)(2,1)} %all-gather.3.cloned.1.call-done) | copy-start | bytes 9437188
  1123.1 1.6 copy-start.30
  1123.1 1.7 copy-start.32
  1132.5 1.9 copy-start.6
  1132.5 1.9 copy-start.8
  (18 other events, 24.1 us)
Sparse Core Ops, SparseCore 0:
  84.3 42.6 all-gather.2
  130.9 144.2 all-reduce.10
  277.1 43.8 all-gather.4
  336.0 124.2 all-reduce.18
  528.2 125.8 all-reduce.16
  721.7 126.0 all-reduce.14
  915.7 125.8 all-reduce.12
where the time goes:
time: 1150 us; the launch traced here: 1140 us
  waiting for transfers between devices  732 us (64%)
  other arithmetic  304 us (26%)
  local copies, waits for them, and re-layouts  51.3 us (4%)
  matrix products  32.9 us (3%)
  between operations  21.1 us (2%)
    psum x4, waiting for transfers between devices, spread(): return lax.psum(jnp.where(mine, x, jnp.zeros_like(x)), axis)  502 us
    psum x1, waiting for transfers between devices, shards(): summed = lax.psum(partial_value, 'shot')  144 us
    another operation x28, other arithmetic, shards(): lower_factor = jnp.linalg.cholesky(pivot_block)  138 us
    another operation x9, other arithmetic, shards(): jax.scipy.linalg.cho_solve((lower_factor, True), matrix[top_row:top_row +...  82.4 us
    another operation x2, other arithmetic  68.2 us
    all_gather x1, waiting for transfers between devices, shards(): gathered = lax.all_gather(summed, 'lag', axis=1, tiled=True)  45.7 us
    all_gather x1, waiting for transfers between devices, shards(): all_spec = lax.all_gather(own_spec, 'lag', axis=1, tiled=True)  40.3 us
  transfers between devices with their start and end apart: 7, of which 7 were waited for; matrix products, arithmetic and copies ran while one was open for 0% of the time, Pallas kernels for 0%

commit v1 on v0

v1 whole, which is shorter than its diff:
```python
import jax
import jax.numpy as jnp
from jax import lax
from jax.experimental import pallas as pl
from jax.experimental.pallas import tpu as pltpu
from jax.sharding import PartitionSpec as P

LAGS = 4
CHUNK = 1024
FINE = 128
f32 = jnp.float32
bf = jnp.bfloat16
VM = pl.BlockSpec(memory_space=pltpu.VMEM)


def wave(times, samples, band_size):
    harmonic = jnp.arange(1, band_size + 1, dtype=jnp.int32)
    phase = times[:, None] * harmonic[None, :] % (2 * samples)
    angle = phase.astype(f32) * (jnp.pi / samples)
    return jnp.cos(angle), jnp.sin(angle)

def forward_kernel(x_ref, live_ref, cc_ref, cs_ref, fc_ref, fs_ref, spec_ref, table_ref, acc):
    step = pl.program_id(0)
    chunk, width = table_ref.shape
    band = width // 2
    fine = fc_ref.shape[0]
    rows = acc.shape[0]
    for r in range(chunk // fine):
        h = step * (chunk // fine) + r
        cc = cc_ref[pl.ds(h, 1), :]
        cs = cs_ref[pl.ds(h, 1), :]
        at = slice(r * fine, (r + 1) * fine)
        table_ref[at, :band] = (cc * fc_ref[...] - cs * fs_ref[...]).astype(bf)
        table_ref[at, band:] = (cs * fc_ref[...] + cc * fs_ref[...]).astype(bf)
    part = jnp.dot(x_ref[...].reshape(rows, chunk), table_ref[...], preferred_element_type=f32)

    @pl.when(step == 0)
    def _():
        acc[...] = part

    @pl.when(step > 0)
    def _():
        acc[...] += part

    @pl.when(step == pl.num_programs(0) - 1)
    def _():
        spec_ref[...] = (acc[...] * live_ref[...]).astype(bf)

def forward(traces, live):
    shots, chans, samples = traces.shape
    band = samples // 16
    rows = shots * chans
    cc, cs = wave(jnp.arange(samples // FINE, dtype=jnp.int32) * FINE, samples, band)
    fc, fs = wave(jnp.arange(FINE, dtype=jnp.int32), samples, band)
    return pl.pallas_call(
        forward_kernel, grid=(samples // CHUNK,),
        out_shape=(jax.ShapeDtypeStruct((rows, 2 * band), bf), jax.ShapeDtypeStruct((samples, 2 * band), bf)),
        in_specs=[pl.BlockSpec((shots, chans, CHUNK), lambda i: (0, 0, i)), VM, VM, VM, VM, VM],
        out_specs=(pl.BlockSpec((rows, 2 * band), lambda i: (0, 0)), pl.BlockSpec((CHUNK, 2 * band), lambda i: (i, 0))),
        scratch_shapes=[pltpu.VMEM((rows, 2 * band), f32)],
        compiler_params=pltpu.CompilerParams(vmem_limit_bytes=40 * 2**20),
    )(traces, live.reshape(rows, 1), cc, cs, fc, fs)

def inverse_kernel(filter_ref, all_ref, own_ref, cos_ref, sin_ref, live_ref, table_ref, out_ref, error):
    shots, chans, chunk = out_ref.shape
    band = cos_ref.shape[1]

    @pl.when(pl.program_id(0) == 0)
    def _():
        weights = filter_ref[...].reshape(LAGS * chans, filter_ref.shape[2])
        for s in range(shots):
            mixed = jnp.dot(weights, all_ref[s], preferred_element_type=f32)
            even = jnp.zeros((chans, band), f32)
            odd = jnp.zeros((chans, band), f32)
            for j in range(LAGS):
                part = mixed[j * chans : (j + 1) * chans]
                c, n = cos_ref[j : j + 1, :], sin_ref[j : j + 1, :]
                even = even + (part[:, :band] * c - part[:, band:] * n)
                odd = odd + (part[:, band:] * c + part[:, :band] * n)
            at = slice(s * chans, (s + 1) * chans)
            error[at, :band] = (own_ref[at, :band].astype(f32) - even).astype(bf)
            error[at, band:] = (own_ref[at, band:].astype(f32) - odd).astype(bf)

    restored = lax.dot_general(error[...], table_ref[...], (((1,), (1,)), ((), ())), preferred_element_type=f32)
    samples = pl.num_programs(0) * chunk
    out_ref[...] = (restored * (1.0 / samples) * live_ref[...]).astype(bf).reshape(out_ref.shape)

def inverse(filter_bf, all_spec, own_spec, cosine, sine, live, table):
    shots, channels, width = all_spec.shape
    chans = filter_bf.shape[1]
    samples = table.shape[0]
    rows = shots * chans
    return pl.pallas_call(
        inverse_kernel, grid=(samples // CHUNK,),
        out_shape=jax.ShapeDtypeStruct((shots, chans, samples), bf),
        in_specs=[VM, VM, VM, VM, VM, VM, pl.BlockSpec((CHUNK, width), lambda i: (i, 0))],
        out_specs=pl.BlockSpec((shots, chans, CHUNK), lambda i: (0, 0, i)),
        scratch_shapes=[pltpu.VMEM((rows, width), bf)],
        compiler_params=pltpu.CompilerParams(vmem_limit_bytes=40 * 2**20),
    )(filter_bf, all_spec, own_spec, cosine, sine, live.reshape(rows, 1), table)


def delay_apply(spectrum, cosine, sine):
    band_size = cosine.shape[-1]
    real_part = spectrum[..., :band_size]
    imag_part = spectrum[..., band_size:]
    return jnp.concatenate(
        [real_part * cosine - imag_part * sine, imag_part * cosine + real_part * sine], axis=-1
    )


def invert_128(groups):
    lane = lax.broadcasted_iota(jnp.int32, (8, 128), 1)
    sub = lax.broadcasted_iota(jnp.int32, (8, 128), 0)
    groups = list(groups)
    for s in range(16):
        lo = 8 * s
        inside = (lane >= lo) & (lane < lo + 8)
        rows = groups[s]
        entry = {}
        for j in range(8):
            for i in range(j, 8):
                entry[i, j] = jnp.broadcast_to(rows[i:i+1, lo+j:lo+j+1], (8, 128))
        unit = jnp.where(lane - lo == sub, 1.0, 0.0)
        start = jnp.where(inside, unit, rows)
        y = [jnp.broadcast_to(start[j:j+1, :], (8, 128)) for j in range(8)]
        low = {}
        dinv = []
        for j in range(8):
            d = 1.0 / entry[j, j]
            dinv.append(d)
            for i in range(j + 1, 8):
                low[i, j] = entry[i, j] * d
            for i in range(j + 1, 8):
                for k in range(j + 1, i + 1):
                    entry[i, k] = entry[i, k] - low[i, j] * entry[k, j]
                y[i] = y[i] - low[i, j] * y[j]
        v = [None] * 8
        for j in reversed(range(8)):
            t = y[j] * dinv[j]
            for i in range(j + 1, 8):
                t = t - low[i, j] * v[i]
            v[j] = t
        order = [(s + 1 + g) % 16 for g in range(15)]
        for g in order:
            x = groups[g]
            t = jnp.where(inside, 0.0, x)
            for j in range(8):
                t = t - jnp.broadcast_to(x[:, lo+j:lo+j+1], (8, 128)) * v[j]
            groups[g] = t
        t = v[0]
        for j in range(1, 8):
            t = jnp.where(sub == j, v[j], t)
        groups[s] = t
    return groups


def mm(a, b, ca=1, cb=0):
    return lax.dot_general(a, b, (((ca,), (cb,)), ((), ())), precision=lax.Precision.HIGHEST, preferred_element_type=f32)

def solve_kernel(corr_ref, rhs_ref, out_ref, tiles, gains, ys, block, whole):
    n = corr_ref.shape[1]
    h = n // 2
    eye = lax.broadcasted_iota(jnp.int32, (n, n), 0) == lax.broadcasted_iota(jnp.int32, (n, n), 1)
    zero_lag = corr_ref[0]
    whiten = 0.1 * jnp.sum(jnp.where(eye, zero_lag, 0.0)) / n + 1e-06
    zero_lag = zero_lag + jnp.where(eye, whiten, 0.0)
    for i in range(LAGS):
        tiles[i, i] = zero_lag
        for j in range(i):
            tiles[i, j] = corr_ref[i - j]
        ys[i] = rhs_ref[i]
    block[...] = zero_lag[:h, :h]

    def first_half(p):
        inv = block[...]
        corner = tiles[p, p, h:, :h]
        left = mm(corner, inv)
        whole[:h, :h] = inv
        whole[h:, :h] = left
        block[...] = tiles[p, p, h:, h:] - mm(left, corner, 1, 1)

    def second_half(p):
        inv = block[...]
        left = whole[h:, :h]
        low = mm(inv, left)
        whole[:h, :h] += mm(left, low, 0, 0)
        whole[h:, :h] = -low
        whole[:h, h:] = -low.T
        whole[h:, h:] = inv
        full = whole[...]
        for i in range(p + 1, LAGS):
            gains[i, p] = mm(tiles[i, p], full)
            for j in range(p + 1, i + 1):
                tiles[i, j] -= mm(gains[i, p], tiles[j, p], 1, 1)
        if p + 1 < LAGS:
            block[...] = tiles[p + 1, p + 1, :h, :h]
        y = mm(ys[p], full)
        ys[p] = y
        for j in range(p + 1, LAGS):
            ys[j] -= mm(y, tiles[j, p], 1, 1)

    def step(q, carry):
        even = 0.5 * (block[...] + block[...].T)
        groups = invert_128([even[8 * i : 8 * i + 8, :] for i in range(16)])
        for i in range(16):
            block[8 * i : 8 * i + 8, :] = groups[i]
        for p in range(LAGS):
            pl.when(q == 2 * p)(lambda p=p: first_half(p))
            pl.when(q == 2 * p + 1)(lambda p=p: second_half(p))
        return carry

    lax.fori_loop(0, 2 * LAGS, step, 0)
    for p in reversed(range(LAGS)):
        x = ys[p]
        for j in range(p + 1, LAGS):
            x = x - mm(ys[j], gains[j, p])
        ys[p] = x
        out_ref[p] = x.astype(out_ref.dtype)

def solve_filter(corr, rhs):
    n = corr.shape[1]; m = rhs.shape[1]; h = n // 2
    vm = pl.BlockSpec(memory_space=pltpu.VMEM)
    return pl.pallas_call(solve_kernel, out_shape=jax.ShapeDtypeStruct((LAGS, m, n), jnp.bfloat16), in_specs=[vm, vm], out_specs=vm,
        scratch_shapes=[pltpu.VMEM((LAGS, LAGS, n, n), f32), pltpu.VMEM((LAGS, LAGS, n, n), f32), pltpu.VMEM((LAGS, m, n), f32), pltpu.VMEM((h, h), f32), pltpu.VMEM((n, n), f32)],
        compiler_params=pltpu.CompilerParams(vmem_limit_bytes=40 * 2**20))(corr, rhs)


def gather_all(x, axis):
    parts = lax.axis_size(axis)
    return lax.all_to_all(
        jnp.broadcast_to(x[None], (parts,) + x.shape), axis, split_axis=0, concat_axis=0, tiled=True
    )


def sum_over(x, axis):
    parts = lax.axis_size(axis)
    rows = x.shape[0] // parts
    split = x.reshape((parts, rows) + x.shape[1:])
    swapped = lax.all_to_all(split, axis, split_axis=0, concat_axis=0, tiled=True)
    return gather_all(jnp.sum(swapped, axis=0), axis).reshape(x.shape)


def shards(traces, live_mask, gap_samples):
    shot_count, local_chan, samples = traces.shape
    band_size = samples // 16
    live = live_mask.astype(f32)
    own_rows, table = forward(traces, live)
    own_spec = own_rows.reshape(shot_count, local_chan, 2 * band_size)
    all_spec = lax.all_gather(own_spec, "lag", axis=1, tiled=True)
    spacing = samples // (2 * band_size)
    tap_delays = jnp.arange(LAGS, dtype=jnp.int32) * spacing
    lag_list = jnp.concatenate([tap_delays, gap_samples[0] + tap_delays])
    cosine, sine = wave(lag_list, samples, band_size)
    turn = jnp.where(jnp.arange(2 * LAGS) < LAGS, 1.0, -1.0).astype(f32)[:, None]
    rotated = delay_apply(
        own_spec.astype(f32)[None], cosine[:, None, None, :], (turn * sine)[:, None, None, :]
    ).astype(jnp.bfloat16)
    partial_value = jnp.einsum("ksaf,sbf->kab", rotated, all_spec, preferred_element_type=f32)
    channels = all_spec.shape[1]
    total_shots = shot_count * lax.axis_size("shot")
    summed = sum_over(partial_value.reshape(2 * LAGS * local_chan, channels), "shot")
    summed = summed * (1.0 / samples) * (1.0 / (samples * total_shots))
    summed = summed.reshape(2 * LAGS, local_chan, channels)
    gathered = gather_all(summed[:LAGS], "lag")
    correlation = jnp.swapaxes(gathered, 0, 1).reshape(LAGS, channels, channels)
    filter_bf = solve_filter(correlation, summed[LAGS:])
    return inverse(filter_bf, all_spec, own_rows, cosine[LAGS:], sine[LAGS:], live, table)


def solution(mesh):
    placed = (P("shot", "lag", None), P("shot", "lag"), P())
    return jax.shard_map(
        shards, mesh=mesh, in_specs=placed, out_specs=P("shot", "lag", None), check_vma=False
    )
```

time: 1150 us -> 188 us (0.16)
  waiting for transfers between devices: 732 us -> 56.4 us
  other arithmetic: 304 us -> 3.96 us
  Pallas kernels: 0 us -> 71.2 us
  local copies, waits for them, and re-layouts: 51.3 us -> 2.73 us
  blocking collectives: 0 us -> 30.4 us
  matrix products: 32.9 us -> 3.04 us
    psum x5 -> x0, waiting for transfers between devices: 646 us -> none  [the longest x4 502 us: spread(): return lax.psum(jnp.where(mine, x, jnp.zeros_like(x)), axis)]
    another operation x39 -> x1, other arithmetic: 289 us -> 0.42 us  [the longest x28 138 us: shards(): lower_factor = jnp.linalg.cholesky(pivot_block)]
    pallas_call x0 -> x3, Pallas kernels: none -> 71.2 us  [the longest x1 48.9 us: solve_filter(): pl.pallas_call(solve_kernel, out_shape=jax.ShapeDtypeStruct((LAGS, m, n),...]
    all_gather x1 -> x0, waiting for transfers between devices: 45.7 us -> none  [shards(): gathered = lax.all_gather(summed, 'lag', axis=1, tiled=True)]
    all_to_all x0 -> x2, blocking collectives: none -> 30.4 us  [the longest x1 17.6 us: sum_over(): lax.all_to_all(split, axis, split_axis=0, concat_axis=0, tiled=True)]
    unnamed x98 -> x4, local copies, waits for them, and re-layouts: 21.5 us -> 1.41 us
    another operation x37 -> x0, local copies, waits for them, and re-layouts: 19 us -> none  [the longest x29 18.9 us: shards(): jax.scipy.linalg.cho_solve((lower_factor, True), matrix[top_row:top_row +...]
    dot_general x22 -> x1, matrix products: 20.2 us -> 3.04 us  [shards(): jnp.einsum('ksaf,sbf->kab', rotated, all_spec, preferred_element_type=f32)]
  transfers between devices with their start and end apart: 7 -> 2, of which waited for: 7 -> 2; matrix products, arithmetic and copies ran while one was open for 0% -> 1% of each run, Pallas kernels for 0% -> 0%
where the time goes in v1:
time: 188 us
  Pallas kernels  71.2 us (38%)
  waiting for transfers between devices  56.4 us (30%)
  blocking collectives  30.4 us (16%)
  between operations  14.2 us (8%)
  starting transfers between devices  5.89 us (3%)
  other arithmetic  3.96 us (2%)
  matrix products  3.04 us (2%)
  local copies, waits for them, and re-layouts  2.73 us (1%)
    pallas_call x1, Pallas kernels, solve_filter(): pl.pallas_call(solve_kernel, out_shape=jax.ShapeDtypeStruct((LAGS, m, n),...  48.9 us
    all_gather x1, waiting for transfers between devices, shards(): all_spec = lax.all_gather(own_spec, 'lag', axis=1, tiled=True)  40.5 us
    all_to_all x1, blocking collectives, sum_over(): lax.all_to_all(split, axis, split_axis=0, concat_axis=0, tiled=True)  17.6 us
    all_to_all x1, waiting for transfers between devices, gather_all(): lax.all_to_all(jnp.broadcast_to(x[None], (parts,) + x.shape), axis, split...  15.8 us
    all_to_all x1, blocking collectives, gather_all(): lax.all_to_all(jnp.broadcast_to(x[None], (parts,) + x.shape), axis, split...  12.8 us
    pallas_call x1, Pallas kernels, inverse(): pl.pallas_call(inverse_kernel, grid=(samples // CHUNK,), out_shape=jax.Sh...  12.4 us
    pallas_call x1, Pallas kernels, forward(): pl.pallas_call(forward_kernel, grid=(samples // CHUNK,), out_shape=(jax.S...  9.86 us
    all_to_all x1, starting transfers between devices, gather_all(): lax.all_to_all(jnp.broadcast_to(x[None], (parts,) + x.shape), axis, split...  5.89 us
  transfers between devices with their start and end apart: 2, of which 2 were waited for; matrix products, arithmetic and copies ran while one was open for 1% of the time, Pallas kernels for 0%

profile of v1, /device:TPU:1, one launch (start us, length us, event | category | flops | bytes accessed | tf_op | source)
XLA Modules:
  0.0 187.8 jit_solution(13771285852388371184)
XLA Ops:
  6.5 0.0 all-gather.2.cloned.1.call-start
  6.5 0.7 convert_element_type.37
  7.2 0.1 reshape.124.live_ref
  7.3 1.0 fusion.14
  8.4 0.6 fusion.16
  9.0 0.0 copy-start.1
  9.0 1.4 copy-done.1
  10.4 9.9 %shard_map.37 = (bf16[96,1024]{1,0:T(8,128)(2,1)}, bf16[8192,1024]{1,0:T(8,128)(2,1)}) custom-call(bf16[6,16,8192]{2,1,0:T(8,128)(2,1)S(1)} %copy-done.1, f32[96,1]{1,0:T(8,128)S(1)} %reshape.124.live_ref, f32[64,512]{1,0:T(8,128)S(1)} %get-tuple-element.19.cc_ref, f32[64,512]{1,0:T(8,128)S(1)} %get-tuple-element.18.cs_ref, ...), custom_call_target="tpu_custom_call" | custom-call | tf_op jit(solution)/shard_map/pallas_call | solution.py:55
  20.2 0.0 all-gather.2.cloned.1.call-update
  20.9 1.0 convert.9
  21.9 0.1 pad_add_fusion
  22.0 0.2 fusion.21
  22.2 0.4 subtract_convert_fusion
  22.6 40.5 %all-gather.2.cloned.1.call-done.all_ref = bf16[6,256,1024]{2,1,0:T(8,128)(2,1)} async-done(((bf16[6,16,1024]{2,1,0:T(8,128)(2,1)}), bf16[6,256,1024]{2,1,0:T(8,128)(2,1)}) %all-gather.2.cloned.1.call-update) | async-done | bytes 3145744 | tf_op jit(solution)/shard_map/all_gather | solution.py:250
  63.1 3.0 %fusion = f32[8,16,256,1]{2,1,3,0:T(8,128)S(1)} fusion(bf16[6,256,1024]{2,1,0:T(8,128)(2,1)} %all-gather.2.cloned.1.call-done.all_ref, bf16[8,6,16,512]{3,2,1,0:T(8,128)(2,1)S(1)} %get-tuple-element.10, bf16[8,6,16,512]{3,2,1,0:T(8,128)(2,1)S(1)} %get-tuple-element.9), kind=kOutput, calls=%fused_computation | convolution fusion | flops 405798912 | bytes 4849664 | tf_op jit(solution)/shard_map/ksaf,sbf->kab/dot_general | solution.py:259
  66.2 17.6 %all_to_all.15 = f32[16,8,256]{2,1,0:T(8,128)S(1)} all-to-all(f32[16,8,256]{2,1,0:T(8,128)S(1)} %bitcast.24), channel_id=1, replica_groups=mesh['shot'=16,'lag'=16] {'shot'}, dimensions={0} | all-to-all | bytes 262144 | tf_op jit(solution)/shard_map/all_to_all | solution.py:240
  83.8 12.8 %all_to_all.16 = f32[16,8,256]{2,1,0:T(8,128)S(1)} all-to-all(f32[16,8,256]{2,1,0:T(8,128)S(1)} %broadcast_in_dim.16), channel_id=1, replica_groups=mesh['shot'=16,'lag'=16] {'shot'}, dimensions={0} | all-to-all | bytes 262144 | tf_op jit(solution)/shard_map/all_to_all | solution.py:231
  96.7 1.1 broadcast_in_dim.18
  97.8 5.9 %all-to-all-start.2 = ((f32[16,4,16,256]{3,2,1,0:T(8,128)}), f32[16,4,16,256]{3,2,1,0:T(8,128)S(1)}, u32[]{:S(2)}, u32[]{:S(2)}) async-start(f32[16,4,16,256]{3,2,1,0:T(8,128)} %broadcast_in_dim.18), calls=%async_computation.2 | async-start | bytes 2097152 | tf_op jit(solution)/shard_map/all_to_all | solution.py:231
  103.7 15.8 %all-to-all-done.2 = f32[16,4,16,256]{3,2,1,0:T(8,128)S(1)} async-done(((f32[16,4,16,256]{3,2,1,0:T(8,128)}), f32[16,4,16,256]{3,2,1,0:T(8,128)S(1)}, u32[]{:S(2)}, u32[]{:S(2)}) %all-to-all-start.2) | async-done | bytes 1048608 | tf_op jit(solution)/shard_map/all_to_all | solution.py:231
  119.5 0.0 copy-start
  119.5 0.1 copy.7
  119.6 48.9 %shard_map.38.filter_ref = bf16[4,16,256]{2,1,0:T(8,128)(2,1)S(1)} custom-call(f32[4,256,256]{2,1,0:T(8,128)S(1)} %bitcast.20, f32[4,16,256]{2,1,0:T(8,128)S(1)} %bitcast.21), custom_call_target="tpu_custom_call" | custom-call | tf_op jit(solution)/shard_map/pallas_call | solution.py:224
  168.5 0.0 copy-done
  168.5 12.4 %shard_map.39 = bf16[6,16,8192]{2,1,0:T(8,128)(2,1)} custom-call(bf16[4,16,256]{2,1,0:T(8,128)(2,1)S(1)} %shard_map.38.filter_ref, bf16[6,256,1024]{2,1,0:T(8,128)(2,1)S(1)} %copy-done, bf16[96,1024]{1,0:T(8,128)(2,1)} %get-tuple-element.7.own_ref, f32[4,512]{1,0:T(4,128)S(1)} %slice.35.cos_ref, f32[4,512]{1,0:T(4,128)S(1)} %slice.36.sin_ref, ...), custom_call_target="tpu_custom_call" | custom-call | tf_op jit(solution)/shard_map/pallas_call | solution.py:93
  (11 shorter events, 0.1 us)
Async XLA Ops:
  6.5 56.6 %all-gather.2.cloned.1.call-start = ((), (), s32[]{:S(2)}) async-start(), calls=%async_computation.3 | async-start | bytes 3342336 | tf_op jit(solution)/shard_map/all_gather | solution.py:250
  9.0 1.4 copy-start.1
  97.8 21.7 %all-to-all-start.2 = ((f32[16,4,16,256]{3,2,1,0:T(8,128)}), f32[16,4,16,256]{3,2,1,0:T(8,128)S(1)}, u32[]{:S(2)}, u32[]{:S(2)}) async-start(f32[16,4,16,256]{3,2,1,0:T(8,128)} %broadcast_in_dim.18), calls=%async_computation.2 | async-start | bytes 2097152 | tf_op jit(solution)/shard_map/all_to_all | solution.py:231
  119.5 49.0 %copy-start = (bf16[6,256,1024]{2,1,0:T(8,128)(2,1)S(1)}, bf16[6,256,1024]{2,1,0:T(8,128)(2,1)}, u32[]{:S(2)}) copy-start(bf16[6,256,1024]{2,1,0:T(8,128)(2,1)} %all-gather.2.cloned.1.call-done.all_ref) | copy-start | bytes 9437188
Sparse Core Ops, SparseCore 0:
  20.4 42.6 all-gather.1

commit v2 on v1

--- a/solution.py
+++ b/solution.py
@@ -61,7 +61,8 @@
         compiler_params=pltpu.CompilerParams(vmem_limit_bytes=40 * 2**20),
     )(traces, live.reshape(rows, 1), cc, cs, fc, fs)
 
-def inverse_kernel(filter_ref, all_ref, own_ref, cos_ref, sin_ref, live_ref, table_ref, out_ref, error):
+def inverse_kernel(order_ref, filter_ref, own_ref, cos_ref, sin_ref, live_ref, table_ref, *refs):
+    *piece_refs, out_ref, error, full = refs
     shots, chans, chunk = out_ref.shape
     band = cos_ref.shape[1]
 
@@ -69,7 +70,8 @@
     def _():
         weights = filter_ref[...].reshape(LAGS * chans, filter_ref.shape[2])
         for s in range(shots):
-            mixed = jnp.dot(weights, all_ref[s], preferred_element_type=f32)
+            place(order_ref, piece_refs, s, full)
+            mixed = jnp.dot(weights, full[...], preferred_element_type=f32)
             even = jnp.zeros((chans, band), f32)
             odd = jnp.zeros((chans, band), f32)
             for j in range(LAGS):
@@ -85,31 +87,26 @@
     samples = pl.num_programs(0) * chunk
     out_ref[...] = (restored * (1.0 / samples) * live_ref[...]).astype(bf).reshape(out_ref.shape)
 
-def inverse(filter_bf, all_spec, own_spec, cosine, sine, live, table):
-    shots, channels, width = all_spec.shape
-    chans = filter_bf.shape[1]
+def inverse(order, filter_bf, pieces, own_rows, cosine, sine, live, table):
+    shots, chans = live.shape
+    rows, width = own_rows.shape
     samples = table.shape[0]
-    rows = shots * chans
+    channels = filter_bf.shape[2]
     return pl.pallas_call(
-        inverse_kernel, grid=(samples // CHUNK,),
+        inverse_kernel,
+        grid=(samples // CHUNK,),
         out_shape=jax.ShapeDtypeStruct((shots, chans, samples), bf),
-        in_specs=[VM, VM, VM, VM, VM, VM, pl.BlockSpec((CHUNK, width), lambda i: (i, 0))],
+        in_specs=[pl.BlockSpec(memory_space=pltpu.SMEM)]
+        + [VM] * 5
+        + [pl.BlockSpec((CHUNK, width), lambda i: (i, 0))]
+        + [VM] * len(pieces),
         out_specs=pl.BlockSpec((shots, chans, CHUNK), lambda i: (0, 0, i)),
-        scratch_shapes=[pltpu.VMEM((rows, width), bf)],
+        scratch_shapes=[pltpu.VMEM((rows, width), bf), pltpu.VMEM((channels, width), bf)],
         compiler_params=pltpu.CompilerParams(vmem_limit_bytes=40 * 2**20),
-    )(filter_bf, all_spec, own_spec, cosine, sine, live.reshape(rows, 1), table)
-
-
-def delay_apply(spectrum, cosine, sine):
-    band_size = cosine.shape[-1]
-    real_part = spectrum[..., :band_size]
-    imag_part = spectrum[..., band_size:]
-    return jnp.concatenate(
-        [real_part * cosine - imag_part * sine, imag_part * cosine + real_part * sine], axis=-1
-    )
-
-
-def invert_128(groups):
+    )(order, filter_bf, own_rows, cosine, sine, live.reshape(rows, 1), table, *pieces)
+
+
+def invert_128(groups, spare):
     lane = lax.broadcasted_iota(jnp.int32, (8, 128), 1)
     sub = lax.broadcasted_iota(jnp.int32, (8, 128), 0)
     groups = list(groups)
@@ -117,13 +114,16 @@
         lo = 8 * s
         inside = (lane >= lo) & (lane < lo + 8)
         rows = groups[s]
-        entry = {}
+        unit = jnp.where(lane - lo == sub, 1.0, 0.0)
         for j in range(8):
-            for i in range(j, 8):
-                entry[i, j] = jnp.broadcast_to(rows[i:i+1, lo+j:lo+j+1], (8, 128))
-        unit = jnp.where(lane - lo == sub, 1.0, 0.0)
-        start = jnp.where(inside, unit, rows)
-        y = [jnp.broadcast_to(start[j:j+1, :], (8, 128)) for j in range(8)]
+            spare[s % 2, j] = jnp.broadcast_to(rows[:, lo + j : lo + j + 1], (8, 128))
+        spare[s % 2, 8] = jnp.where(inside, unit, rows)
+        entry = {
+            (i, j): jnp.broadcast_to(spare[s % 2, j, i : i + 1, :], (8, 128))
+            for j in range(8)
+            for i in range(j, 8)
+        }
+        y = [jnp.broadcast_to(spare[s % 2, 8, j : j + 1, :], (8, 128)) for j in range(8)]
         low = {}
         dinv = []
         for j in range(8):
@@ -158,8 +158,11 @@
 def mm(a, b, ca=1, cb=0):
     return lax.dot_general(a, b, (((ca,), (cb,)), ((), ())), precision=lax.Precision.HIGHEST, preferred_element_type=f32)
 
-def solve_kernel(corr_ref, rhs_ref, out_ref, tiles, gains, ys, block, whole):
+def solve_kernel(order_ref, rhs_ref, *refs):
+    *piece_refs, out_ref, corr_ref, tiles, gains, ys, block, whole, spare = refs
     n = corr_ref.shape[1]
+    for k in range(LAGS):
+        place(order_ref, piece_refs, k, corr_ref.at[k])
     h = n // 2
     eye = lax.broadcasted_iota(jnp.int32, (n, n), 0) == lax.broadcasted_iota(jnp.int32, (n, n), 1)
     zero_lag = corr_ref[0]
@@ -202,7 +205,7 @@
 
     def step(q, carry):
         even = 0.5 * (block[...] + block[...].T)
-        groups = invert_128([even[8 * i : 8 * i + 8, :] for i in range(16)])
+        groups = invert_128([even[8 * i : 8 * i + 8, :] for i in range(16)], spare)
         for i in range(16):
             block[8 * i : 8 * i + 8, :] = groups[i]
         for p in range(LAGS):
@@ -218,12 +221,108 @@
         ys[p] = x
         out_ref[p] = x.astype(out_ref.dtype)
 
-def solve_filter(corr, rhs):
-    n = corr.shape[1]; m = rhs.shape[1]; h = n // 2
-    vm = pl.BlockSpec(memory_space=pltpu.VMEM)
-    return pl.pallas_call(solve_kernel, out_shape=jax.ShapeDtypeStruct((LAGS, m, n), jnp.bfloat16), in_specs=[vm, vm], out_specs=vm,
-        scratch_shapes=[pltpu.VMEM((LAGS, LAGS, n, n), f32), pltpu.VMEM((LAGS, LAGS, n, n), f32), pltpu.VMEM((LAGS, m, n), f32), pltpu.VMEM((h, h), f32), pltpu.VMEM((n, n), f32)],
-        compiler_params=pltpu.CompilerParams(vmem_limit_bytes=40 * 2**20))(corr, rhs)
+def solve_filter(order, pieces, rhs):
+    chans = rhs.shape[1]
+    n = rhs.shape[2]
+    half = n // 2
+    return pl.pallas_call(
+        solve_kernel,
+        out_shape=jax.ShapeDtypeStruct((LAGS, chans, n), bf),
+        in_specs=[pl.BlockSpec(memory_space=pltpu.SMEM)] + [VM] * (1 + len(pieces)),
+        out_specs=VM,
+        scratch_shapes=[
+            pltpu.VMEM((LAGS, n, n), f32),
+            pltpu.VMEM((LAGS, LAGS, n, n), f32),
+            pltpu.VMEM((LAGS, LAGS, n, n), f32),
+            pltpu.VMEM((LAGS, chans, n), f32),
+            pltpu.VMEM((half, half), f32),
+            pltpu.VMEM((n, n), f32),
+            pltpu.VMEM((2, 9, 8, half), f32),
+        ],
+        compiler_params=pltpu.CompilerParams(vmem_limit_bytes=40 * 2**20),
+    )(order, rhs, *pieces)
+
+
+def place(order_ref, piece_refs, shot, full):
+    count = 0
+    for ref in piece_refs:
+        for i in range(ref.shape[0]):
+            rows = ref.shape[2]
+            full[pl.ds(pl.multiple_of(order_ref[count] * rows, rows), rows), :] = ref[i, shot]
+            count += 1
+
+
+def correlate_kernel(order_ref, own_ref, cos_ref, sin_ref, *refs):
+    *piece_refs, out_ref, rotated, full = refs
+    shots = piece_refs[0].shape[1]
+    chans = piece_refs[0].shape[2]
+    band = cos_ref.shape[1]
+    for s in range(shots):
+        place(order_ref, piece_refs, s, full)
+        even = own_ref[s * chans : (s + 1) * chans, :band].astype(f32)
+        odd = own_ref[s * chans : (s + 1) * chans, band:].astype(f32)
+        for k in range(2 * LAGS):
+            c, n = cos_ref[k : k + 1, :], sin_ref[k : k + 1, :]
+            at = slice(k * chans, (k + 1) * chans)
+            rotated[at, :band] = (even * c - odd * n).astype(bf)
+            rotated[at, band:] = (odd * c + even * n).astype(bf)
+        part = lax.dot_general(
+            rotated[...], full[...], (((1,), (1,)), ((), ())), preferred_element_type=f32
+        )
+        if s == 0:
+            out_ref[...] = part
+        else:
+            out_ref[...] += part
+
+
+def correlate(order, own_rows, cosine, sine, pieces):
+    width = own_rows.shape[1]
+    chans = pieces[0].shape[2]
+    channels = chans * order.shape[0]
+    rows = 2 * LAGS * chans
+    return pl.pallas_call(
+        correlate_kernel,
+        out_shape=jax.ShapeDtypeStruct((rows, channels), f32),
+        in_specs=[pl.BlockSpec(memory_space=pltpu.SMEM)] + [VM] * (3 + len(pieces)),
+        out_specs=VM,
+        scratch_shapes=[pltpu.VMEM((rows, width), bf), pltpu.VMEM((channels, width), bf)],
+        compiler_params=pltpu.CompilerParams(vmem_limit_bytes=40 * 2**20),
+    )(order, own_rows, cosine, sine, *pieces)
+
+
+def lag_moves():
+    def move(dx, dy, dc):
+        return [
+            ((x * 4 + y) * 2 + c, ((x ^ dx) * 4 + (y + dy) % 4) * 2 + (c ^ dc))
+            for x in range(2)
+            for y in range(4)
+            for c in range(2)
+        ]
+
+    return move(1, 0, 0), move(0, 1, 0), move(0, -1, 0), move(0, 0, 1)
+
+
+def gather_lag(value):
+    over_x, up, down, over_core = lag_moves()
+    own = value[None]
+    pair = jnp.concatenate([own, lax.ppermute(own, "lag", over_x)], axis=0)
+    below = lax.ppermute(pair, "lag", up)
+    above = lax.ppermute(pair, "lag", down)
+    far_own = lax.ppermute(below[:1], "lag", up)
+    far_other = lax.ppermute(above[1:], "lag", down)
+    near = [pair, below, above, far_own, far_other]
+    return near + [lax.ppermute(piece, "lag", over_core) for piece in near]
+
+
+def lag_order():
+    index = lax.axis_index("lag")
+    x, y, core = index // 8, index // 2 % 4, index % 2
+    places = [
+        (x ^ dx) * 8 + (y + dy) % 4 * 2 + (core ^ dc)
+        for dc in (0, 1)
+        for dx, dy in ((0, 0), (1, 0), (0, 3), (1, 3), (0, 1), (1, 1), (0, 2), (1, 2))
+    ]
+    return jnp.stack(places).astype(jnp.int32)
 
 
 def gather_all(x, axis):
@@ -247,25 +346,22 @@
     live = live_mask.astype(f32)
     own_rows, table = forward(traces, live)
     own_spec = own_rows.reshape(shot_count, local_chan, 2 * band_size)
-    all_spec = lax.all_gather(own_spec, "lag", axis=1, tiled=True)
+    order = lag_order()
+    spectra = gather_lag(own_spec)
     spacing = samples // (2 * band_size)
     tap_delays = jnp.arange(LAGS, dtype=jnp.int32) * spacing
     lag_list = jnp.concatenate([tap_delays, gap_samples[0] + tap_delays])
     cosine, sine = wave(lag_list, samples, band_size)
     turn = jnp.where(jnp.arange(2 * LAGS) < LAGS, 1.0, -1.0).astype(f32)[:, None]
-    rotated = delay_apply(
-        own_spec.astype(f32)[None], cosine[:, None, None, :], (turn * sine)[:, None, None, :]
-    ).astype(jnp.bfloat16)
-    partial_value = jnp.einsum("ksaf,sbf->kab", rotated, all_spec, preferred_element_type=f32)
-    channels = all_spec.shape[1]
+    partial_value = correlate(order, own_rows, cosine, turn * sine, spectra)
+    channels = partial_value.shape[1]
     total_shots = shot_count * lax.axis_size("shot")
-    summed = sum_over(partial_value.reshape(2 * LAGS * local_chan, channels), "shot")
+    summed = sum_over(partial_value, "shot")
     summed = summed * (1.0 / samples) * (1.0 / (samples * total_shots))
     summed = summed.reshape(2 * LAGS, local_chan, channels)
-    gathered = gather_all(summed[:LAGS], "lag")
-    correlation = jnp.swapaxes(gathered, 0, 1).reshape(LAGS, channels, channels)
-    filter_bf = solve_filter(correlation, summed[LAGS:])
-    return inverse(filter_bf, all_spec, own_rows, cosine[LAGS:], sine[LAGS:], live, table)
+    correlation = gather_lag(summed[:LAGS])
+    filter_bf = solve_filter(order, correlation, summed[LAGS:])
+    return inverse(order, filter_bf, spectra, own_rows, cosine[LAGS:], sine[LAGS:], live, table)
 
 
 def solution(mesh):

time: 188 us -> 156 us (0.83)
  waiting for transfers between devices: 56.4 us -> 10.6 us
  starting transfers between devices: 5.89 us -> 37.6 us
  between operations: 14.2 us -> 0.79 us
  matrix products: 3.04 us -> 0 us
  Pallas kernels: 71.2 us -> 69.2 us
  blocking collectives: 30.4 us -> 32.3 us
    all_gather x1 -> x0, waiting for transfers between devices: 40.5 us -> none  [shards(): all_spec = lax.all_gather(own_spec, 'lag', axis=1, tiled=True)]
    ppermute x0 -> x20, starting transfers between devices: none -> 37.6 us  [the longest x10 23.9 us: gather_lag(): return near + [lax.ppermute(piece, 'lag', over_core) for piece in near]]
    all_to_all x1 -> x0, waiting for transfers between devices: 15.8 us -> none  [gather_all(): lax.all_to_all(jnp.broadcast_to(x[None], (parts,) + x.shape), axis, split...]
    ppermute x0 -> x20, waiting for transfers between devices: none -> 10.6 us  [the longest x2 5.78 us: gather_lag(): pair = jnp.concatenate([own, lax.ppermute(own, 'lag', over_x)], axis=0)]
    all_to_all x1 -> x0, starting transfers between devices: 5.89 us -> none  [gather_all(): lax.all_to_all(jnp.broadcast_to(x[None], (parts,) + x.shape), axis, split...]
    dot_general x1 -> x0, matrix products: 3.04 us -> none  [shards(): jnp.einsum('ksaf,sbf->kab', rotated, all_spec, preferred_element_type=f32)]
    pallas_call x1 -> x2, Pallas kernels: 48.9 us -> 46.6 us  [the longest x1 44.6 us: solve_filter(): pl.pallas_call(solve_kernel, out_shape=jax.ShapeDtypeStruct((LAGS, chans,...]
    all_to_all x1, blocking collectives: 17.6 us -> 19.5 us  [sum_over(): lax.all_to_all(split, axis, split_axis=0, concat_axis=0, tiled=True)]
  transfers between devices with their start and end apart: 2 -> 20, of which waited for: 2 -> 5; matrix products, arithmetic and copies ran while one was open for 1% -> 1% of each run, Pallas kernels for 0% -> 0%
where the time goes in v2:
time: 156 us
  Pallas kernels  69.2 us (44%)
  starting transfers between devices  37.6 us (24%)
  blocking collectives  32.3 us (21%)
  waiting for transfers between devices  10.6 us (7%)
  other arithmetic  3.24 us (2%)
  local copies, waits for them, and re-layouts  2.36 us (2%)
    pallas_call x1, Pallas kernels, solve_filter(): pl.pallas_call(solve_kernel, out_shape=jax.ShapeDtypeStruct((LAGS, chans,...  44.6 us
    ppermute x10, starting transfers between devices, gather_lag(): return near + [lax.ppermute(piece, 'lag', over_core) for piece in near]  23.9 us
    all_to_all x1, blocking collectives, sum_over(): lax.all_to_all(split, axis, split_axis=0, concat_axis=0, tiled=True)  19.5 us
    all_to_all x1, blocking collectives, gather_all(): lax.all_to_all(jnp.broadcast_to(x[None], (parts,) + x.shape), axis, split...  12.8 us
    pallas_call x1, Pallas kernels, inverse(): pl.pallas_call(inverse_kernel, grid=(samples // CHUNK,), out_shape=jax.Sh...  12.7 us
    pallas_call x1, Pallas kernels, forward(): pl.pallas_call(forward_kernel, grid=(samples // CHUNK,), out_shape=(jax.S...  9.87 us
    ppermute x2, waiting for transfers between devices, gather_lag(): pair = jnp.concatenate([own, lax.ppermute(own, 'lag', over_x)], axis=0)  5.78 us
    ppermute x2, starting transfers between devices, gather_lag(): far_other = lax.ppermute(above[1:], 'lag', down)  4.77 us
  transfers between devices with their start and end apart: 20, of which 5 were waited for; matrix products, arithmetic and copies ran while one was open for 1% of the time, Pallas kernels for 0%

profile of v2, /device:TPU:1, one launch (start us, length us, event | category | flops | bytes accessed | tf_op | source)
XLA Modules:
  0.0 156.0 jit_solution(14734295098272790002)
XLA Ops:
  0.0 0.7 convert_element_type.16
  0.8 1.0 fusion.9
  1.8 0.6 fusion.11
  2.4 1.4 copy-done
  3.8 9.9 %shard_map.37 = (bf16[96,1024]{1,0:T(8,128)(2,1)S(1)}, bf16[8192,1024]{1,0:T(8,128)(2,1)}) custom-call(bf16[6,16,8192]{2,1,0:T(8,128)(2,1)S(1)} %copy-done, f32[96,1]{1,0:T(8,128)S(1)} %reshape.35.live_ref, f32[64,512]{1,0:T(8,128)S(1)} %get-tuple-element.15.cc_ref, f32[64,512]{1,0:T(8,128)S(1)} %get-tuple-element.14.cs_ref, ...), custom_call_target="tpu_custom_call" | custom-call | tf_op jit(solution)/shard_map/pallas_call | solution.py:55
  13.7 2.0 %collective-permute-start = (bf16[1,6,16,1024]{3,2,1,0:T(8,128)(2,1)S(1)}, bf16[1,6,16,1024]{3,2,1,0:T(8,128)(2,1)S(1)}, u32[]{:S(2)}, u32[]{:S(2)}) collective-permute-start(bf16[1,6,16,1024]{3,2,1,0:T(8,128)(2,1)S(1)} %bitcast.22), channel_id=1, source_target_pairs={{0,8},{1,9},{2,10},{3,11},{4,12},{5,13},{6,14},{7,15},{8,0},{9,1},... | collective-permute-start | bytes 589832 | tf_op jit(solution)/shard_map/ppermute | solution.py:308
  15.7 3.3 %collective-permute-done = bf16[1,6,16,1024]{3,2,1,0:T(8,128)(2,1)S(1)} collective-permute-done((bf16[1,6,16,1024]{3,2,1,0:T(8,128)(2,1)S(1)}, bf16[1,6,16,1024]{3,2,1,0:T(8,128)(2,1)S(1)}, u32[]{:S(2)}, u32[]{:S(2)}) %collective-permute-start) | collective-permute-done | bytes 196640 | tf_op jit(solution)/shard_map/ppermute | solution.py:308
  19.1 4.1 %collective-permute-start.2 = (bf16[2,6,16,1024]{3,2,1,0:T(8,128)(2,1)S(1)}, bf16[2,6,16,1024]{3,2,1,0:T(8,128)(2,1)S(1)}, u32[]{:S(2)}, u32[]{:S(2)}) collective-permute-start(bf16[2,6,16,1024]{3,2,1,0:T(8,128)(2,1)S(1)} %pad_maximum_fusion.refs_0_), channel_id=1, source_target_pairs={{0,6},{1,7},{2,0},{3,1},{4,2},{5,3},{6,4},{7,5},{8,14},{9,15},{10,... | collective-permute-start | bytes 1179656 | tf_op jit(solution)/shard_map/ppermute | solution.py:310
  23.8 1.9 %collective-permute-start.5 = (bf16[2,6,16,1024]{3,2,1,0:T(8,128)(2,1)S(1)}, bf16[2,6,16,1024]{3,2,1,0:T(8,128)(2,1)S(1)}, u32[]{:S(2)}, u32[]{:S(2)}) collective-permute-start(bf16[2,6,16,1024]{3,2,1,0:T(8,128)(2,1)S(1)} %pad_maximum_fusion.refs_0_), channel_id=1, source_target_pairs={{0,1},{1,0},{2,3},{3,2},{4,5},{5,4},{6,7},{7,6},{8,9},{9,8},{10,11... | collective-permute-start | bytes 1179656 | tf_op jit(solution)/shard_map/ppermute | solution.py:314
  25.7 4.3 %collective-permute-done.2.refs_2_ = bf16[2,6,16,1024]{3,2,1,0:T(8,128)(2,1)S(1)} collective-permute-done((bf16[2,6,16,1024]{3,2,1,0:T(8,128)(2,1)S(1)}, bf16[2,6,16,1024]{3,2,1,0:T(8,128)(2,1)S(1)}, u32[]{:S(2)}, u32[]{:S(2)}) %collective-permute-start.2) | collective-permute-done | bytes 393248 | tf_op jit(solution)/shard_map/ppermute | solution.py:310
  30.0 3.5 %collective-permute-start.4 = (bf16[1,6,16,1024]{3,2,1,0:T(8,128)(2,1)S(1)}, bf16[1,6,16,1024]{3,2,1,0:T(8,128)(2,1)S(1)}, u32[]{:S(2)}, u32[]{:S(2)}) collective-permute-start(bf16[1,6,16,1024]{3,2,1,0:T(8,128)(2,1)S(1)} %slice.40), channel_id=1, source_target_pairs={{0,6},{1,7},{2,0},{3,1},{4,2},{5,3},{6,4},{7,5},{8,14},{9,15},{10,... | collective-permute-start | bytes 589832 | tf_op jit(solution)/shard_map/ppermute | solution.py:312
  33.6 2.8 %collective-permute-start.7 = (bf16[2,6,16,1024]{3,2,1,0:T(8,128)(2,1)S(1)}, bf16[2,6,16,1024]{3,2,1,0:T(8,128)(2,1)S(1)}, u32[]{:S(2)}, u32[]{:S(2)}) collective-permute-start(bf16[2,6,16,1024]{3,2,1,0:T(8,128)(2,1)S(1)} %collective-permute-done.2.refs_2_), channel_id=1, source_target_pairs={{0,1},{1,0},{2,3},{3,2},{4,5},{5,4},{6,7},{7,6},{8,9},{9,8},{10,11... | collective-permute-start | bytes 1179656 | tf_op jit(solution)/shard_map/ppermute | solution.py:314
  36.7 2.7 %collective-permute-start.9 = (bf16[1,6,16,1024]{3,2,1,0:T(8,128)(2,1)S(1)}, bf16[1,6,16,1024]{3,2,1,0:T(8,128)(2,1)S(1)}, u32[]{:S(2)}, u32[]{:S(2)}) collective-permute-start(bf16[1,6,16,1024]{3,2,1,0:T(8,128)(2,1)S(1)} %collective-permute-done.4.refs_4_), channel_id=1, source_target_pairs={{0,1},{1,0},{2,3},{3,2},{4,5},{5,4},{6,7},{7,6},{8,9},{9,8},{10,11... | collective-permute-start | bytes 589832 | tf_op jit(solution)/shard_map/ppermute | solution.py:314
  39.5 3.8 %collective-permute-start.8 = (bf16[1,6,16,1024]{3,2,1,0:T(8,128)(2,1)S(1)}, bf16[1,6,16,1024]{3,2,1,0:T(8,128)(2,1)S(1)}, u32[]{:S(2)}, u32[]{:S(2)}) collective-permute-start(bf16[1,6,16,1024]{3,2,1,0:T(8,128)(2,1)S(1)} %collective-permute-done.3.refs_3_), channel_id=1, source_target_pairs={{0,1},{1,0},{2,3},{3,2},{4,5},{5,4},{6,7},{7,6},{8,9},{9,8},{10,11... | collective-permute-start | bytes 589832 | tf_op jit(solution)/shard_map/ppermute | solution.py:314
  43.2 0.8 fusion.16
  44.0 0.3 collective-permute-done.8.refs_8_
  44.3 2.0 %shard_map.38 = f32[128,256]{1,0:T(8,128)S(1)} custom-call(s32[16]{0:T(128)S(1)} %stack.67.order_ref, bf16[96,1024]{1,0:T(8,128)(2,1)S(1)} %get-tuple-element.7.own_ref, f32[8,512]{1,0:T(8,128)S(1)} %get-tuple-element.13.cos_ref, f32[8,512]{1,0:T(8,128)S(1)} %get-tuple-element.12.sin_ref, bf16[2,6,16,1024]{3,2,1,0:T(8,128)(2,1)S(1)} %pad_maximum_fusion.refs_0_, ...), custom_call_target="tpu_custom_call" | custom-call | tf_op jit(solution)/shard_map/pallas_call | solution.py:283
  46.3 19.5 %all_to_all.10 = f32[16,8,256]{2,1,0:T(8,128)S(1)} all-to-all(f32[16,8,256]{2,1,0:T(8,128)S(1)} %bitcast.24), channel_id=1, replica_groups=mesh['shot'=16,'lag'=16] {'shot'}, dimensions={0} | all-to-all | bytes 262144 | tf_op jit(solution)/shard_map/all_to_all | solution.py:339
  65.8 12.8 %all_to_all.11 = f32[16,8,256]{2,1,0:T(8,128)S(1)} all-to-all(f32[16,8,256]{2,1,0:T(8,128)S(1)} %broadcast_in_dim.14), channel_id=1, replica_groups=mesh['shot'=16,'lag'=16] {'shot'}, dimensions={0} | all-to-all | bytes 262144 | tf_op jit(solution)/shard_map/all_to_all | solution.py:330
  78.6 0.7 collective-permute-start.10
  79.4 2.5 %collective-permute-done.10 = f32[1,4,16,256]{3,2,1,0:T(8,128)S(1)} collective-permute-done((f32[1,4,16,256]{3,2,1,0:T(8,128)S(1)}, f32[1,4,16,256]{3,2,1,0:T(8,128)S(1)}, u32[]{:S(2)}, u32[]{:S(2)}) %collective-permute-start.10) | collective-permute-done | bytes 65568 | tf_op jit(solution)/shard_map/ppermute | solution.py:308
  81.9 0.3 collective-permute-start.12
  82.2 1.4 collective-permute-start.11
  83.6 4.2 %collective-permute-start.15 = (f32[2,4,16,256]{3,2,1,0:T(8,128)S(1)}, f32[2,4,16,256]{3,2,1,0:T(8,128)S(1)}, u32[]{:S(2)}, u32[]{:S(2)}) collective-permute-start(f32[2,4,16,256]{3,2,1,0:T(8,128)S(1)} %pad_maximum_fusion.1.refs_0_), channel_id=1, source_target_pairs={{0,1},{1,0},{2,3},{3,2},{4,5},{5,4},{6,7},{7,6},{8,9},{9,8},{10,11... | collective-permute-start | bytes 393224 | tf_op jit(solution)/shard_map/ppermute | solution.py:314
  87.8 1.3 collective-permute-start.14
  89.1 0.3 collective-permute-start.13
  89.4 3.4 %collective-permute-start.17 = (f32[2,4,16,256]{3,2,1,0:T(8,128)S(1)}, f32[2,4,16,256]{3,2,1,0:T(8,128)S(1)}, u32[]{:S(2)}, u32[]{:S(2)}) collective-permute-start(f32[2,4,16,256]{3,2,1,0:T(8,128)S(1)} %collective-permute-done.12.refs_2_), channel_id=1, source_target_pairs={{0,1},{1,0},{2,3},{3,2},{4,5},{5,4},{6,7},{7,6},{8,9},{9,8},{10,11... | collective-permute-start | bytes 393224 | tf_op jit(solution)/shard_map/ppermute | solution.py:314
  92.8 2.1 %collective-permute-start.19 = (f32[1,4,16,256]{3,2,1,0:T(8,128)S(1)}, f32[1,4,16,256]{3,2,1,0:T(8,128)S(1)}, u32[]{:S(2)}, u32[]{:S(2)}) collective-permute-start(f32[1,4,16,256]{3,2,1,0:T(8,128)S(1)} %collective-permute-done.14.refs_4_), channel_id=1, source_target_pairs={{0,1},{1,0},{2,3},{3,2},{4,5},{5,4},{6,7},{7,6},{8,9},{9,8},{10,11... | collective-permute-start | bytes 196616 | tf_op jit(solution)/shard_map/ppermute | solution.py:314
  95.0 2.8 %collective-permute-start.18 = (f32[1,4,16,256]{3,2,1,0:T(8,128)S(1)}, f32[1,4,16,256]{3,2,1,0:T(8,128)S(1)}, u32[]{:S(2)}, u32[]{:S(2)}) collective-permute-start(f32[1,4,16,256]{3,2,1,0:T(8,128)S(1)} %collective-permute-done.13.refs_3_), channel_id=1, source_target_pairs={{0,1},{1,0},{2,3},{3,2},{4,5},{5,4},{6,7},{7,6},{8,9},{9,8},{10,11... | collective-permute-start | bytes 196616 | tf_op jit(solution)/shard_map/ppermute | solution.py:314
  97.8 0.7 slice.46.sin_ref
  98.7 44.6 %shard_map.39.filter_ref = bf16[4,16,256]{2,1,0:T(8,128)(2,1)S(1)} custom-call(s32[16]{0:T(128)S(1)} %stack.67.order_ref, f32[4,16,256]{2,1,0:T(8,128)S(1)} %bitcast.25, f32[2,4,16,256]{3,2,1,0:T(8,128)S(1)} %pad_maximum_fusion.1.refs_0_, f32[2,4,16,256]{3,2,1,0:T(8,128)S(1)} %collective-permute-done.11.refs_1_, ...), custom_call_target="tpu_custom_call" | custom-call | tf_op jit(solution)/shard_map/pallas_call | solution.py:228
  143.3 12.7 %shard_map.40 = bf16[6,16,8192]{2,1,0:T(8,128)(2,1)} custom-call(s32[16]{0:T(128)S(1)} %stack.67.order_ref, bf16[4,16,256]{2,1,0:T(8,128)(2,1)S(1)} %shard_map.39.filter_ref, bf16[96,1024]{1,0:T(8,128)(2,1)S(1)} %get-tuple-element.7.own_ref, f32[4,512]{1,0:T(4,128)S(1)} %slice.45.cos_ref, f32[4,512]{1,0:T(4,128)S(1)} %slice.46.sin_ref, ...), custom_call_target="tpu_custom_call" | custom-call | tf_op jit(solution)/shard_map/pallas_call | solution.py:95
  (39 shorter events, 0.8 us)
Async XLA Ops:
  2.4 1.4 copy-start
  13.7 5.3 %collective-permute-start = (bf16[1,6,16,1024]{3,2,1,0:T(8,128)(2,1)S(1)}, bf16[1,6,16,1024]{3,2,1,0:T(8,128)(2,1)S(1)}, u32[]{:S(2)}, u32[]{:S(2)}) collective-permute-start(bf16[1,6,16,1024]{3,2,1,0:T(8,128)(2,1)S(1)} %bitcast.22), channel_id=1, source_target_pairs={{0,8},{1,9},{2,10},{3,11},{4,12},{5,13},{6,14},{7,15},{8,0},{9,1},... | collective-permute-start | bytes 589832 | tf_op jit(solution)/shard_map/ppermute | solution.py:308
  19.1 10.9 %collective-permute-start.2 = (bf16[2,6,16,1024]{3,2,1,0:T(8,128)(2,1)S(1)}, bf16[2,6,16,1024]{3,2,1,0:T(8,128)(2,1)S(1)}, u32[]{:S(2)}, u32[]{:S(2)}) collective-permute-start(bf16[2,6,16,1024]{3,2,1,0:T(8,128)(2,1)S(1)} %pad_maximum_fusion.refs_0_), channel_id=1, source_target_pairs={{0,6},{1,7},{2,0},{3,1},{4,2},{5,3},{6,4},{7,5},{8,14},{9,15},{10,... | collective-permute-start | bytes 1179656 | tf_op jit(solution)/shard_map/ppermute | solution.py:310
  23.1 10.4 %collective-permute-start.1 = (bf16[2,6,16,1024]{3,2,1,0:T(8,128)(2,1)S(1)}, bf16[2,6,16,1024]{3,2,1,0:T(8,128)(2,1)S(1)}, u32[]{:S(2)}, u32[]{:S(2)}) collective-permute-start(bf16[2,6,16,1024]{3,2,1,0:T(8,128)(2,1)S(1)} %pad_maximum_fusion.refs_0_), channel_id=1, source_target_pairs={{0,2},{1,3},{2,4},{3,5},{4,6},{5,7},{6,0},{7,1},{8,10},{9,11},{10,... | collective-permute-start | bytes 1179656 | tf_op jit(solution)/shard_map/ppermute | solution.py:309
  23.8 20.2 %collective-permute-start.5 = (bf16[2,6,16,1024]{3,2,1,0:T(8,128)(2,1)S(1)}, bf16[2,6,16,1024]{3,2,1,0:T(8,128)(2,1)S(1)}, u32[]{:S(2)}, u32[]{:S(2)}) collective-permute-start(bf16[2,6,16,1024]{3,2,1,0:T(8,128)(2,1)S(1)} %pad_maximum_fusion.refs_0_), channel_id=1, source_target_pairs={{0,1},{1,0},{2,3},{3,2},{4,5},{5,4},{6,7},{7,6},{8,9},{9,8},{10,11... | collective-permute-start | bytes 1179656 | tf_op jit(solution)/shard_map/ppermute | solution.py:314
  30.0 6.7 %collective-permute-start.4 = (bf16[1,6,16,1024]{3,2,1,0:T(8,128)(2,1)S(1)}, bf16[1,6,16,1024]{3,2,1,0:T(8,128)(2,1)S(1)}, u32[]{:S(2)}, u32[]{:S(2)}) collective-permute-start(bf16[1,6,16,1024]{3,2,1,0:T(8,128)(2,1)S(1)} %slice.40), channel_id=1, source_target_pairs={{0,6},{1,7},{2,0},{3,1},{4,2},{5,3},{6,4},{7,5},{8,14},{9,15},{10,... | collective-permute-start | bytes 589832 | tf_op jit(solution)/shard_map/ppermute | solution.py:312
  33.5 5.9 %collective-permute-start.3 = (bf16[1,6,16,1024]{3,2,1,0:T(8,128)(2,1)S(1)}, bf16[1,6,16,1024]{3,2,1,0:T(8,128)(2,1)S(1)}, u32[]{:S(2)}, u32[]{:S(2)}) collective-permute-start(bf16[1,6,16,1024]{3,2,1,0:T(8,128)(2,1)S(1)} %slice.39), channel_id=1, source_target_pairs={{0,2},{1,3},{2,4},{3,5},{4,6},{5,7},{6,0},{7,1},{8,10},{9,11},{10,... | collective-permute-start | bytes 589832 | tf_op jit(solution)/shard_map/ppermute | solution.py:311
  33.6 10.4 %collective-permute-start.7 = (bf16[2,6,16,1024]{3,2,1,0:T(8,128)(2,1)S(1)}, bf16[2,6,16,1024]{3,2,1,0:T(8,128)(2,1)S(1)}, u32[]{:S(2)}, u32[]{:S(2)}) collective-permute-start(bf16[2,6,16,1024]{3,2,1,0:T(8,128)(2,1)S(1)} %collective-permute-done.2.refs_2_), channel_id=1, source_target_pairs={{0,1},{1,0},{2,3},{3,2},{4,5},{5,4},{6,7},{7,6},{8,9},{9,8},{10,11... | collective-permute-start | bytes 1179656 | tf_op jit(solution)/shard_map/ppermute | solution.py:314
  36.5 7.9 %collective-permute-start.6 = (bf16[2,6,16,1024]{3,2,1,0:T(8,128)(2,1)S(1)}, bf16[2,6,16,1024]{3,2,1,0:T(8,128)(2,1)S(1)}, u32[]{:S(2)}, u32[]{:S(2)}) collective-permute-start(bf16[2,6,16,1024]{3,2,1,0:T(8,128)(2,1)S(1)} %collective-permute-done.1.refs_1_), channel_id=1, source_target_pairs={{0,1},{1,0},{2,3},{3,2},{4,5},{5,4},{6,7},{7,6},{8,9},{9,8},{10,11... | collective-permute-start | bytes 1179656 | tf_op jit(solution)/shard_map/ppermute | solution.py:314
  36.7 7.3 %collective-permute-start.9 = (bf16[1,6,16,1024]{3,2,1,0:T(8,128)(2,1)S(1)}, bf16[1,6,16,1024]{3,2,1,0:T(8,128)(2,1)S(1)}, u32[]{:S(2)}, u32[]{:S(2)}) collective-permute-start(bf16[1,6,16,1024]{3,2,1,0:T(8,128)(2,1)S(1)} %collective-permute-done.4.refs_4_), channel_id=1, source_target_pairs={{0,1},{1,0},{2,3},{3,2},{4,5},{5,4},{6,7},{7,6},{8,9},{9,8},{10,11... | collective-permute-start | bytes 589832 | tf_op jit(solution)/shard_map/ppermute | solution.py:314
  39.5 4.9 %collective-permute-start.8 = (bf16[1,6,16,1024]{3,2,1,0:T(8,128)(2,1)S(1)}, bf16[1,6,16,1024]{3,2,1,0:T(8,128)(2,1)S(1)}, u32[]{:S(2)}, u32[]{:S(2)}) collective-permute-start(bf16[1,6,16,1024]{3,2,1,0:T(8,128)(2,1)S(1)} %collective-permute-done.3.refs_3_), channel_id=1, source_target_pairs={{0,1},{1,0},{2,3},{3,2},{4,5},{5,4},{6,7},{7,6},{8,9},{9,8},{10,11... | collective-permute-start | bytes 589832 | tf_op jit(solution)/shard_map/ppermute | solution.py:314
  78.6 3.2 %collective-permute-start.10 = (f32[1,4,16,256]{3,2,1,0:T(8,128)S(1)}, f32[1,4,16,256]{3,2,1,0:T(8,128)S(1)}, u32[]{:S(2)}, u32[]{:S(2)}) collective-permute-start(f32[1,4,16,256]{3,2,1,0:T(8,128)S(1)} %bitcast.26), channel_id=1, source_target_pairs={{0,8},{1,9},{2,10},{3,11},{4,12},{5,13},{6,14},{7,15},{8,0},{9,1},... | collective-permute-start | bytes 196616 | tf_op jit(solution)/shard_map/ppermute | solution.py:308
  81.9 5.9 %collective-permute-start.12 = (f32[2,4,16,256]{3,2,1,0:T(8,128)S(1)}, f32[2,4,16,256]{3,2,1,0:T(8,128)S(1)}, u32[]{:S(2)}, u32[]{:S(2)}) collective-permute-start(f32[2,4,16,256]{3,2,1,0:T(8,128)S(1)} %pad_maximum_fusion.1.refs_0_), channel_id=1, source_target_pairs={{0,6},{1,7},{2,0},{3,1},{4,2},{5,3},{6,4},{7,5},{8,14},{9,15},{10,... | collective-permute-start | bytes 393224 | tf_op jit(solution)/shard_map/ppermute | solution.py:310
  82.2 6.9 %collective-permute-start.11 = (f32[2,4,16,256]{3,2,1,0:T(8,128)S(1)}, f32[2,4,16,256]{3,2,1,0:T(8,128)S(1)}, u32[]{:S(2)}, u32[]{:S(2)}) collective-permute-start(f32[2,4,16,256]{3,2,1,0:T(8,128)S(1)} %pad_maximum_fusion.1.refs_0_), channel_id=1, source_target_pairs={{0,2},{1,3},{2,4},{3,5},{4,6},{5,7},{6,0},{7,1},{8,10},{9,11},{10,... | collective-permute-start | bytes 393224 | tf_op jit(solution)/shard_map/ppermute | solution.py:309
  83.6 14.9 %collective-permute-start.15 = (f32[2,4,16,256]{3,2,1,0:T(8,128)S(1)}, f32[2,4,16,256]{3,2,1,0:T(8,128)S(1)}, u32[]{:S(2)}, u32[]{:S(2)}) collective-permute-start(f32[2,4,16,256]{3,2,1,0:T(8,128)S(1)} %pad_maximum_fusion.1.refs_0_), channel_id=1, source_target_pairs={{0,1},{1,0},{2,3},{3,2},{4,5},{5,4},{6,7},{7,6},{8,9},{9,8},{10,11... | collective-permute-start | bytes 393224 | tf_op jit(solution)/shard_map/ppermute | solution.py:314
  87.8 5.1 %collective-permute-start.14 = (f32[1,4,16,256]{3,2,1,0:T(8,128)S(1)}, f32[1,4,16,256]{3,2,1,0:T(8,128)S(1)}, u32[]{:S(2)}, u32[]{:S(2)}) collective-permute-start(f32[1,4,16,256]{3,2,1,0:T(8,128)S(1)} %slice.44), channel_id=1, source_target_pairs={{0,6},{1,7},{2,0},{3,1},{4,2},{5,3},{6,4},{7,5},{8,14},{9,15},{10,... | collective-permute-start | bytes 196616 | tf_op jit(solution)/shard_map/ppermute | solution.py:312
  89.1 5.9 %collective-permute-start.13 = (f32[1,4,16,256]{3,2,1,0:T(8,128)S(1)}, f32[1,4,16,256]{3,2,1,0:T(8,128)S(1)}, u32[]{:S(2)}, u32[]{:S(2)}) collective-permute-start(f32[1,4,16,256]{3,2,1,0:T(8,128)S(1)} %slice.43), channel_id=1, source_target_pairs={{0,2},{1,3},{2,4},{3,5},{4,6},{5,7},{6,0},{7,1},{8,10},{9,11},{10,... | collective-permute-start | bytes 196616 | tf_op jit(solution)/shard_map/ppermute | solution.py:311
  89.4 9.1 %collective-permute-start.17 = (f32[2,4,16,256]{3,2,1,0:T(8,128)S(1)}, f32[2,4,16,256]{3,2,1,0:T(8,128)S(1)}, u32[]{:S(2)}, u32[]{:S(2)}) collective-permute-start(f32[2,4,16,256]{3,2,1,0:T(8,128)S(1)} %collective-permute-done.12.refs_2_), channel_id=1, source_target_pairs={{0,1},{1,0},{2,3},{3,2},{4,5},{5,4},{6,7},{7,6},{8,9},{9,8},{10,11... | collective-permute-start | bytes 393224 | tf_op jit(solution)/shard_map/ppermute | solution.py:314
  92.8 5.8 %collective-permute-start.16 = (f32[2,4,16,256]{3,2,1,0:T(8,128)S(1)}, f32[2,4,16,256]{3,2,1,0:T(8,128)S(1)}, u32[]{:S(2)}, u32[]{:S(2)}) collective-permute-start(f32[2,4,16,256]{3,2,1,0:T(8,128)S(1)} %collective-permute-done.11.refs_1_), channel_id=1, source_target_pairs={{0,1},{1,0},{2,3},{3,2},{4,5},{5,4},{6,7},{7,6},{8,9},{9,8},{10,11... | collective-permute-start | bytes 393224 | tf_op jit(solution)/shard_map/ppermute | solution.py:314
  92.8 5.7 %collective-permute-start.19 = (f32[1,4,16,256]{3,2,1,0:T(8,128)S(1)}, f32[1,4,16,256]{3,2,1,0:T(8,128)S(1)}, u32[]{:S(2)}, u32[]{:S(2)}) collective-permute-start(f32[1,4,16,256]{3,2,1,0:T(8,128)S(1)} %collective-permute-done.14.refs_4_), channel_id=1, source_target_pairs={{0,1},{1,0},{2,3},{3,2},{4,5},{5,4},{6,7},{7,6},{8,9},{9,8},{10,11... | collective-permute-start | bytes 196616 | tf_op jit(solution)/shard_map/ppermute | solution.py:314
  95.0 3.7 %collective-permute-start.18 = (f32[1,4,16,256]{3,2,1,0:T(8,128)S(1)}, f32[1,4,16,256]{3,2,1,0:T(8,128)S(1)}, u32[]{:S(2)}, u32[]{:S(2)}) collective-permute-start(f32[1,4,16,256]{3,2,1,0:T(8,128)S(1)} %collective-permute-done.13.refs_3_), channel_id=1, source_target_pairs={{0,1},{1,0},{2,3},{3,2},{4,5},{5,4},{6,7},{7,6},{8,9},{9,8},{10,11... | collective-permute-start | bytes 196616 | tf_op jit(solution)/shard_map/ppermute | solution.py:314

commit v3 on v2

--- a/solution.py
+++ b/solution.py
@@ -332,12 +332,11 @@
     )
 
 
-def sum_over(x, axis):
-    parts = lax.axis_size(axis)
-    rows = x.shape[0] // parts
-    split = x.reshape((parts, rows) + x.shape[1:])
-    swapped = lax.all_to_all(split, axis, split_axis=0, concat_axis=0, tiled=True)
-    return gather_all(jnp.sum(swapped, axis=0), axis).reshape(x.shape)
+def sum_over_shot(value):
+    for bit in (8, 1, 2, 4):
+        pairs = [(i, i ^ bit) for i in range(16)]
+        value = value + lax.ppermute(value, "shot", pairs)
+    return value
 
 
 def shards(traces, live_mask, gap_samples):
@@ -356,11 +355,12 @@
     partial_value = correlate(order, own_rows, cosine, turn * sine, spectra)
     channels = partial_value.shape[1]
     total_shots = shot_count * lax.axis_size("shot")
-    summed = sum_over(partial_value, "shot")
-    summed = summed * (1.0 / samples) * (1.0 / (samples * total_shots))
-    summed = summed.reshape(2 * LAGS, local_chan, channels)
-    correlation = gather_lag(summed[:LAGS])
-    filter_bf = solve_filter(order, correlation, summed[LAGS:])
+    scale = (1.0 / samples) * (1.0 / (samples * total_shots))
+    half = LAGS * local_chan
+    targets = jnp.sum(gather_all(partial_value[half:], "shot"), axis=0) * scale
+    summed = sum_over_shot(partial_value[:half]) * scale
+    correlation = gather_lag(summed.reshape(LAGS, local_chan, channels))
+    filter_bf = solve_filter(order, correlation, targets.reshape(LAGS, local_chan, channels))
     return inverse(order, filter_bf, spectra, own_rows, cosine[LAGS:], sine[LAGS:], live, table)
 
 

time: 156 us -> 181 us (1.16)
  waiting for transfers between devices: 10.6 us -> 44.8 us
  blocking collectives: 32.3 us -> 0 us
  starting transfers between devices: 37.6 us -> 54 us
  other arithmetic: 3.24 us -> 6.01 us
  local copies, waits for them, and re-layouts: 2.36 us -> 5.1 us
    all_to_all x2 -> x0, blocking collectives: 32.3 us -> none  [the longest x1 19.5 us: sum_over(): lax.all_to_all(split, axis, split_axis=0, concat_axis=0, tiled=True)]
    ppermute x0 -> x4, waiting for transfers between devices: none -> 32.1 us  [sum_over_shot(): value = value + lax.ppermute(value, 'shot', pairs)]
    all_to_all x0 -> x1, starting transfers between devices: none -> 10.8 us  [gather_all(): lax.all_to_all(jnp.broadcast_to(x[None], (parts,) + x.shape), axis, split...]
    ppermute x0 -> x4, starting transfers between devices: none -> 9.86 us  [sum_over_shot(): value = value + lax.ppermute(value, 'shot', pairs)]
    ppermute x2, waiting for transfers between devices: 0.01 us -> 5.69 us  [gather_lag(): below = lax.ppermute(pair, 'lag', up)]
    ppermute x10, starting transfers between devices: 23.9 us -> 18.4 us  [gather_lag(): return near + [lax.ppermute(piece, 'lag', over_core) for piece in near]]
    ppermute x2, waiting for transfers between devices: 4.28 us -> 0.01 us  [gather_lag(): above = lax.ppermute(pair, 'lag', down)]
    reduce_sum x1, other arithmetic: 0.02 us -> 1.92 us  [shards(): targets = jnp.sum(gather_all(partial_value[half:], 'shot'), axis=0) * scale]
  transfers between devices with their start and end apart: 20 -> 25, of which waited for: 5 -> 10; matrix products, arithmetic and copies ran while one was open for 1% -> 3% of each run, Pallas kernels for 0% -> 0%
where the time goes in v3:
time: 181 us
  Pallas kernels  70.1 us (39%)
  starting transfers between devices  54 us (30%)
  waiting for transfers between devices  44.8 us (25%)
  other arithmetic  6.01 us (3%)
  local copies, waits for them, and re-layouts  5.1 us (3%)
    pallas_call x1, Pallas kernels, solve_filter(): pl.pallas_call(solve_kernel, out_shape=jax.ShapeDtypeStruct((LAGS, chans,...  45.5 us
    ppermute x4, waiting for transfers between devices, sum_over_shot(): value = value + lax.ppermute(value, 'shot', pairs)  32.1 us
    ppermute x10, starting transfers between devices, gather_lag(): return near + [lax.ppermute(piece, 'lag', over_core) for piece in near]  18.4 us
    pallas_call x1, Pallas kernels, inverse(): pl.pallas_call(inverse_kernel, grid=(samples // CHUNK,), out_shape=jax.Sh...  12.7 us
    all_to_all x1, starting transfers between devices, gather_all(): lax.all_to_all(jnp.broadcast_to(x[None], (parts,) + x.shape), axis, split...  10.8 us
    pallas_call x1, Pallas kernels, forward(): pl.pallas_call(forward_kernel, grid=(samples // CHUNK,), out_shape=(jax.S...  9.91 us
    ppermute x4, starting transfers between devices, sum_over_shot(): value = value + lax.ppermute(value, 'shot', pairs)  9.86 us
    ppermute x2, waiting for transfers between devices, gather_lag(): pair = jnp.concatenate([own, lax.ppermute(own, 'lag', over_x)], axis=0)  6.24 us
  transfers between devices with their start and end apart: 25, of which 10 were waited for; matrix products, arithmetic and copies ran while one was open for 3% of the time, Pallas kernels for 0%

profile of v3, /device:TPU:1, one launch (start us, length us, event | category | flops | bytes accessed | tf_op | source)
XLA Modules:
  0.0 180.8 jit_solution(11970440367238857724)
XLA Ops:
  0.8 1.0 fusion.9
  2.4 1.4 copy-done
  3.8 9.9 %shard_map.37 = (bf16[96,1024]{1,0:T(8,128)(2,1)S(1)}, bf16[8192,1024]{1,0:T(8,128)(2,1)}) custom-call(bf16[6,16,8192]{2,1,0:T(8,128)(2,1)S(1)} %copy-done, f32[96,1]{1,0:T(8,128)S(1)} %reshape.24.live_ref, f32[64,512]{1,0:T(8,128)S(1)} %get-tuple-element.15.cc_ref, f32[64,512]{1,0:T(8,128)S(1)} %get-tuple-element.14.cs_ref, ...), custom_call_target="tpu_custom_call" | custom-call | tf_op jit(solution)/shard_map/pallas_call | solution.py:55
  13.7 2.0 %collective-permute-start = (bf16[1,6,16,1024]{3,2,1,0:T(8,128)(2,1)S(1)}, bf16[1,6,16,1024]{3,2,1,0:T(8,128)(2,1)S(1)}, u32[]{:S(2)}, u32[]{:S(2)}) collective-permute-start(bf16[1,6,16,1024]{3,2,1,0:T(8,128)(2,1)S(1)} %bitcast.21), channel_id=1, source_target_pairs={{0,8},{1,9},{2,10},{3,11},{4,12},{5,13},{6,14},{7,15},{8,0},{9,1},... | collective-permute-start | bytes 589832 | tf_op jit(solution)/shard_map/ppermute | solution.py:308
  15.8 3.3 %collective-permute-done = bf16[1,6,16,1024]{3,2,1,0:T(8,128)(2,1)S(1)} collective-permute-done((bf16[1,6,16,1024]{3,2,1,0:T(8,128)(2,1)S(1)}, bf16[1,6,16,1024]{3,2,1,0:T(8,128)(2,1)S(1)}, u32[]{:S(2)}, u32[]{:S(2)}) %collective-permute-start) | collective-permute-done | bytes 196640 | tf_op jit(solution)/shard_map/ppermute | solution.py:308
  19.1 2.6 %collective-permute-start.1 = (bf16[2,6,16,1024]{3,2,1,0:T(8,128)(2,1)S(1)}, bf16[2,6,16,1024]{3,2,1,0:T(8,128)(2,1)S(1)}, u32[]{:S(2)}, u32[]{:S(2)}) collective-permute-start(bf16[2,6,16,1024]{3,2,1,0:T(8,128)(2,1)S(1)} %pad_maximum_fusion.refs_0_), channel_id=1, source_target_pairs={{0,2},{1,3},{2,4},{3,5},{4,6},{5,7},{6,0},{7,1},{8,10},{9,11},{10,... | collective-permute-start | bytes 1179656 | tf_op jit(solution)/shard_map/ppermute | solution.py:309
  21.8 1.5 collective-permute-start.2
  23.9 2.8 %collective-permute-start.5 = (bf16[2,6,16,1024]{3,2,1,0:T(8,128)(2,1)S(1)}, bf16[2,6,16,1024]{3,2,1,0:T(8,128)(2,1)S(1)}, u32[]{:S(2)}, u32[]{:S(2)}) collective-permute-start(bf16[2,6,16,1024]{3,2,1,0:T(8,128)(2,1)S(1)} %pad_maximum_fusion.refs_0_), channel_id=1, source_target_pairs={{0,1},{1,0},{2,3},{3,2},{4,5},{5,4},{6,7},{7,6},{8,9},{9,8},{10,11... | collective-permute-start | bytes 1179656 | tf_op jit(solution)/shard_map/ppermute | solution.py:314
  26.8 3.3 %collective-permute-done.1.refs_1_ = bf16[2,6,16,1024]{3,2,1,0:T(8,128)(2,1)S(1)} collective-permute-done((bf16[2,6,16,1024]{3,2,1,0:T(8,128)(2,1)S(1)}, bf16[2,6,16,1024]{3,2,1,0:T(8,128)(2,1)S(1)}, u32[]{:S(2)}, u32[]{:S(2)}) %collective-permute-start.1) | collective-permute-done | bytes 393248 | tf_op jit(solution)/shard_map/ppermute | solution.py:309
  30.9 2.0 %collective-permute-start.4 = (bf16[1,6,16,1024]{3,2,1,0:T(8,128)(2,1)S(1)}, bf16[1,6,16,1024]{3,2,1,0:T(8,128)(2,1)S(1)}, u32[]{:S(2)}, u32[]{:S(2)}) collective-permute-start(bf16[1,6,16,1024]{3,2,1,0:T(8,128)(2,1)S(1)} %slice.33), channel_id=1, source_target_pairs={{0,6},{1,7},{2,0},{3,1},{4,2},{5,3},{6,4},{7,5},{8,14},{9,15},{10,... | collective-permute-start | bytes 589832 | tf_op jit(solution)/shard_map/ppermute | solution.py:312
  32.9 3.7 %collective-permute-start.6 = (bf16[2,6,16,1024]{3,2,1,0:T(8,128)(2,1)S(1)}, bf16[2,6,16,1024]{3,2,1,0:T(8,128)(2,1)S(1)}, u32[]{:S(2)}, u32[]{:S(2)}) collective-permute-start(bf16[2,6,16,1024]{3,2,1,0:T(8,128)(2,1)S(1)} %collective-permute-done.1.refs_1_), channel_id=1, source_target_pairs={{0,1},{1,0},{2,3},{3,2},{4,5},{5,4},{6,7},{7,6},{8,9},{9,8},{10,11... | collective-permute-start | bytes 1179656 | tf_op jit(solution)/shard_map/ppermute | solution.py:314
  36.9 3.4 %collective-permute-start.8 = (bf16[1,6,16,1024]{3,2,1,0:T(8,128)(2,1)S(1)}, bf16[1,6,16,1024]{3,2,1,0:T(8,128)(2,1)S(1)}, u32[]{:S(2)}, u32[]{:S(2)}) collective-permute-start(bf16[1,6,16,1024]{3,2,1,0:T(8,128)(2,1)S(1)} %collective-permute-done.3.refs_3_), channel_id=1, source_target_pairs={{0,1},{1,0},{2,3},{3,2},{4,5},{5,4},{6,7},{7,6},{8,9},{9,8},{10,11... | collective-permute-start | bytes 589832 | tf_op jit(solution)/shard_map/ppermute | solution.py:314
  41.7 2.0 %shard_map.38 = f32[128,256]{1,0:T(8,128)S(1)} custom-call(s32[16]{0:T(128)S(1)} %stack.67.order_ref, bf16[96,1024]{1,0:T(8,128)(2,1)S(1)} %get-tuple-element.7.own_ref, f32[8,512]{1,0:T(8,128)S(1)} %get-tuple-element.13.cos_ref, f32[8,512]{1,0:T(8,128)S(1)} %get-tuple-element.12.sin_ref, bf16[2,6,16,1024]{3,2,1,0:T(8,128)(2,1)S(1)} %pad_maximum_fusion.refs_0_, ...), custom_call_target="tpu_custom_call" | custom-call | tf_op jit(solution)/shard_map/pallas_call | solution.py:283
  43.7 2.8 %collective-permute-start.10 = (f32[64,256]{1,0:T(8,128)S(1)}, f32[64,256]{1,0:T(8,128)S(1)}, u32[]{:S(2)}, u32[]{:S(2)}) collective-permute-start(f32[64,256]{1,0:T(8,128)S(1)} %slice.35), channel_id=1, source_target_pairs={{0,128},{16,144},{32,160},{48,176},{64,192},{80,208},{96,224},{112... | collective-permute-start | bytes 196616 | tf_op jit(solution)/shard_map/ppermute | solution.py:338
  46.5 1.9 %collective-permute-done.10 = f32[64,256]{1,0:T(8,128)S(1)} collective-permute-done((f32[64,256]{1,0:T(8,128)S(1)}, f32[64,256]{1,0:T(8,128)S(1)}, u32[]{:S(2)}, u32[]{:S(2)}) %collective-permute-start.10) | collective-permute-done | bytes 65568 | tf_op jit(solution)/shard_map/ppermute | solution.py:338
  48.4 1.1 broadcast_in_dim.12
  49.5 10.8 %all-to-all-start = ((f32[16,64,256]{2,1,0:T(8,128)}), f32[16,64,256]{2,1,0:T(8,128)}, u32[]{:S(2)}, u32[]{:S(2)}) async-start(f32[16,64,256]{2,1,0:T(8,128)} %broadcast_in_dim.12), calls=%async_computation | async-start | bytes 2097152 | tf_op jit(solution)/shard_map/all_to_all | solution.py:330
  60.3 1.3 collective-permute-start.11
  61.6 23.8 %collective-permute-done.11 = f32[64,256]{1,0:T(8,128)S(1)} collective-permute-done((f32[64,256]{1,0:T(8,128)S(1)}, f32[64,256]{1,0:T(8,128)S(1)}, u32[]{:S(2)}, u32[]{:S(2)}) %collective-permute-start.11) | collective-permute-done | bytes 65568 | tf_op jit(solution)/shard_map/ppermute | solution.py:338
  86.2 4.3 %collective-permute-done.12 = f32[64,256]{1,0:T(8,128)S(1)} collective-permute-done((f32[64,256]{1,0:T(8,128)S(1)}, f32[64,256]{1,0:T(8,128)S(1)}, u32[]{:S(2)}, u32[]{:S(2)}) %collective-permute-start.12) | collective-permute-done | bytes 65568 | tf_op jit(solution)/shard_map/ppermute | solution.py:338
  90.5 4.9 %collective-permute-start.13 = (f32[64,256]{1,0:T(8,128)S(1)}, f32[64,256]{1,0:T(8,128)S(1)}, u32[]{:S(2)}, u32[]{:S(2)}) collective-permute-start(f32[64,256]{1,0:T(8,128)S(1)} %add.229), channel_id=1, source_target_pairs={{0,64},{16,80},{32,96},{48,112},{64,0},{80,16},{96,32},{112,48},{1... | collective-permute-start | bytes 196616 | tf_op jit(solution)/shard_map/ppermute | solution.py:338
  95.4 2.2 %collective-permute-done.13 = f32[64,256]{1,0:T(8,128)S(1)} collective-permute-done((f32[64,256]{1,0:T(8,128)S(1)}, f32[64,256]{1,0:T(8,128)S(1)}, u32[]{:S(2)}, u32[]{:S(2)}) %collective-permute-start.13) | collective-permute-done | bytes 65568 | tf_op jit(solution)/shard_map/ppermute | solution.py:338
  98.0 3.0 %collective-permute-done.14 = f32[1,4,16,256]{3,2,1,0:T(8,128)S(1)} collective-permute-done((f32[1,4,16,256]{3,2,1,0:T(8,128)S(1)}, f32[1,4,16,256]{3,2,1,0:T(8,128)S(1)}, u32[]{:S(2)}, u32[]{:S(2)}) %collective-permute-start.14) | collective-permute-done | bytes 65568 | tf_op jit(solution)/shard_map/ppermute | solution.py:308
  101.2 2.7 %collective-permute-start.16 = (f32[2,4,16,256]{3,2,1,0:T(8,128)S(1)}, f32[2,4,16,256]{3,2,1,0:T(8,128)}, u32[]{:S(2)}, u32[]{:S(2)}) collective-permute-start(f32[2,4,16,256]{3,2,1,0:T(8,128)S(1)} %pad_maximum_fusion.1.refs_0_), channel_id=1, source_target_pairs={{0,6},{1,7},{2,0},{3,1},{4,2},{5,3},{6,4},{7,5},{8,14},{9,15},{10,... | collective-permute-start | bytes 393224 | tf_op jit(solution)/shard_map/ppermute | solution.py:310
  103.8 2.4 %collective-permute-done.15.refs_1_ = f32[2,4,16,256]{3,2,1,0:T(8,128)} collective-permute-done((f32[2,4,16,256]{3,2,1,0:T(8,128)S(1)}, f32[2,4,16,256]{3,2,1,0:T(8,128)}, u32[]{:S(2)}, u32[]{:S(2)}) %collective-permute-start.15) | collective-permute-done | bytes 131104 | tf_op jit(solution)/shard_map/ppermute | solution.py:309
  107.1 0.8 slice.37
  107.9 2.7 %collective-permute-start.18 = (f32[1,4,16,256]{3,2,1,0:T(8,128)S(1)}, f32[1,4,16,256]{3,2,1,0:T(8,128)}, u32[]{:S(2)}, u32[]{:S(2)}) collective-permute-start(f32[1,4,16,256]{3,2,1,0:T(8,128)S(1)} %slice.37), channel_id=1, source_target_pairs={{0,6},{1,7},{2,0},{3,1},{4,2},{5,3},{6,4},{7,5},{8,14},{9,15},{10,... | collective-permute-start | bytes 196616 | tf_op jit(solution)/shard_map/ppermute | solution.py:312
  111.3 7.3 %collective-permute-start.19 = (f32[2,4,16,256]{3,2,1,0:T(8,128)S(1)}, f32[2,4,16,256]{3,2,1,0:T(8,128)}, u32[]{:S(2)}, u32[]{:S(2)}) collective-permute-start(f32[2,4,16,256]{3,2,1,0:T(8,128)S(1)} %pad_maximum_fusion.1.refs_0_), channel_id=1, source_target_pairs={{0,1},{1,0},{2,3},{3,2},{4,5},{5,4},{6,7},{7,6},{8,9},{9,8},{10,11... | collective-permute-start | bytes 393224 | tf_op jit(solution)/shard_map/ppermute | solution.py:314
  119.8 1.9 %reduce_sum.9 = f32[64,256]{1,0:T(8,128)} reduce(f32[16,64,256]{2,1,0:T(8,128)} %all-to-all-done, f32[]{:T(128)} %constant.136.clone.1), dimensions={0}, to_apply=%region_0.1 | reduce | flops 245760 | bytes 1114116 | tf_op jit(solution)/shard_map/reduce_sum | solution.py:360
  121.7 0.8 broadcast_multiply_fusion
  122.6 45.5 %shard_map.39.filter_ref = bf16[4,16,256]{2,1,0:T(8,128)(2,1)S(1)} custom-call(s32[16]{0:T(128)S(1)} %stack.67.order_ref, f32[4,16,256]{2,1,0:T(8,128)S(1)} %bitcast.23, f32[2,4,16,256]{3,2,1,0:T(8,128)S(1)} %pad_maximum_fusion.1.refs_0_, f32[2,4,16,256]{3,2,1,0:T(8,128)} %collective-permute-done.15.refs_1_, ...), custom_call_target="tpu_custom_call" | custom-call | tf_op jit(solution)/shard_map/pallas_call | solution.py:228
  168.1 12.7 %shard_map.40 = bf16[6,16,8192]{2,1,0:T(8,128)(2,1)} custom-call(s32[16]{0:T(128)S(1)} %stack.67.order_ref, bf16[4,16,256]{2,1,0:T(8,128)(2,1)S(1)} %shard_map.39.filter_ref, bf16[96,1024]{1,0:T(8,128)(2,1)S(1)} %get-tuple-element.7.own_ref, f32[4,512]{1,0:T(4,128)S(1)} %slice.38.cos_ref, f32[4,512]{1,0:T(4,128)S(1)} %slice.39.sin_ref, ...), custom_call_target="tpu_custom_call" | custom-call | tf_op jit(solution)/shard_map/pallas_call | solution.py:95
  (51 shorter events, 8.1 us)
Async XLA Ops:
  2.4 1.4 copy-start
  13.7 5.3 %collective-permute-start = (bf16[1,6,16,1024]{3,2,1,0:T(8,128)(2,1)S(1)}, bf16[1,6,16,1024]{3,2,1,0:T(8,128)(2,1)S(1)}, u32[]{:S(2)}, u32[]{:S(2)}) collective-permute-start(bf16[1,6,16,1024]{3,2,1,0:T(8,128)(2,1)S(1)} %bitcast.21), channel_id=1, source_target_pairs={{0,8},{1,9},{2,10},{3,11},{4,12},{5,13},{6,14},{7,15},{8,0},{9,1},... | collective-permute-start | bytes 589832 | tf_op jit(solution)/shard_map/ppermute | solution.py:308
  19.1 11.0 %collective-permute-start.1 = (bf16[2,6,16,1024]{3,2,1,0:T(8,128)(2,1)S(1)}, bf16[2,6,16,1024]{3,2,1,0:T(8,128)(2,1)S(1)}, u32[]{:S(2)}, u32[]{:S(2)}) collective-permute-start(bf16[2,6,16,1024]{3,2,1,0:T(8,128)(2,1)S(1)} %pad_maximum_fusion.refs_0_), channel_id=1, source_target_pairs={{0,2},{1,3},{2,4},{3,5},{4,6},{5,7},{6,0},{7,1},{8,10},{9,11},{10,... | collective-permute-start | bytes 1179656 | tf_op jit(solution)/shard_map/ppermute | solution.py:309
  21.8 9.2 %collective-permute-start.2 = (bf16[2,6,16,1024]{3,2,1,0:T(8,128)(2,1)S(1)}, bf16[2,6,16,1024]{3,2,1,0:T(8,128)(2,1)S(1)}, u32[]{:S(2)}, u32[]{:S(2)}) collective-permute-start(bf16[2,6,16,1024]{3,2,1,0:T(8,128)(2,1)S(1)} %pad_maximum_fusion.refs_0_), channel_id=1, source_target_pairs={{0,6},{1,7},{2,0},{3,1},{4,2},{5,3},{6,4},{7,5},{8,14},{9,15},{10,... | collective-permute-start | bytes 1179656 | tf_op jit(solution)/shard_map/ppermute | solution.py:310
  23.9 17.1 %collective-permute-start.5 = (bf16[2,6,16,1024]{3,2,1,0:T(8,128)(2,1)S(1)}, bf16[2,6,16,1024]{3,2,1,0:T(8,128)(2,1)S(1)}, u32[]{:S(2)}, u32[]{:S(2)}) collective-permute-start(bf16[2,6,16,1024]{3,2,1,0:T(8,128)(2,1)S(1)} %pad_maximum_fusion.refs_0_), channel_id=1, source_target_pairs={{0,1},{1,0},{2,3},{3,2},{4,5},{5,4},{6,7},{7,6},{8,9},{9,8},{10,11... | collective-permute-start | bytes 1179656 | tf_op jit(solution)/shard_map/ppermute | solution.py:314
  30.1 6.8 %collective-permute-start.3 = (bf16[1,6,16,1024]{3,2,1,0:T(8,128)(2,1)S(1)}, bf16[1,6,16,1024]{3,2,1,0:T(8,128)(2,1)S(1)}, u32[]{:S(2)}, u32[]{:S(2)}) collective-permute-start(bf16[1,6,16,1024]{3,2,1,0:T(8,128)(2,1)S(1)} %slice.32), channel_id=1, source_target_pairs={{0,2},{1,3},{2,4},{3,5},{4,6},{5,7},{6,0},{7,1},{8,10},{9,11},{10,... | collective-permute-start | bytes 589832 | tf_op jit(solution)/shard_map/ppermute | solution.py:311
  30.9 9.3 %collective-permute-start.4 = (bf16[1,6,16,1024]{3,2,1,0:T(8,128)(2,1)S(1)}, bf16[1,6,16,1024]{3,2,1,0:T(8,128)(2,1)S(1)}, u32[]{:S(2)}, u32[]{:S(2)}) collective-permute-start(bf16[1,6,16,1024]{3,2,1,0:T(8,128)(2,1)S(1)} %slice.33), channel_id=1, source_target_pairs={{0,6},{1,7},{2,0},{3,1},{4,2},{5,3},{6,4},{7,5},{8,14},{9,15},{10,... | collective-permute-start | bytes 589832 | tf_op jit(solution)/shard_map/ppermute | solution.py:312
  32.9 8.1 %collective-permute-start.6 = (bf16[2,6,16,1024]{3,2,1,0:T(8,128)(2,1)S(1)}, bf16[2,6,16,1024]{3,2,1,0:T(8,128)(2,1)S(1)}, u32[]{:S(2)}, u32[]{:S(2)}) collective-permute-start(bf16[2,6,16,1024]{3,2,1,0:T(8,128)(2,1)S(1)} %collective-permute-done.1.refs_1_), channel_id=1, source_target_pairs={{0,1},{1,0},{2,3},{3,2},{4,5},{5,4},{6,7},{7,6},{8,9},{9,8},{10,11... | collective-permute-start | bytes 1179656 | tf_op jit(solution)/shard_map/ppermute | solution.py:314
  36.7 4.3 %collective-permute-start.7 = (bf16[2,6,16,1024]{3,2,1,0:T(8,128)(2,1)S(1)}, bf16[2,6,16,1024]{3,2,1,0:T(8,128)(2,1)S(1)}, u32[]{:S(2)}, u32[]{:S(2)}) collective-permute-start(bf16[2,6,16,1024]{3,2,1,0:T(8,128)(2,1)S(1)} %collective-permute-done.2.refs_2_), channel_id=1, source_target_pairs={{0,1},{1,0},{2,3},{3,2},{4,5},{5,4},{6,7},{7,6},{8,9},{9,8},{10,11... | collective-permute-start | bytes 1179656 | tf_op jit(solution)/shard_map/ppermute | solution.py:314
  36.9 4.4 %collective-permute-start.8 = (bf16[1,6,16,1024]{3,2,1,0:T(8,128)(2,1)S(1)}, bf16[1,6,16,1024]{3,2,1,0:T(8,128)(2,1)S(1)}, u32[]{:S(2)}, u32[]{:S(2)}) collective-permute-start(bf16[1,6,16,1024]{3,2,1,0:T(8,128)(2,1)S(1)} %collective-permute-done.3.refs_3_), channel_id=1, source_target_pairs={{0,1},{1,0},{2,3},{3,2},{4,5},{5,4},{6,7},{7,6},{8,9},{9,8},{10,11... | collective-permute-start | bytes 589832 | tf_op jit(solution)/shard_map/ppermute | solution.py:314
  40.2 1.4 collective-permute-start.9
  43.7 4.7 %collective-permute-start.10 = (f32[64,256]{1,0:T(8,128)S(1)}, f32[64,256]{1,0:T(8,128)S(1)}, u32[]{:S(2)}, u32[]{:S(2)}) collective-permute-start(f32[64,256]{1,0:T(8,128)S(1)} %slice.35), channel_id=1, source_target_pairs={{0,128},{16,144},{32,160},{48,176},{64,192},{80,208},{96,224},{112... | collective-permute-start | bytes 196616 | tf_op jit(solution)/shard_map/ppermute | solution.py:338
  49.5 70.3 %all-to-all-start = ((f32[16,64,256]{2,1,0:T(8,128)}), f32[16,64,256]{2,1,0:T(8,128)}, u32[]{:S(2)}, u32[]{:S(2)}) async-start(f32[16,64,256]{2,1,0:T(8,128)} %broadcast_in_dim.12), calls=%async_computation | async-start | bytes 2097152 | tf_op jit(solution)/shard_map/all_to_all | solution.py:330
  60.3 25.1 %collective-permute-start.11 = (f32[64,256]{1,0:T(8,128)S(1)}, f32[64,256]{1,0:T(8,128)S(1)}, u32[]{:S(2)}, u32[]{:S(2)}) collective-permute-start(f32[64,256]{1,0:T(8,128)S(1)} %get-tuple-element.9), channel_id=1, source_target_pairs={{0,16},{16,0},{32,48},{48,32},{64,80},{80,64},{96,112},{112,96},{1... | collective-permute-start | bytes 196616 | tf_op jit(solution)/shard_map/ppermute | solution.py:338
  85.4 5.1 %collective-permute-start.12 = (f32[64,256]{1,0:T(8,128)S(1)}, f32[64,256]{1,0:T(8,128)S(1)}, u32[]{:S(2)}, u32[]{:S(2)}) collective-permute-start(f32[64,256]{1,0:T(8,128)S(1)} %add.228), channel_id=1, source_target_pairs={{0,32},{16,48},{32,0},{48,16},{64,96},{80,112},{96,64},{112,80},{1... | collective-permute-start | bytes 196616 | tf_op jit(solution)/shard_map/ppermute | solution.py:338
  90.5 7.1 %collective-permute-start.13 = (f32[64,256]{1,0:T(8,128)S(1)}, f32[64,256]{1,0:T(8,128)S(1)}, u32[]{:S(2)}, u32[]{:S(2)}) collective-permute-start(f32[64,256]{1,0:T(8,128)S(1)} %add.229), channel_id=1, source_target_pairs={{0,64},{16,80},{32,96},{48,112},{64,0},{80,16},{96,32},{112,48},{1... | collective-permute-start | bytes 196616 | tf_op jit(solution)/shard_map/ppermute | solution.py:338
  97.6 3.4 %collective-permute-start.14 = (f32[1,4,16,256]{3,2,1,0:T(8,128)S(1)}, f32[1,4,16,256]{3,2,1,0:T(8,128)S(1)}, u32[]{:S(2)}, u32[]{:S(2)}) collective-permute-start(f32[1,4,16,256]{3,2,1,0:T(8,128)S(1)} %bitcast.24), channel_id=1, source_target_pairs={{0,8},{1,9},{2,10},{3,11},{4,12},{5,13},{6,14},{7,15},{8,0},{9,1},... | collective-permute-start | bytes 196616 | tf_op jit(solution)/shard_map/ppermute | solution.py:308
  101.0 5.2 %collective-permute-start.15 = (f32[2,4,16,256]{3,2,1,0:T(8,128)S(1)}, f32[2,4,16,256]{3,2,1,0:T(8,128)}, u32[]{:S(2)}, u32[]{:S(2)}) collective-permute-start(f32[2,4,16,256]{3,2,1,0:T(8,128)S(1)} %pad_maximum_fusion.1.refs_0_), channel_id=1, source_target_pairs={{0,2},{1,3},{2,4},{3,5},{4,6},{5,7},{6,0},{7,1},{8,10},{9,11},{10,... | collective-permute-start | bytes 393224 | tf_op jit(solution)/shard_map/ppermute | solution.py:309
  101.2 5.9 %collective-permute-start.16 = (f32[2,4,16,256]{3,2,1,0:T(8,128)S(1)}, f32[2,4,16,256]{3,2,1,0:T(8,128)}, u32[]{:S(2)}, u32[]{:S(2)}) collective-permute-start(f32[2,4,16,256]{3,2,1,0:T(8,128)S(1)} %pad_maximum_fusion.1.refs_0_), channel_id=1, source_target_pairs={{0,6},{1,7},{2,0},{3,1},{4,2},{5,3},{6,4},{7,5},{8,14},{9,15},{10,... | collective-permute-start | bytes 393224 | tf_op jit(solution)/shard_map/ppermute | solution.py:310
  107.1 12.0 %collective-permute-start.17 = (f32[1,4,16,256]{3,2,1,0:T(8,128)S(1)}, f32[1,4,16,256]{3,2,1,0:T(8,128)}, u32[]{:S(2)}, u32[]{:S(2)}) collective-permute-start(f32[1,4,16,256]{3,2,1,0:T(8,128)S(1)} %slice.36), channel_id=1, source_target_pairs={{0,2},{1,3},{2,4},{3,5},{4,6},{5,7},{6,0},{7,1},{8,10},{9,11},{10,... | collective-permute-start | bytes 196616 | tf_op jit(solution)/shard_map/ppermute | solution.py:311
  107.9 11.4 %collective-permute-start.18 = (f32[1,4,16,256]{3,2,1,0:T(8,128)S(1)}, f32[1,4,16,256]{3,2,1,0:T(8,128)}, u32[]{:S(2)}, u32[]{:S(2)}) collective-permute-start(f32[1,4,16,256]{3,2,1,0:T(8,128)S(1)} %slice.37), channel_id=1, source_target_pairs={{0,6},{1,7},{2,0},{3,1},{4,2},{5,3},{6,4},{7,5},{8,14},{9,15},{10,... | collective-permute-start | bytes 196616 | tf_op jit(solution)/shard_map/ppermute | solution.py:312
  111.3 11.2 %collective-permute-start.19 = (f32[2,4,16,256]{3,2,1,0:T(8,128)S(1)}, f32[2,4,16,256]{3,2,1,0:T(8,128)}, u32[]{:S(2)}, u32[]{:S(2)}) collective-permute-start(f32[2,4,16,256]{3,2,1,0:T(8,128)S(1)} %pad_maximum_fusion.1.refs_0_), channel_id=1, source_target_pairs={{0,1},{1,0},{2,3},{3,2},{4,5},{5,4},{6,7},{7,6},{8,9},{9,8},{10,11... | collective-permute-start | bytes 393224 | tf_op jit(solution)/shard_map/ppermute | solution.py:314
  118.6 4.0 %collective-permute-start.20 = (f32[2,4,16,256]{3,2,1,0:T(8,128)}, f32[2,4,16,256]{3,2,1,0:T(8,128)}, u32[]{:S(2)}, u32[]{:S(2)}) collective-permute-start(f32[2,4,16,256]{3,2,1,0:T(8,128)} %collective-permute-done.15.refs_1_), channel_id=1, source_target_pairs={{0,1},{1,0},{2,3},{3,2},{4,5},{5,4},{6,7},{7,6},{8,9},{9,8},{10,11... | collective-permute-start | bytes 393224 | tf_op jit(solution)/shard_map/ppermute | solution.py:314
  118.6 4.0 %collective-permute-start.21 = (f32[2,4,16,256]{3,2,1,0:T(8,128)}, f32[2,4,16,256]{3,2,1,0:T(8,128)}, u32[]{:S(2)}, u32[]{:S(2)}) collective-permute-start(f32[2,4,16,256]{3,2,1,0:T(8,128)} %collective-permute-done.16.refs_2_), channel_id=1, source_target_pairs={{0,1},{1,0},{2,3},{3,2},{4,5},{5,4},{6,7},{7,6},{8,9},{9,8},{10,11... | collective-permute-start | bytes 393224 | tf_op jit(solution)/shard_map/ppermute | solution.py:314
  119.1 3.5 %collective-permute-start.22 = (f32[1,4,16,256]{3,2,1,0:T(8,128)}, f32[1,4,16,256]{3,2,1,0:T(8,128)}, u32[]{:S(2)}, u32[]{:S(2)}) collective-permute-start(f32[1,4,16,256]{3,2,1,0:T(8,128)} %collective-permute-done.17.refs_3_), channel_id=1, source_target_pairs={{0,1},{1,0},{2,3},{3,2},{4,5},{5,4},{6,7},{7,6},{8,9},{9,8},{10,11... | collective-permute-start | bytes 196616 | tf_op jit(solution)/shard_map/ppermute | solution.py:314
  119.4 3.2 %collective-permute-start.23 = (f32[1,4,16,256]{3,2,1,0:T(8,128)}, f32[1,4,16,256]{3,2,1,0:T(8,128)}, u32[]{:S(2)}, u32[]{:S(2)}) collective-permute-start(f32[1,4,16,256]{3,2,1,0:T(8,128)} %collective-permute-done.18.refs_4_), channel_id=1, source_target_pairs={{0,1},{1,0},{2,3},{3,2},{4,5},{5,4},{6,7},{7,6},{8,9},{9,8},{10,11... | collective-permute-start | bytes 196616 | tf_op jit(solution)/shard_map/ppermute | solution.py:314

commit v4 on v3

--- a/solution.py
+++ b/solution.py
@@ -6,7 +6,8 @@
 from jax.sharding import PartitionSpec as P
 
 LAGS = 4
-CHUNK = 1024
+CHUNK = 2048
+BACK_CHUNK = 4096
 FINE = 128
 f32 = jnp.float32
 bf = jnp.bfloat16
@@ -19,12 +20,19 @@
     angle = phase.astype(f32) * (jnp.pi / samples)
     return jnp.cos(angle), jnp.sin(angle)
 
-def forward_kernel(x_ref, live_ref, cc_ref, cs_ref, fc_ref, fs_ref, spec_ref, table_ref, acc):
+def quarter_turn(even, odd, sign):
+    turn = (lax.broadcasted_iota(jnp.int32, even.shape, 1) + 1) % 4
+    cross = jnp.where(turn == 1, sign, jnp.where(turn == 3, -sign, 0.0)).astype(f32)
+    along = jnp.where(turn == 0, 1.0, jnp.where(turn == 2, -1.0, 0.0)).astype(f32)
+    return even * along - odd * cross, odd * along + even * cross
+
+
+def forward_kernel(early_ref, late_ref, live_ref, cc_ref, cs_ref, fc_ref, fs_ref, spec_ref, table_ref, acc):
     step = pl.program_id(0)
     chunk, width = table_ref.shape
     band = width // 2
     fine = fc_ref.shape[0]
-    rows = acc.shape[0]
+    rows = spec_ref.shape[0]
     for r in range(chunk // fine):
         h = step * (chunk // fine) + r
         cc = cc_ref[pl.ds(h, 1), :]
@@ -32,7 +40,10 @@
         at = slice(r * fine, (r + 1) * fine)
         table_ref[at, :band] = (cc * fc_ref[...] - cs * fs_ref[...]).astype(bf)
         table_ref[at, band:] = (cs * fc_ref[...] + cc * fs_ref[...]).astype(bf)
-    part = jnp.dot(x_ref[...].reshape(rows, chunk), table_ref[...], preferred_element_type=f32)
+    both = jnp.concatenate(
+        [early_ref[...].reshape(rows, chunk), late_ref[...].reshape(rows, chunk)], axis=0
+    )
+    part = jnp.dot(both, table_ref[...], preferred_element_type=f32)
 
     @pl.when(step == 0)
     def _():
@@ -44,29 +55,47 @@
 
     @pl.when(step == pl.num_programs(0) - 1)
     def _():
-        spec_ref[...] = (acc[...] * live_ref[...]).astype(bf)
+        even, odd = quarter_turn(acc[rows:, :band], acc[rows:, band:], 1.0)
+        spec_ref[:, :band] = ((acc[:rows, :band] + even) * live_ref[...]).astype(bf)
+        spec_ref[:, band:] = ((acc[:rows, band:] + odd) * live_ref[...]).astype(bf)
+
 
 def forward(traces, live):
     shots, chans, samples = traces.shape
     band = samples // 16
     rows = shots * chans
-    cc, cs = wave(jnp.arange(samples // FINE, dtype=jnp.int32) * FINE, samples, band)
+    steps = samples // 2 // CHUNK
+    cc, cs = wave(jnp.arange(samples // 2 // FINE, dtype=jnp.int32) * FINE, samples, band)
     fc, fs = wave(jnp.arange(FINE, dtype=jnp.int32), samples, band)
     return pl.pallas_call(
-        forward_kernel, grid=(samples // CHUNK,),
-        out_shape=(jax.ShapeDtypeStruct((rows, 2 * band), bf), jax.ShapeDtypeStruct((samples, 2 * band), bf)),
-        in_specs=[pl.BlockSpec((shots, chans, CHUNK), lambda i: (0, 0, i)), VM, VM, VM, VM, VM],
-        out_specs=(pl.BlockSpec((rows, 2 * band), lambda i: (0, 0)), pl.BlockSpec((CHUNK, 2 * band), lambda i: (i, 0))),
-        scratch_shapes=[pltpu.VMEM((rows, 2 * band), f32)],
+        forward_kernel,
+        grid=(steps,),
+        out_shape=(
+            jax.ShapeDtypeStruct((rows, 2 * band), bf),
+            jax.ShapeDtypeStruct((samples // 2, 2 * band), bf),
+        ),
+        in_specs=[
+            pl.BlockSpec((shots, chans, CHUNK), lambda i: (0, 0, i)),
+            pl.BlockSpec((shots, chans, CHUNK), lambda i: (0, 0, i + steps)),
+        ]
+        + [VM] * 5,
+        out_specs=(
+            pl.BlockSpec((rows, 2 * band), lambda i: (0, 0)),
+            pl.BlockSpec((CHUNK, 2 * band), lambda i: (i, 0)),
+        ),
+        scratch_shapes=[pltpu.VMEM((2 * rows, 2 * band), f32)],
         compiler_params=pltpu.CompilerParams(vmem_limit_bytes=40 * 2**20),
-    )(traces, live.reshape(rows, 1), cc, cs, fc, fs)
+    )(traces, traces, live.reshape(rows, 1), cc, cs, fc, fs)
+
 
 def inverse_kernel(order_ref, filter_ref, own_ref, cos_ref, sin_ref, live_ref, table_ref, *refs):
-    *piece_refs, out_ref, error, full = refs
+    *piece_refs, out_ref, error, full, later = refs
+    half = pl.program_id(1)
+    rows = own_ref.shape[0]
     shots, chans, chunk = out_ref.shape
     band = cos_ref.shape[1]
 
-    @pl.when(pl.program_id(0) == 0)
+    @pl.when((pl.program_id(0) == 0) & (half == 0))
     def _():
         weights = filter_ref[...].reshape(LAGS * chans, filter_ref.shape[2])
         for s in range(shots):
@@ -83,25 +112,45 @@
             error[at, :band] = (own_ref[at, :band].astype(f32) - even).astype(bf)
             error[at, band:] = (own_ref[at, band:].astype(f32) - odd).astype(bf)
 
-    restored = lax.dot_general(error[...], table_ref[...], (((1,), (1,)), ((), ())), preferred_element_type=f32)
-    samples = pl.num_programs(0) * chunk
-    out_ref[...] = (restored * (1.0 / samples) * live_ref[...]).astype(bf).reshape(out_ref.shape)
+        turned = quarter_turn(error[:rows, :band].astype(f32), error[:rows, band:].astype(f32), -1.0)
+        error[rows:, :band] = turned[0].astype(bf)
+        error[rows:, band:] = turned[1].astype(bf)
+
+    samples = 2 * pl.num_programs(0) * chunk
+
+    @pl.when(half == 0)
+    def _():
+        restored = lax.dot_general(
+            error[...], table_ref[...], (((1,), (1,)), ((), ())), preferred_element_type=f32
+        )
+        later[...] = (restored[rows:] * (1.0 / samples) * live_ref[...]).astype(bf)
+        out_ref[...] = (restored[:rows] * (1.0 / samples) * live_ref[...]).astype(bf).reshape(out_ref.shape)
+
+    @pl.when(half == 1)
+    def _():
+        out_ref[...] = later[...].reshape(out_ref.shape)
+
 
 def inverse(order, filter_bf, pieces, own_rows, cosine, sine, live, table):
     shots, chans = live.shape
     rows, width = own_rows.shape
-    samples = table.shape[0]
+    samples = 2 * table.shape[0]
+    steps = table.shape[0] // BACK_CHUNK
     channels = filter_bf.shape[2]
     return pl.pallas_call(
         inverse_kernel,
-        grid=(samples // CHUNK,),
+        grid=(steps, 2),
         out_shape=jax.ShapeDtypeStruct((shots, chans, samples), bf),
         in_specs=[pl.BlockSpec(memory_space=pltpu.SMEM)]
         + [VM] * 5
-        + [pl.BlockSpec((CHUNK, width), lambda i: (i, 0))]
+        + [pl.BlockSpec((BACK_CHUNK, width), lambda i, h: (i, 0))]
         + [VM] * len(pieces),
-        out_specs=pl.BlockSpec((shots, chans, CHUNK), lambda i: (0, 0, i)),
-        scratch_shapes=[pltpu.VMEM((rows, width), bf), pltpu.VMEM((channels, width), bf)],
+        out_specs=pl.BlockSpec((shots, chans, BACK_CHUNK), lambda i, h: (0, 0, i + h * steps)),
+        scratch_shapes=[
+            pltpu.VMEM((2 * rows, width), bf),
+            pltpu.VMEM((channels, width), bf),
+            pltpu.VMEM((rows, BACK_CHUNK), bf),
+        ],
         compiler_params=pltpu.CompilerParams(vmem_limit_bytes=40 * 2**20),
     )(order, filter_bf, own_rows, cosine, sine, live.reshape(rows, 1), table, *pieces)
 
@@ -159,29 +208,33 @@
     return lax.dot_general(a, b, (((ca,), (cb,)), ((), ())), precision=lax.Precision.HIGHEST, preferred_element_type=f32)
 
 def solve_kernel(order_ref, rhs_ref, *refs):
-    *piece_refs, out_ref, corr_ref, tiles, gains, ys, block, whole, spare = refs
-    n = corr_ref.shape[1]
-    for k in range(LAGS):
-        place(order_ref, piece_refs, k, corr_ref.at[k])
+    *piece_refs, out_ref, columns, gains, block, whole, spare = refs
+    chans, n = rhs_ref.shape[1:]
     h = n // 2
-    eye = lax.broadcasted_iota(jnp.int32, (n, n), 0) == lax.broadcasted_iota(jnp.int32, (n, n), 1)
-    zero_lag = corr_ref[0]
-    whiten = 0.1 * jnp.sum(jnp.where(eye, zero_lag, 0.0)) / n + 1e-06
-    zero_lag = zero_lag + jnp.where(eye, whiten, 0.0)
-    for i in range(LAGS):
-        tiles[i, i] = zero_lag
-        for j in range(i):
-            tiles[i, j] = corr_ref[i - j]
-        ys[i] = rhs_ref[i]
-    block[...] = zero_lag[:h, :h]
+    end = LAGS * n + chans
+    count = 0
+    for ref in piece_refs:
+        for i in range(ref.shape[0]):
+            start = pl.multiple_of(order_ref[count] * chans, chans)
+            for k in range(LAGS):
+                for j in range(LAGS - k):
+                    columns[j, pl.ds((j + k) * n + start, chans), :] = ref[i, k]
+            count += 1
+    for j in range(LAGS):
+        columns[j, LAGS * n :, :] = rhs_ref[j]
+    row = lax.broadcasted_iota(jnp.int32, (n, n), 0)
+    eye = row == lax.broadcasted_iota(jnp.int32, (n, n), 1)
+    whiten = 0.1 * jnp.sum(jnp.where(eye, columns[0, :n], 0.0)) / n + 1e-06
+    whiten = jnp.where(eye[:h, :h], whiten, 0.0)
+    block[...] = columns[0, :h, :h] + whiten
 
     def first_half(p):
         inv = block[...]
-        corner = tiles[p, p, h:, :h]
+        corner = columns[p, p * n + h : (p + 1) * n, :h]
         left = mm(corner, inv)
         whole[:h, :h] = inv
         whole[h:, :h] = left
-        block[...] = tiles[p, p, h:, h:] - mm(left, corner, 1, 1)
+        block[...] = columns[p, p * n + h : (p + 1) * n, h:] + whiten - mm(left, corner, 1, 1)
 
     def second_half(p):
         inv = block[...]
@@ -191,17 +244,13 @@
         whole[h:, :h] = -low
         whole[:h, h:] = -low.T
         whole[h:, h:] = inv
-        full = whole[...]
-        for i in range(p + 1, LAGS):
-            gains[i, p] = mm(tiles[i, p], full)
-            for j in range(p + 1, i + 1):
-                tiles[i, j] -= mm(gains[i, p], tiles[j, p], 1, 1)
+        below = (p + 1) * n
+        gain = mm(columns[p, below:, :], whole[...])
+        gains[p, below:, :] = gain
+        for j in range(p + 1, LAGS):
+            columns[j, j * n :, :] -= mm(gain[j * n - below :], columns[p, j * n : (j + 1) * n, :], 1, 1)
         if p + 1 < LAGS:
-            block[...] = tiles[p + 1, p + 1, :h, :h]
-        y = mm(ys[p], full)
-        ys[p] = y
-        for j in range(p + 1, LAGS):
-            ys[j] -= mm(y, tiles[j, p], 1, 1)
+            block[...] = columns[p + 1, below : below + h, :h] + whiten
 
     def step(q, carry):
         even = 0.5 * (block[...] + block[...].T)
@@ -214,12 +263,14 @@
         return carry
 
     lax.fori_loop(0, 2 * LAGS, step, 0)
+    solved = {}
     for p in reversed(range(LAGS)):
-        x = ys[p]
+        x = gains[p, LAGS * n : end, :]
         for j in range(p + 1, LAGS):
-            x = x - mm(ys[j], gains[j, p])
-        ys[p] = x
+            x = x - mm(solved[j], gains[p, j * n : (j + 1) * n, :])
+        solved[p] = x
         out_ref[p] = x.astype(out_ref.dtype)
+
 
 def solve_filter(order, pieces, rhs):
     chans = rhs.shape[1]
@@ -231,10 +282,8 @@
         in_specs=[pl.BlockSpec(memory_space=pltpu.SMEM)] + [VM] * (1 + len(pieces)),
         out_specs=VM,
         scratch_shapes=[
-            pltpu.VMEM((LAGS, n, n), f32),
-            pltpu.VMEM((LAGS, LAGS, n, n), f32),
-            pltpu.VMEM((LAGS, LAGS, n, n), f32),
-            pltpu.VMEM((LAGS, chans, n), f32),
+            pltpu.VMEM((LAGS, LAGS * n + chans, n), f32),
+            pltpu.VMEM((LAGS, LAGS * n + chans, n), f32),
             pltpu.VMEM((half, half), f32),
             pltpu.VMEM((n, n), f32),
             pltpu.VMEM((2, 9, 8, half), f32),
@@ -325,13 +374,6 @@
     return jnp.stack(places).astype(jnp.int32)
 
 
-def gather_all(x, axis):
-    parts = lax.axis_size(axis)
-    return lax.all_to_all(
-        jnp.broadcast_to(x[None], (parts,) + x.shape), axis, split_axis=0, concat_axis=0, tiled=True
-    )
-
-
 def sum_over_shot(value):
     for bit in (8, 1, 2, 4):
         pairs = [(i, i ^ bit) for i in range(16)]
@@ -356,11 +398,10 @@
     channels = partial_value.shape[1]
     total_shots = shot_count * lax.axis_size("shot")
     scale = (1.0 / samples) * (1.0 / (samples * total_shots))
-    half = LAGS * local_chan
-    targets = jnp.sum(gather_all(partial_value[half:], "shot"), axis=0) * scale
-    summed = sum_over_shot(partial_value[:half]) * scale
-    correlation = gather_lag(summed.reshape(LAGS, local_chan, channels))
-    filter_bf = solve_filter(order, correlation, targets.reshape(LAGS, local_chan, channels))
+    summed = sum_over_shot(partial_value) * scale
+    summed = summed.reshape(2 * LAGS, local_chan, channels)
+    correlation = gather_lag(summed[:LAGS])
+    filter_bf = solve_filter(order, correlation, summed[LAGS:])
     return inverse(order, filter_bf, spectra, own_rows, cosine[LAGS:], sine[LAGS:], live, table)
 
 

time: 181 us -> 144 us (0.80)
  waiting for transfers between devices: 44.8 us -> 24 us
  Pallas kernels: 70.1 us -> 54.5 us
  other arithmetic: 6.01 us -> 2.42 us
  local copies, waits for them, and re-layouts: 5.1 us -> 8.28 us
    ppermute x4, waiting for transfers between devices: 32.1 us -> 12.5 us  [sum_over_shot(): value = value + lax.ppermute(value, 'shot', pairs)]
    pallas_call x2, Pallas kernels: 22.6 us -> 9.19 us  [the longest x1 5.56 us: inverse(): pl.pallas_call(inverse_kernel, grid=(steps, 2), out_shape=jax.ShapeDtypeS...]
    all_to_all x1 -> x0, starting transfers between devices: 10.8 us -> none  [gather_all(): lax.all_to_all(jnp.broadcast_to(x[None], (parts,) + x.shape), axis, split...]
    ppermute x10, starting transfers between devices: 18.4 us -> 26 us  [gather_lag(): return near + [lax.ppermute(piece, 'lag', over_core) for piece in near]]
    unnamed x2 -> x6, local copies, waits for them, and re-layouts: 1.4 us -> 8.05 us
    ppermute x2, waiting for transfers between devices: 5.69 us -> 0.01 us  [gather_lag(): below = lax.ppermute(pair, 'lag', up)]
    ppermute x2, waiting for transfers between devices: 0.01 us -> 4.26 us  [gather_lag(): above = lax.ppermute(pair, 'lag', down)]
    ppermute x4, starting transfers between devices: 9.86 us -> 13.7 us  [sum_over_shot(): value = value + lax.ppermute(value, 'shot', pairs)]
  transfers between devices with their start and end apart: 25 -> 24, of which waited for: 10 -> 9; matrix products, arithmetic and copies ran while one was open for 3% -> 0% of each run, Pallas kernels for 0% -> 0%
where the time goes in v4:
time: 144 us
  Pallas kernels  54.5 us (38%)
  starting transfers between devices  53.9 us (37%)
  waiting for transfers between devices  24 us (17%)
  local copies, waits for them, and re-layouts  8.28 us (6%)
  other arithmetic  2.42 us (2%)
    pallas_call x1, Pallas kernels, solve_filter(): pl.pallas_call(solve_kernel, out_shape=jax.ShapeDtypeStruct((LAGS, chans,...  43.3 us
    ppermute x10, starting transfers between devices, gather_lag(): return near + [lax.ppermute(piece, 'lag', over_core) for piece in near]  26 us
    ppermute x4, starting transfers between devices, sum_over_shot(): value = value + lax.ppermute(value, 'shot', pairs)  13.7 us
    ppermute x4, waiting for transfers between devices, sum_over_shot(): value = value + lax.ppermute(value, 'shot', pairs)  12.5 us
    unnamed x6, local copies, waits for them, and re-layouts  8.05 us
    pallas_call x1, Pallas kernels, inverse(): pl.pallas_call(inverse_kernel, grid=(steps, 2), out_shape=jax.ShapeDtypeS...  5.56 us
    ppermute x2, waiting for transfers between devices, gather_lag(): pair = jnp.concatenate([own, lax.ppermute(own, 'lag', over_x)], axis=0)  5.47 us
    ppermute x2, starting transfers between devices, gather_lag(): far_other = lax.ppermute(above[1:], 'lag', down)  4.88 us
  transfers between devices with their start and end apart: 24, of which 9 were waited for; matrix products, arithmetic and copies ran while one was open for 0% of the time, Pallas kernels for 0%

profile of v4, /device:TPU:1, one launch (start us, length us, event | category | flops | bytes accessed | tf_op | source)
XLA Modules:
  0.0 143.9 jit_solution(647317201969785160)
XLA Ops:
  2.2 1.4 copy-done.2
  3.6 3.6 %shard_map.37 = (bf16[96,1024]{1,0:T(8,128)(2,1)S(1)}, bf16[4096,1024]{1,0:T(8,128)(2,1)S(1)}) custom-call(bf16[6,16,8192]{2,1,0:T(8,128)(2,1)S(1)} %copy-done.2, bf16[6,16,8192]{2,1,0:T(8,128)(2,1)S(1)} %copy-done.2, f32[96,1]{1,0:T(8,128)S(1)} %reshape.23.live_ref, f32[32,512]{1,0:T(8,128)S(1)} %get-tuple-element.15.cc_ref, ...), custom_call_target="tpu_custom_call" | custom-call | tf_op jit(solution)/shard_map/pallas_call | solution.py:70
  7.2 3.3 %copy-done = bf16[4096,1024]{1,0:T(8,128)(2,1)} copy-done((bf16[4096,1024]{1,0:T(8,128)(2,1)}, bf16[4096,1024]{1,0:T(8,128)(2,1)S(1)}, u32[]{:S(2)}) %copy-start) | copy-done | bytes 8388632
  10.5 2.1 %collective-permute-start = (bf16[1,6,16,1024]{3,2,1,0:T(8,128)(2,1)S(1)}, bf16[1,6,16,1024]{3,2,1,0:T(8,128)(2,1)S(1)}, u32[]{:S(2)}, u32[]{:S(2)}) collective-permute-start(bf16[1,6,16,1024]{3,2,1,0:T(8,128)(2,1)S(1)} %bitcast.21), channel_id=1, source_target_pairs={{0,8},{1,9},{2,10},{3,11},{4,12},{5,13},{6,14},{7,15},{8,0},{9,1},... | collective-permute-start | bytes 589832 | tf_op jit(solution)/shard_map/ppermute | solution.py:357
  12.5 3.3 %collective-permute-done = bf16[1,6,16,1024]{3,2,1,0:T(8,128)(2,1)S(1)} collective-permute-done((bf16[1,6,16,1024]{3,2,1,0:T(8,128)(2,1)S(1)}, bf16[1,6,16,1024]{3,2,1,0:T(8,128)(2,1)S(1)}, u32[]{:S(2)}, u32[]{:S(2)}) %collective-permute-start) | collective-permute-done | bytes 196640 | tf_op jit(solution)/shard_map/ppermute | solution.py:357
  15.9 4.1 %collective-permute-start.2 = (bf16[2,6,16,1024]{3,2,1,0:T(8,128)(2,1)S(1)}, bf16[2,6,16,1024]{3,2,1,0:T(8,128)(2,1)S(1)}, u32[]{:S(2)}, u32[]{:S(2)}) collective-permute-start(bf16[2,6,16,1024]{3,2,1,0:T(8,128)(2,1)S(1)} %pad_maximum_fusion.refs_0_), channel_id=1, source_target_pairs={{0,6},{1,7},{2,0},{3,1},{4,2},{5,3},{6,4},{7,5},{8,14},{9,15},{10,... | collective-permute-start | bytes 1179656 | tf_op jit(solution)/shard_map/ppermute | solution.py:359
  20.6 1.9 %collective-permute-start.5 = (bf16[2,6,16,1024]{3,2,1,0:T(8,128)(2,1)S(1)}, bf16[2,6,16,1024]{3,2,1,0:T(8,128)(2,1)S(1)}, u32[]{:S(2)}, u32[]{:S(2)}) collective-permute-start(bf16[2,6,16,1024]{3,2,1,0:T(8,128)(2,1)S(1)} %pad_maximum_fusion.refs_0_), channel_id=1, source_target_pairs={{0,1},{1,0},{2,3},{3,2},{4,5},{5,4},{6,7},{7,6},{8,9},{9,8},{10,11... | collective-permute-start | bytes 1179656 | tf_op jit(solution)/shard_map/ppermute | solution.py:363
  22.5 4.3 %collective-permute-done.2.refs_2_ = bf16[2,6,16,1024]{3,2,1,0:T(8,128)(2,1)S(1)} collective-permute-done((bf16[2,6,16,1024]{3,2,1,0:T(8,128)(2,1)S(1)}, bf16[2,6,16,1024]{3,2,1,0:T(8,128)(2,1)S(1)}, u32[]{:S(2)}, u32[]{:S(2)}) %collective-permute-start.2) | collective-permute-done | bytes 393248 | tf_op jit(solution)/shard_map/ppermute | solution.py:359
  26.8 3.5 %collective-permute-start.4 = (bf16[1,6,16,1024]{3,2,1,0:T(8,128)(2,1)S(1)}, bf16[1,6,16,1024]{3,2,1,0:T(8,128)(2,1)S(1)}, u32[]{:S(2)}, u32[]{:S(2)}) collective-permute-start(bf16[1,6,16,1024]{3,2,1,0:T(8,128)(2,1)S(1)} %slice.38), channel_id=1, source_target_pairs={{0,6},{1,7},{2,0},{3,1},{4,2},{5,3},{6,4},{7,5},{8,14},{9,15},{10,... | collective-permute-start | bytes 589832 | tf_op jit(solution)/shard_map/ppermute | solution.py:361
  30.4 2.8 %collective-permute-start.7 = (bf16[2,6,16,1024]{3,2,1,0:T(8,128)(2,1)S(1)}, bf16[2,6,16,1024]{3,2,1,0:T(8,128)(2,1)S(1)}, u32[]{:S(2)}, u32[]{:S(2)}) collective-permute-start(bf16[2,6,16,1024]{3,2,1,0:T(8,128)(2,1)S(1)} %collective-permute-done.2.refs_2_), channel_id=1, source_target_pairs={{0,1},{1,0},{2,3},{3,2},{4,5},{5,4},{6,7},{7,6},{8,9},{9,8},{10,11... | collective-permute-start | bytes 1179656 | tf_op jit(solution)/shard_map/ppermute | solution.py:363
  33.5 2.7 %collective-permute-start.9 = (bf16[1,6,16,1024]{3,2,1,0:T(8,128)(2,1)S(1)}, bf16[1,6,16,1024]{3,2,1,0:T(8,128)(2,1)S(1)}, u32[]{:S(2)}, u32[]{:S(2)}) collective-permute-start(bf16[1,6,16,1024]{3,2,1,0:T(8,128)(2,1)S(1)} %collective-permute-done.4.refs_4_), channel_id=1, source_target_pairs={{0,1},{1,0},{2,3},{3,2},{4,5},{5,4},{6,7},{7,6},{8,9},{9,8},{10,11... | collective-permute-start | bytes 589832 | tf_op jit(solution)/shard_map/ppermute | solution.py:363
  36.2 3.8 %collective-permute-start.8 = (bf16[1,6,16,1024]{3,2,1,0:T(8,128)(2,1)S(1)}, bf16[1,6,16,1024]{3,2,1,0:T(8,128)(2,1)S(1)}, u32[]{:S(2)}, u32[]{:S(2)}) collective-permute-start(bf16[1,6,16,1024]{3,2,1,0:T(8,128)(2,1)S(1)} %collective-permute-done.3.refs_3_), channel_id=1, source_target_pairs={{0,1},{1,0},{2,3},{3,2},{4,5},{5,4},{6,7},{7,6},{8,9},{9,8},{10,11... | collective-permute-start | bytes 589832 | tf_op jit(solution)/shard_map/ppermute | solution.py:363
  41.1 2.0 %shard_map.38 = f32[128,256]{1,0:T(8,128)S(1)} custom-call(s32[16]{0:T(128)S(1)} %stack.67.order_ref, bf16[96,1024]{1,0:T(8,128)(2,1)S(1)} %get-tuple-element.7.own_ref, f32[8,512]{1,0:T(8,128)S(1)} %get-tuple-element.13.cos_ref, f32[8,512]{1,0:T(8,128)S(1)} %get-tuple-element.12.sin_ref, bf16[2,6,16,1024]{3,2,1,0:T(8,128)(2,1)S(1)} %pad_maximum_fusion.refs_0_, ...), custom_call_target="tpu_custom_call" | custom-call | tf_op jit(solution)/shard_map/pallas_call | solution.py:332
  43.1 2.9 %collective-permute-start.10 = (f32[128,256]{1,0:T(8,128)S(1)}, f32[128,256]{1,0:T(8,128)S(1)}, u32[]{:S(2)}, u32[]{:S(2)}) collective-permute-start(f32[128,256]{1,0:T(8,128)S(1)} %shard_map.38), channel_id=1, source_target_pairs={{0,128},{16,144},{32,160},{48,176},{64,192},{80,208},{96,224},{112... | collective-permute-start | bytes 393224 | tf_op jit(solution)/shard_map/ppermute | solution.py:380
  46.0 3.4 %collective-permute-done.10 = f32[128,256]{1,0:T(8,128)S(1)} collective-permute-done((f32[128,256]{1,0:T(8,128)S(1)}, f32[128,256]{1,0:T(8,128)S(1)}, u32[]{:S(2)}, u32[]{:S(2)}) %collective-permute-start.10) | collective-permute-done | bytes 131104 | tf_op jit(solution)/shard_map/ppermute | solution.py:380
  49.4 1.9 %collective-permute-start.11 = (f32[128,256]{1,0:T(8,128)S(1)}, f32[128,256]{1,0:T(8,128)S(1)}, u32[]{:S(2)}, u32[]{:S(2)}) collective-permute-start(f32[128,256]{1,0:T(8,128)S(1)} %add.227), channel_id=1, source_target_pairs={{0,16},{16,0},{32,48},{48,32},{64,80},{80,64},{96,112},{112,96},{1... | collective-permute-start | bytes 393224 | tf_op jit(solution)/shard_map/ppermute | solution.py:380
  51.3 2.4 %collective-permute-done.11 = f32[128,256]{1,0:T(8,128)S(1)} collective-permute-done((f32[128,256]{1,0:T(8,128)S(1)}, f32[128,256]{1,0:T(8,128)S(1)}, u32[]{:S(2)}, u32[]{:S(2)}) %collective-permute-start.11) | collective-permute-done | bytes 131104 | tf_op jit(solution)/shard_map/ppermute | solution.py:380
  53.7 3.1 %collective-permute-start.12 = (f32[128,256]{1,0:T(8,128)S(1)}, f32[128,256]{1,0:T(8,128)S(1)}, u32[]{:S(2)}, u32[]{:S(2)}) collective-permute-start(f32[128,256]{1,0:T(8,128)S(1)} %add.228), channel_id=1, source_target_pairs={{0,32},{16,48},{32,0},{48,16},{64,96},{80,112},{96,64},{112,80},{1... | collective-permute-start | bytes 393224 | tf_op jit(solution)/shard_map/ppermute | solution.py:380
  56.8 4.1 %collective-permute-done.12 = f32[128,256]{1,0:T(8,128)S(1)} collective-permute-done((f32[128,256]{1,0:T(8,128)S(1)}, f32[128,256]{1,0:T(8,128)S(1)}, u32[]{:S(2)}, u32[]{:S(2)}) %collective-permute-start.12) | collective-permute-done | bytes 131104 | tf_op jit(solution)/shard_map/ppermute | solution.py:380
  60.9 5.8 %collective-permute-start.13 = (f32[128,256]{1,0:T(8,128)S(1)}, f32[128,256]{1,0:T(8,128)S(1)}, u32[]{:S(2)}, u32[]{:S(2)}) collective-permute-start(f32[128,256]{1,0:T(8,128)S(1)} %add.229), channel_id=1, source_target_pairs={{0,64},{16,80},{32,96},{48,112},{64,0},{80,16},{96,32},{112,48},{1... | collective-permute-start | bytes 393224 | tf_op jit(solution)/shard_map/ppermute | solution.py:380
  66.8 2.6 %collective-permute-done.13 = f32[128,256]{1,0:T(8,128)S(1)} collective-permute-done((f32[128,256]{1,0:T(8,128)S(1)}, f32[128,256]{1,0:T(8,128)S(1)}, u32[]{:S(2)}, u32[]{:S(2)}) %collective-permute-start.13) | collective-permute-done | bytes 131104 | tf_op jit(solution)/shard_map/ppermute | solution.py:380
  69.4 1.3 collective-permute-start.14
  70.7 2.2 %collective-permute-done.14 = f32[1,4,16,256]{3,2,1,0:T(8,128)S(1)} collective-permute-done((f32[1,4,16,256]{3,2,1,0:T(8,128)S(1)}, f32[1,4,16,256]{3,2,1,0:T(8,128)S(1)}, u32[]{:S(2)}, u32[]{:S(2)}) %collective-permute-start.14) | collective-permute-done | bytes 65568 | tf_op jit(solution)/shard_map/ppermute | solution.py:357
  73.2 1.2 collective-permute-start.15
  74.4 6.2 %collective-permute-start.19 = (f32[2,4,16,256]{3,2,1,0:T(8,128)S(1)}, f32[2,4,16,256]{3,2,1,0:T(8,128)S(1)}, u32[]{:S(2)}, u32[]{:S(2)}) collective-permute-start(f32[2,4,16,256]{3,2,1,0:T(8,128)S(1)} %pad_maximum_fusion.1.refs_0_), channel_id=1, source_target_pairs={{0,1},{1,0},{2,3},{3,2},{4,5},{5,4},{6,7},{7,6},{8,9},{9,8},{10,11... | collective-permute-start | bytes 393224 | tf_op jit(solution)/shard_map/ppermute | solution.py:363
  80.6 1.4 collective-permute-start.18
  82.3 3.4 %collective-permute-start.21 = (f32[2,4,16,256]{3,2,1,0:T(8,128)S(1)}, f32[2,4,16,256]{3,2,1,0:T(8,128)S(1)}, u32[]{:S(2)}, u32[]{:S(2)}) collective-permute-start(f32[2,4,16,256]{3,2,1,0:T(8,128)S(1)} %collective-permute-done.16.refs_2_), channel_id=1, source_target_pairs={{0,1},{1,0},{2,3},{3,2},{4,5},{5,4},{6,7},{7,6},{8,9},{9,8},{10,11... | collective-permute-start | bytes 393224 | tf_op jit(solution)/shard_map/ppermute | solution.py:363
  85.7 2.1 %collective-permute-start.23 = (f32[1,4,16,256]{3,2,1,0:T(8,128)S(1)}, f32[1,4,16,256]{3,2,1,0:T(8,128)S(1)}, u32[]{:S(2)}, u32[]{:S(2)}) collective-permute-start(f32[1,4,16,256]{3,2,1,0:T(8,128)S(1)} %collective-permute-done.18.refs_4_), channel_id=1, source_target_pairs={{0,1},{1,0},{2,3},{3,2},{4,5},{5,4},{6,7},{7,6},{8,9},{9,8},{10,11... | collective-permute-start | bytes 196616 | tf_op jit(solution)/shard_map/ppermute | solution.py:363
  87.9 2.9 %collective-permute-start.22 = (f32[1,4,16,256]{3,2,1,0:T(8,128)S(1)}, f32[1,4,16,256]{3,2,1,0:T(8,128)S(1)}, u32[]{:S(2)}, u32[]{:S(2)}) collective-permute-start(f32[1,4,16,256]{3,2,1,0:T(8,128)S(1)} %collective-permute-done.17.refs_3_), channel_id=1, source_target_pairs={{0,1},{1,0},{2,3},{3,2},{4,5},{5,4},{6,7},{7,6},{8,9},{9,8},{10,11... | collective-permute-start | bytes 196616 | tf_op jit(solution)/shard_map/ppermute | solution.py:363
  91.6 43.3 %shard_map.39.filter_ref = bf16[4,16,256]{2,1,0:T(8,128)(2,1)S(1)} custom-call(s32[16]{0:T(128)S(1)} %stack.67.order_ref, f32[4,16,256]{2,1,0:T(8,128)S(1)} %bitcast.23, f32[2,4,16,256]{3,2,1,0:T(8,128)S(1)} %pad_maximum_fusion.1.refs_0_, f32[2,4,16,256]{3,2,1,0:T(8,128)S(1)} %collective-permute-done.15.refs_1_, ...), custom_call_target="tpu_custom_call" | custom-call | tf_op jit(solution)/shard_map/pallas_call | solution.py:279
  135.0 3.4 %copy-done.1 = bf16[4096,1024]{1,0:T(8,128)(2,1)S(1)} copy-done((bf16[4096,1024]{1,0:T(8,128)(2,1)S(1)}, bf16[4096,1024]{1,0:T(8,128)(2,1)}, u32[]{:S(2)}) %copy-start.1) | copy-done | bytes 8388632
  138.3 5.6 %shard_map.40 = bf16[6,16,8192]{2,1,0:T(8,128)(2,1)} custom-call(s32[16]{0:T(128)S(1)} %stack.67.order_ref, bf16[4,16,256]{2,1,0:T(8,128)(2,1)S(1)} %shard_map.39.filter_ref, bf16[96,1024]{1,0:T(8,128)(2,1)S(1)} %get-tuple-element.7.own_ref, f32[4,512]{1,0:T(4,128)S(1)} %slice.43.cos_ref, f32[4,512]{1,0:T(4,128)S(1)} %slice.44.sin_ref, ...), custom_call_target="tpu_custom_call" | custom-call | tf_op jit(solution)/shard_map/pallas_call | solution.py:140
  (50 shorter events, 5.2 us)
Async XLA Ops:
  2.2 1.4 copy-start.2
  7.2 3.3 %copy-start = (bf16[4096,1024]{1,0:T(8,128)(2,1)}, bf16[4096,1024]{1,0:T(8,128)(2,1)S(1)}, u32[]{:S(2)}) copy-start(bf16[4096,1024]{1,0:T(8,128)(2,1)S(1)} %get-tuple-element.8.table_ref) | copy-start | bytes 25165828
  10.5 5.3 %collective-permute-start = (bf16[1,6,16,1024]{3,2,1,0:T(8,128)(2,1)S(1)}, bf16[1,6,16,1024]{3,2,1,0:T(8,128)(2,1)S(1)}, u32[]{:S(2)}, u32[]{:S(2)}) collective-permute-start(bf16[1,6,16,1024]{3,2,1,0:T(8,128)(2,1)S(1)} %bitcast.21), channel_id=1, source_target_pairs={{0,8},{1,9},{2,10},{3,11},{4,12},{5,13},{6,14},{7,15},{8,0},{9,1},... | collective-permute-start | bytes 589832 | tf_op jit(solution)/shard_map/ppermute | solution.py:357
  15.9 10.9 %collective-permute-start.2 = (bf16[2,6,16,1024]{3,2,1,0:T(8,128)(2,1)S(1)}, bf16[2,6,16,1024]{3,2,1,0:T(8,128)(2,1)S(1)}, u32[]{:S(2)}, u32[]{:S(2)}) collective-permute-start(bf16[2,6,16,1024]{3,2,1,0:T(8,128)(2,1)S(1)} %pad_maximum_fusion.refs_0_), channel_id=1, source_target_pairs={{0,6},{1,7},{2,0},{3,1},{4,2},{5,3},{6,4},{7,5},{8,14},{9,15},{10,... | collective-permute-start | bytes 1179656 | tf_op jit(solution)/shard_map/ppermute | solution.py:359
  19.9 10.4 %collective-permute-start.1 = (bf16[2,6,16,1024]{3,2,1,0:T(8,128)(2,1)S(1)}, bf16[2,6,16,1024]{3,2,1,0:T(8,128)(2,1)S(1)}, u32[]{:S(2)}, u32[]{:S(2)}) collective-permute-start(bf16[2,6,16,1024]{3,2,1,0:T(8,128)(2,1)S(1)} %pad_maximum_fusion.refs_0_), channel_id=1, source_target_pairs={{0,2},{1,3},{2,4},{3,5},{4,6},{5,7},{6,0},{7,1},{8,10},{9,11},{10,... | collective-permute-start | bytes 1179656 | tf_op jit(solution)/shard_map/ppermute | solution.py:358
  20.6 19.6 %collective-permute-start.5 = (bf16[2,6,16,1024]{3,2,1,0:T(8,128)(2,1)S(1)}, bf16[2,6,16,1024]{3,2,1,0:T(8,128)(2,1)S(1)}, u32[]{:S(2)}, u32[]{:S(2)}) collective-permute-start(bf16[2,6,16,1024]{3,2,1,0:T(8,128)(2,1)S(1)} %pad_maximum_fusion.refs_0_), channel_id=1, source_target_pairs={{0,1},{1,0},{2,3},{3,2},{4,5},{5,4},{6,7},{7,6},{8,9},{9,8},{10,11... | collective-permute-start | bytes 1179656 | tf_op jit(solution)/shard_map/ppermute | solution.py:363
  26.8 6.7 %collective-permute-start.4 = (bf16[1,6,16,1024]{3,2,1,0:T(8,128)(2,1)S(1)}, bf16[1,6,16,1024]{3,2,1,0:T(8,128)(2,1)S(1)}, u32[]{:S(2)}, u32[]{:S(2)}) collective-permute-start(bf16[1,6,16,1024]{3,2,1,0:T(8,128)(2,1)S(1)} %slice.38), channel_id=1, source_target_pairs={{0,6},{1,7},{2,0},{3,1},{4,2},{5,3},{6,4},{7,5},{8,14},{9,15},{10,... | collective-permute-start | bytes 589832 | tf_op jit(solution)/shard_map/ppermute | solution.py:361
  30.3 5.9 %collective-permute-start.3 = (bf16[1,6,16,1024]{3,2,1,0:T(8,128)(2,1)S(1)}, bf16[1,6,16,1024]{3,2,1,0:T(8,128)(2,1)S(1)}, u32[]{:S(2)}, u32[]{:S(2)}) collective-permute-start(bf16[1,6,16,1024]{3,2,1,0:T(8,128)(2,1)S(1)} %slice.37), channel_id=1, source_target_pairs={{0,2},{1,3},{2,4},{3,5},{4,6},{5,7},{6,0},{7,1},{8,10},{9,11},{10,... | collective-permute-start | bytes 589832 | tf_op jit(solution)/shard_map/ppermute | solution.py:360
  30.4 9.8 %collective-permute-start.7 = (bf16[2,6,16,1024]{3,2,1,0:T(8,128)(2,1)S(1)}, bf16[2,6,16,1024]{3,2,1,0:T(8,128)(2,1)S(1)}, u32[]{:S(2)}, u32[]{:S(2)}) collective-permute-start(bf16[2,6,16,1024]{3,2,1,0:T(8,128)(2,1)S(1)} %collective-permute-done.2.refs_2_), channel_id=1, source_target_pairs={{0,1},{1,0},{2,3},{3,2},{4,5},{5,4},{6,7},{7,6},{8,9},{9,8},{10,11... | collective-permute-start | bytes 1179656 | tf_op jit(solution)/shard_map/ppermute | solution.py:363
  33.2 7.9 %collective-permute-start.6 = (bf16[2,6,16,1024]{3,2,1,0:T(8,128)(2,1)S(1)}, bf16[2,6,16,1024]{3,2,1,0:T(8,128)(2,1)S(1)}, u32[]{:S(2)}, u32[]{:S(2)}) collective-permute-start(bf16[2,6,16,1024]{3,2,1,0:T(8,128)(2,1)S(1)} %collective-permute-done.1.refs_1_), channel_id=1, source_target_pairs={{0,1},{1,0},{2,3},{3,2},{4,5},{5,4},{6,7},{7,6},{8,9},{9,8},{10,11... | collective-permute-start | bytes 1179656 | tf_op jit(solution)/shard_map/ppermute | solution.py:363
  33.5 6.7 %collective-permute-start.9 = (bf16[1,6,16,1024]{3,2,1,0:T(8,128)(2,1)S(1)}, bf16[1,6,16,1024]{3,2,1,0:T(8,128)(2,1)S(1)}, u32[]{:S(2)}, u32[]{:S(2)}) collective-permute-start(bf16[1,6,16,1024]{3,2,1,0:T(8,128)(2,1)S(1)} %collective-permute-done.4.refs_4_), channel_id=1, source_target_pairs={{0,1},{1,0},{2,3},{3,2},{4,5},{5,4},{6,7},{7,6},{8,9},{9,8},{10,11... | collective-permute-start | bytes 589832 | tf_op jit(solution)/shard_map/ppermute | solution.py:363
  36.2 4.9 %collective-permute-start.8 = (bf16[1,6,16,1024]{3,2,1,0:T(8,128)(2,1)S(1)}, bf16[1,6,16,1024]{3,2,1,0:T(8,128)(2,1)S(1)}, u32[]{:S(2)}, u32[]{:S(2)}) collective-permute-start(bf16[1,6,16,1024]{3,2,1,0:T(8,128)(2,1)S(1)} %collective-permute-done.3.refs_3_), channel_id=1, source_target_pairs={{0,1},{1,0},{2,3},{3,2},{4,5},{5,4},{6,7},{7,6},{8,9},{9,8},{10,11... | collective-permute-start | bytes 589832 | tf_op jit(solution)/shard_map/ppermute | solution.py:363
  43.1 6.3 %collective-permute-start.10 = (f32[128,256]{1,0:T(8,128)S(1)}, f32[128,256]{1,0:T(8,128)S(1)}, u32[]{:S(2)}, u32[]{:S(2)}) collective-permute-start(f32[128,256]{1,0:T(8,128)S(1)} %shard_map.38), channel_id=1, source_target_pairs={{0,128},{16,144},{32,160},{48,176},{64,192},{80,208},{96,224},{112... | collective-permute-start | bytes 393224 | tf_op jit(solution)/shard_map/ppermute | solution.py:380
  49.4 4.3 %collective-permute-start.11 = (f32[128,256]{1,0:T(8,128)S(1)}, f32[128,256]{1,0:T(8,128)S(1)}, u32[]{:S(2)}, u32[]{:S(2)}) collective-permute-start(f32[128,256]{1,0:T(8,128)S(1)} %add.227), channel_id=1, source_target_pairs={{0,16},{16,0},{32,48},{48,32},{64,80},{80,64},{96,112},{112,96},{1... | collective-permute-start | bytes 393224 | tf_op jit(solution)/shard_map/ppermute | solution.py:380
  53.7 7.2 %collective-permute-start.12 = (f32[128,256]{1,0:T(8,128)S(1)}, f32[128,256]{1,0:T(8,128)S(1)}, u32[]{:S(2)}, u32[]{:S(2)}) collective-permute-start(f32[128,256]{1,0:T(8,128)S(1)} %add.228), channel_id=1, source_target_pairs={{0,32},{16,48},{32,0},{48,16},{64,96},{80,112},{96,64},{112,80},{1... | collective-permute-start | bytes 393224 | tf_op jit(solution)/shard_map/ppermute | solution.py:380
  60.9 8.4 %collective-permute-start.13 = (f32[128,256]{1,0:T(8,128)S(1)}, f32[128,256]{1,0:T(8,128)S(1)}, u32[]{:S(2)}, u32[]{:S(2)}) collective-permute-start(f32[128,256]{1,0:T(8,128)S(1)} %add.229), channel_id=1, source_target_pairs={{0,64},{16,80},{32,96},{48,112},{64,0},{80,16},{96,32},{112,48},{1... | collective-permute-start | bytes 393224 | tf_op jit(solution)/shard_map/ppermute | solution.py:380
  69.4 3.5 %collective-permute-start.14 = (f32[1,4,16,256]{3,2,1,0:T(8,128)S(1)}, f32[1,4,16,256]{3,2,1,0:T(8,128)S(1)}, u32[]{:S(2)}, u32[]{:S(2)}) collective-permute-start(f32[1,4,16,256]{3,2,1,0:T(8,128)S(1)} %bitcast.24), channel_id=1, source_target_pairs={{0,8},{1,9},{2,10},{3,11},{4,12},{5,13},{6,14},{7,15},{8,0},{9,1},... | collective-permute-start | bytes 196616 | tf_op jit(solution)/shard_map/ppermute | solution.py:357
  72.9 7.8 %collective-permute-start.16 = (f32[2,4,16,256]{3,2,1,0:T(8,128)S(1)}, f32[2,4,16,256]{3,2,1,0:T(8,128)S(1)}, u32[]{:S(2)}, u32[]{:S(2)}) collective-permute-start(f32[2,4,16,256]{3,2,1,0:T(8,128)S(1)} %pad_maximum_fusion.1.refs_0_), channel_id=1, source_target_pairs={{0,6},{1,7},{2,0},{3,1},{4,2},{5,3},{6,4},{7,5},{8,14},{9,15},{10,... | collective-permute-start | bytes 393224 | tf_op jit(solution)/shard_map/ppermute | solution.py:359
  73.2 8.9 %collective-permute-start.15 = (f32[2,4,16,256]{3,2,1,0:T(8,128)S(1)}, f32[2,4,16,256]{3,2,1,0:T(8,128)S(1)}, u32[]{:S(2)}, u32[]{:S(2)}) collective-permute-start(f32[2,4,16,256]{3,2,1,0:T(8,128)S(1)} %pad_maximum_fusion.1.refs_0_), channel_id=1, source_target_pairs={{0,2},{1,3},{2,4},{3,5},{4,6},{5,7},{6,0},{7,1},{8,10},{9,11},{10,... | collective-permute-start | bytes 393224 | tf_op jit(solution)/shard_map/ppermute | solution.py:358
  74.4 16.3 %collective-permute-start.19 = (f32[2,4,16,256]{3,2,1,0:T(8,128)S(1)}, f32[2,4,16,256]{3,2,1,0:T(8,128)S(1)}, u32[]{:S(2)}, u32[]{:S(2)}) collective-permute-start(f32[2,4,16,256]{3,2,1,0:T(8,128)S(1)} %pad_maximum_fusion.1.refs_0_), channel_id=1, source_target_pairs={{0,1},{1,0},{2,3},{3,2},{4,5},{5,4},{6,7},{7,6},{8,9},{9,8},{10,11... | collective-permute-start | bytes 393224 | tf_op jit(solution)/shard_map/ppermute | solution.py:363
  80.6 5.1 %collective-permute-start.18 = (f32[1,4,16,256]{3,2,1,0:T(8,128)S(1)}, f32[1,4,16,256]{3,2,1,0:T(8,128)S(1)}, u32[]{:S(2)}, u32[]{:S(2)}) collective-permute-start(f32[1,4,16,256]{3,2,1,0:T(8,128)S(1)} %slice.42), channel_id=1, source_target_pairs={{0,6},{1,7},{2,0},{3,1},{4,2},{5,3},{6,4},{7,5},{8,14},{9,15},{10,... | collective-permute-start | bytes 196616 | tf_op jit(solution)/shard_map/ppermute | solution.py:361
  82.1 5.8 %collective-permute-start.17 = (f32[1,4,16,256]{3,2,1,0:T(8,128)S(1)}, f32[1,4,16,256]{3,2,1,0:T(8,128)S(1)}, u32[]{:S(2)}, u32[]{:S(2)}) collective-permute-start(f32[1,4,16,256]{3,2,1,0:T(8,128)S(1)} %slice.41), channel_id=1, source_target_pairs={{0,2},{1,3},{2,4},{3,5},{4,6},{5,7},{6,0},{7,1},{8,10},{9,11},{10,... | collective-permute-start | bytes 196616 | tf_op jit(solution)/shard_map/ppermute | solution.py:360
  82.3 8.5 %collective-permute-start.21 = (f32[2,4,16,256]{3,2,1,0:T(8,128)S(1)}, f32[2,4,16,256]{3,2,1,0:T(8,128)S(1)}, u32[]{:S(2)}, u32[]{:S(2)}) collective-permute-start(f32[2,4,16,256]{3,2,1,0:T(8,128)S(1)} %collective-permute-done.16.refs_2_), channel_id=1, source_target_pairs={{0,1},{1,0},{2,3},{3,2},{4,5},{5,4},{6,7},{7,6},{8,9},{9,8},{10,11... | collective-permute-start | bytes 393224 | tf_op jit(solution)/shard_map/ppermute | solution.py:363
  85.7 6.0 %collective-permute-start.20 = (f32[2,4,16,256]{3,2,1,0:T(8,128)S(1)}, f32[2,4,16,256]{3,2,1,0:T(8,128)S(1)}, u32[]{:S(2)}, u32[]{:S(2)}) collective-permute-start(f32[2,4,16,256]{3,2,1,0:T(8,128)S(1)} %collective-permute-done.15.refs_1_), channel_id=1, source_target_pairs={{0,1},{1,0},{2,3},{3,2},{4,5},{5,4},{6,7},{7,6},{8,9},{9,8},{10,11... | collective-permute-start | bytes 393224 | tf_op jit(solution)/shard_map/ppermute | solution.py:363
  85.7 5.1 %collective-permute-start.23 = (f32[1,4,16,256]{3,2,1,0:T(8,128)S(1)}, f32[1,4,16,256]{3,2,1,0:T(8,128)S(1)}, u32[]{:S(2)}, u32[]{:S(2)}) collective-permute-start(f32[1,4,16,256]{3,2,1,0:T(8,128)S(1)} %collective-permute-done.18.refs_4_), channel_id=1, source_target_pairs={{0,1},{1,0},{2,3},{3,2},{4,5},{5,4},{6,7},{7,6},{8,9},{9,8},{10,11... | collective-permute-start | bytes 196616 | tf_op jit(solution)/shard_map/ppermute | solution.py:363
  87.9 3.8 %collective-permute-start.22 = (f32[1,4,16,256]{3,2,1,0:T(8,128)S(1)}, f32[1,4,16,256]{3,2,1,0:T(8,128)S(1)}, u32[]{:S(2)}, u32[]{:S(2)}) collective-permute-start(f32[1,4,16,256]{3,2,1,0:T(8,128)S(1)} %collective-permute-done.17.refs_3_), channel_id=1, source_target_pairs={{0,1},{1,0},{2,3},{3,2},{4,5},{5,4},{6,7},{7,6},{8,9},{9,8},{10,11... | collective-permute-start | bytes 196616 | tf_op jit(solution)/shard_map/ppermute | solution.py:363
  135.0 3.4 %copy-start.1 = (bf16[4096,1024]{1,0:T(8,128)(2,1)S(1)}, bf16[4096,1024]{1,0:T(8,128)(2,1)}, u32[]{:S(2)}) copy-start(bf16[4096,1024]{1,0:T(8,128)(2,1)} %copy-done) | copy-start | bytes 25165828

commit v5 on v4

--- a/solution.py
+++ b/solution.py
@@ -6,7 +6,7 @@
 from jax.sharding import PartitionSpec as P
 
 LAGS = 4
-CHUNK = 2048
+CHUNK = 4096
 BACK_CHUNK = 4096
 FINE = 128
 f32 = jnp.float32
@@ -27,19 +27,24 @@
     return even * along - odd * cross, odd * along + even * cross
 
 
-def forward_kernel(early_ref, late_ref, live_ref, cc_ref, cs_ref, fc_ref, fs_ref, spec_ref, table_ref, acc):
+def fill_table(step, wave_refs, table_ref):
+    cc_ref, cs_ref, fc_ref, fs_ref = wave_refs
+    fine, band = fc_ref.shape
+    count = table_ref.shape[0] // fine
+    for r in range(count):
+        cc = cc_ref[pl.ds(step * count + r, 1), :]
+        cs = cs_ref[pl.ds(step * count + r, 1), :]
+        at = slice(r * fine, (r + 1) * fine)
+        table_ref[at, :band] = (cc * fc_ref[...] - cs * fs_ref[...]).astype(bf)
+        table_ref[at, band:] = (cs * fc_ref[...] + cc * fs_ref[...]).astype(bf)
+
+
+def forward_kernel(early_ref, late_ref, live_ref, cc_ref, cs_ref, fc_ref, fs_ref, spec_ref, acc, table_ref):
     step = pl.program_id(0)
     chunk, width = table_ref.shape
     band = width // 2
-    fine = fc_ref.shape[0]
     rows = spec_ref.shape[0]
-    for r in range(chunk // fine):
-        h = step * (chunk // fine) + r
-        cc = cc_ref[pl.ds(h, 1), :]
-        cs = cs_ref[pl.ds(h, 1), :]
-        at = slice(r * fine, (r + 1) * fine)
-        table_ref[at, :band] = (cc * fc_ref[...] - cs * fs_ref[...]).astype(bf)
-        table_ref[at, band:] = (cs * fc_ref[...] + cc * fs_ref[...]).astype(bf)
+    fill_table(step, (cc_ref, cs_ref, fc_ref, fs_ref), table_ref)
     both = jnp.concatenate(
         [early_ref[...].reshape(rows, chunk), late_ref[...].reshape(rows, chunk)], axis=0
     )
@@ -60,36 +65,29 @@
         spec_ref[:, band:] = ((acc[:rows, band:] + odd) * live_ref[...]).astype(bf)
 
 
-def forward(traces, live):
+def forward(traces, live, waves):
     shots, chans, samples = traces.shape
     band = samples // 16
     rows = shots * chans
     steps = samples // 2 // CHUNK
-    cc, cs = wave(jnp.arange(samples // 2 // FINE, dtype=jnp.int32) * FINE, samples, band)
-    fc, fs = wave(jnp.arange(FINE, dtype=jnp.int32), samples, band)
     return pl.pallas_call(
         forward_kernel,
         grid=(steps,),
-        out_shape=(
-            jax.ShapeDtypeStruct((rows, 2 * band), bf),
-            jax.ShapeDtypeStruct((samples // 2, 2 * band), bf),
-        ),
+        out_shape=jax.ShapeDtypeStruct((rows, 2 * band), bf),
         in_specs=[
             pl.BlockSpec((shots, chans, CHUNK), lambda i: (0, 0, i)),
             pl.BlockSpec((shots, chans, CHUNK), lambda i: (0, 0, i + steps)),
         ]
         + [VM] * 5,
-        out_specs=(
-            pl.BlockSpec((rows, 2 * band), lambda i: (0, 0)),
-            pl.BlockSpec((CHUNK, 2 * band), lambda i: (i, 0)),
-        ),
-        scratch_shapes=[pltpu.VMEM((2 * rows, 2 * band), f32)],
+        out_specs=pl.BlockSpec((rows, 2 * band), lambda i: (0, 0)),
+        scratch_shapes=[pltpu.VMEM((2 * rows, 2 * band), f32), pltpu.VMEM((CHUNK, 2 * band), bf)],
         compiler_params=pltpu.CompilerParams(vmem_limit_bytes=40 * 2**20),
-    )(traces, traces, live.reshape(rows, 1), cc, cs, fc, fs)
-
-
-def inverse_kernel(order_ref, filter_ref, own_ref, cos_ref, sin_ref, live_ref, table_ref, *refs):
-    *piece_refs, out_ref, error, full, later = refs
+    )(traces, traces, live.reshape(rows, 1), *waves)
+
+
+def inverse_kernel(order_ref, filter_ref, own_ref, cos_ref, sin_ref, live_ref, *refs):
+    wave_refs = refs[:4]
+    *piece_refs, out_ref, error, full, later, table_ref = refs[4:]
     half = pl.program_id(1)
     rows = own_ref.shape[0]
     shots, chans, chunk = out_ref.shape
@@ -120,6 +118,7 @@
 
     @pl.when(half == 0)
     def _():
+        fill_table(pl.program_id(0), wave_refs, table_ref)
         restored = lax.dot_general(
             error[...], table_ref[...], (((1,), (1,)), ((), ())), preferred_element_type=f32
         )
@@ -131,28 +130,26 @@
         out_ref[...] = later[...].reshape(out_ref.shape)
 
 
-def inverse(order, filter_bf, pieces, own_rows, cosine, sine, live, table):
+def inverse(order, filter_bf, pieces, own_rows, cosine, sine, live, waves, samples):
     shots, chans = live.shape
     rows, width = own_rows.shape
-    samples = 2 * table.shape[0]
-    steps = table.shape[0] // BACK_CHUNK
+    steps = samples // 2 // BACK_CHUNK
     channels = filter_bf.shape[2]
     return pl.pallas_call(
         inverse_kernel,
         grid=(steps, 2),
         out_shape=jax.ShapeDtypeStruct((shots, chans, samples), bf),
         in_specs=[pl.BlockSpec(memory_space=pltpu.SMEM)]
-        + [VM] * 5
-        + [pl.BlockSpec((BACK_CHUNK, width), lambda i, h: (i, 0))]
-        + [VM] * len(pieces),
+        + [VM] * (9 + len(pieces)),
         out_specs=pl.BlockSpec((shots, chans, BACK_CHUNK), lambda i, h: (0, 0, i + h * steps)),
         scratch_shapes=[
             pltpu.VMEM((2 * rows, width), bf),
             pltpu.VMEM((channels, width), bf),
             pltpu.VMEM((rows, BACK_CHUNK), bf),
+            pltpu.VMEM((BACK_CHUNK, width), bf),
         ],
         compiler_params=pltpu.CompilerParams(vmem_limit_bytes=40 * 2**20),
-    )(order, filter_bf, own_rows, cosine, sine, live.reshape(rows, 1), table, *pieces)
+    )(order, filter_bf, own_rows, cosine, sine, live.reshape(rows, 1), *waves, *pieces)
 
 
 def invert_128(groups, spare):
@@ -385,7 +382,9 @@
     shot_count, local_chan, samples = traces.shape
     band_size = samples // 16
     live = live_mask.astype(f32)
-    own_rows, table = forward(traces, live)
+    coarse = jnp.arange(samples // 2 // FINE, dtype=jnp.int32) * FINE
+    waves = wave(coarse, samples, band_size) + wave(jnp.arange(FINE, dtype=jnp.int32), samples, band_size)
+    own_rows = forward(traces, live, waves)
     own_spec = own_rows.reshape(shot_count, local_chan, 2 * band_size)
     order = lag_order()
     spectra = gather_lag(own_spec)
@@ -402,7 +401,7 @@
     summed = summed.reshape(2 * LAGS, local_chan, channels)
     correlation = gather_lag(summed[:LAGS])
     filter_bf = solve_filter(order, correlation, summed[LAGS:])
-    return inverse(order, filter_bf, spectra, own_rows, cosine[LAGS:], sine[LAGS:], live, table)
+    return inverse(order, filter_bf, spectra, own_rows, cosine[LAGS:], sine[LAGS:], live, waves, samples)
 
 
 def solution(mesh):

time: 144 us -> 138 us (0.958)
  local copies, waits for them, and re-layouts: 8.28 us -> 3.03 us
    unnamed x6 -> x10, local copies, waits for them, and re-layouts: 8.05 us -> 1.45 us
  transfers between devices with their start and end apart: 24 -> 24, of which waited for: 9 -> 10; matrix products, arithmetic and copies ran while one was open for 0% -> 2% of each run, Pallas kernels for 0% -> 0%
where the time goes in v5:
time: 138 us
  Pallas kernels  53.8 us (39%)
  starting transfers between devices  52.5 us (38%)
  waiting for transfers between devices  24 us (17%)
  other arithmetic  3.64 us (3%)
  local copies, waits for them, and re-layouts  3.03 us (2%)
    pallas_call x1, Pallas kernels, solve_filter(): pl.pallas_call(solve_kernel, out_shape=jax.ShapeDtypeStruct((LAGS, chans,...  43.3 us
    ppermute x10, starting transfers between devices, gather_lag(): return near + [lax.ppermute(piece, 'lag', over_core) for piece in near]  24.7 us
    ppermute x4, starting transfers between devices, sum_over_shot(): value = value + lax.ppermute(value, 'shot', pairs)  13.7 us
    ppermute x4, waiting for transfers between devices, sum_over_shot(): value = value + lax.ppermute(value, 'shot', pairs)  12.5 us
    pallas_call x1, Pallas kernels, inverse(): pl.pallas_call(inverse_kernel, grid=(steps, 2), out_shape=jax.ShapeDtypeS...  6.01 us
    ppermute x2, waiting for transfers between devices, gather_lag(): pair = jnp.concatenate([own, lax.ppermute(own, 'lag', over_x)], axis=0)  5.48 us
    ppermute x2, starting transfers between devices, gather_lag(): far_other = lax.ppermute(above[1:], 'lag', down)  4.51 us
    ppermute x2, starting transfers between devices, gather_lag(): above = lax.ppermute(pair, 'lag', down)  4.17 us
  transfers between devices with their start and end apart: 24, of which 10 were waited for; matrix products, arithmetic and copies ran while one was open for 2% of the time, Pallas kernels for 0%

profile of v5, /device:TPU:1, one launch (start us, length us, event | category | flops | bytes accessed | tf_op | source)
XLA Modules:
  0.0 137.8 jit_solution(12507545734458202845)
XLA Ops:
  0.8 1.0 fusion.6
  2.2 1.4 %copy-done = bf16[6,16,8192]{2,1,0:T(8,128)(2,1)S(1)} copy-done((bf16[6,16,8192]{2,1,0:T(8,128)(2,1)S(1)}, bf16[6,16,8192]{2,1,0:T(8,128)(2,1)}, u32[]{:S(2)}) %copy-start) | copy-done | bytes 1572888
  3.6 2.5 %shard_map.37.own_ref = bf16[96,1024]{1,0:T(8,128)(2,1)S(1)} custom-call(bf16[6,16,8192]{2,1,0:T(8,128)(2,1)S(1)} %copy-done, bf16[6,16,8192]{2,1,0:T(8,128)(2,1)S(1)} %copy-done, f32[96,1]{1,0:T(8,128)S(1)} %reshape.23.live_ref, f32[32,512]{1,0:T(8,128)S(1)} %get-tuple-element.11.cc_ref.refs_0_, f32[32,512]{1,0:T(8,128)S(1)} %get-tuple-element.10.cs_ref.refs_1_, ...), custom_call_target="tpu_custom_call" | custom-call | tf_op jit(solution)/shard_map/pallas_call | solution.py:73
  6.1 2.1 %collective-permute-start = (bf16[1,6,16,1024]{3,2,1,0:T(8,128)(2,1)S(1)}, bf16[1,6,16,1024]{3,2,1,0:T(8,128)(2,1)S(1)}, u32[]{:S(2)}, u32[]{:S(2)}) collective-permute-start(bf16[1,6,16,1024]{3,2,1,0:T(8,128)(2,1)S(1)} %bitcast.21), channel_id=1, source_target_pairs={{0,8},{1,9},{2,10},{3,11},{4,12},{5,13},{6,14},{7,15},{8,0},{9,1},... | collective-permute-start | bytes 589832 | tf_op jit(solution)/shard_map/ppermute | solution.py:354
  8.3 3.3 %collective-permute-done = bf16[1,6,16,1024]{3,2,1,0:T(8,128)(2,1)S(1)} collective-permute-done((bf16[1,6,16,1024]{3,2,1,0:T(8,128)(2,1)S(1)}, bf16[1,6,16,1024]{3,2,1,0:T(8,128)(2,1)S(1)}, u32[]{:S(2)}, u32[]{:S(2)}) %collective-permute-start) | collective-permute-done | bytes 196640 | tf_op jit(solution)/shard_map/ppermute | solution.py:354
  11.6 4.1 %collective-permute-start.2 = (bf16[2,6,16,1024]{3,2,1,0:T(8,128)(2,1)S(1)}, bf16[2,6,16,1024]{3,2,1,0:T(8,128)(2,1)S(1)}, u32[]{:S(2)}, u32[]{:S(2)}) collective-permute-start(bf16[2,6,16,1024]{3,2,1,0:T(8,128)(2,1)S(1)} %pad_maximum_fusion.refs_0_.refs_4_), channel_id=1, source_target_pairs={{0,6},{1,7},{2,0},{3,1},{4,2},{5,3},{6,4},{7,5},{8,14},{9,15},{10,... | collective-permute-start | bytes 1179656 | tf_op jit(solution)/shard_map/ppermute | solution.py:356
  16.9 1.8 %collective-permute-start.5 = (bf16[2,6,16,1024]{3,2,1,0:T(8,128)(2,1)S(1)}, bf16[2,6,16,1024]{3,2,1,0:T(8,128)(2,1)S(1)}, u32[]{:S(2)}, u32[]{:S(2)}) collective-permute-start(bf16[2,6,16,1024]{3,2,1,0:T(8,128)(2,1)S(1)} %pad_maximum_fusion.refs_0_.refs_4_), channel_id=1, source_target_pairs={{0,1},{1,0},{2,3},{3,2},{4,5},{5,4},{6,7},{7,6},{8,9},{9,8},{10,11... | collective-permute-start | bytes 1179656 | tf_op jit(solution)/shard_map/ppermute | solution.py:360
  18.7 3.8 %collective-permute-done.2.refs_2_.refs_6_ = bf16[2,6,16,1024]{3,2,1,0:T(8,128)(2,1)S(1)} collective-permute-done((bf16[2,6,16,1024]{3,2,1,0:T(8,128)(2,1)S(1)}, bf16[2,6,16,1024]{3,2,1,0:T(8,128)(2,1)S(1)}, u32[]{:S(2)}, u32[]{:S(2)}) %collective-permute-start.2) | collective-permute-done | bytes 393248 | tf_op jit(solution)/shard_map/ppermute | solution.py:356
  23.2 3.4 %collective-permute-start.4 = (bf16[1,6,16,1024]{3,2,1,0:T(8,128)(2,1)}, bf16[1,6,16,1024]{3,2,1,0:T(8,128)(2,1)S(1)}, u32[]{:S(2)}, u32[]{:S(2)}) collective-permute-start(bf16[1,6,16,1024]{3,2,1,0:T(8,128)(2,1)} %slice.38), channel_id=1, source_target_pairs={{0,6},{1,7},{2,0},{3,1},{4,2},{5,3},{6,4},{7,5},{8,14},{9,15},{10,... | collective-permute-start | bytes 589832 | tf_op jit(solution)/shard_map/ppermute | solution.py:358
  27.3 2.7 %collective-permute-start.7 = (bf16[2,6,16,1024]{3,2,1,0:T(8,128)(2,1)S(1)}, bf16[2,6,16,1024]{3,2,1,0:T(8,128)(2,1)S(1)}, u32[]{:S(2)}, u32[]{:S(2)}) collective-permute-start(bf16[2,6,16,1024]{3,2,1,0:T(8,128)(2,1)S(1)} %collective-permute-done.2.refs_2_.refs_6_), channel_id=1, source_target_pairs={{0,1},{1,0},{2,3},{3,2},{4,5},{5,4},{6,7},{7,6},{8,9},{9,8},{10,11... | collective-permute-start | bytes 1179656 | tf_op jit(solution)/shard_map/ppermute | solution.py:360
  30.9 2.0 %collective-permute-start.9 = (bf16[1,6,16,1024]{3,2,1,0:T(8,128)(2,1)S(1)}, bf16[1,6,16,1024]{3,2,1,0:T(8,128)(2,1)S(1)}, u32[]{:S(2)}, u32[]{:S(2)}) collective-permute-start(bf16[1,6,16,1024]{3,2,1,0:T(8,128)(2,1)S(1)} %collective-permute-done.4.refs_4_.refs_8_), channel_id=1, source_target_pairs={{0,1},{1,0},{2,3},{3,2},{4,5},{5,4},{6,7},{7,6},{8,9},{9,8},{10,11... | collective-permute-start | bytes 589832 | tf_op jit(solution)/shard_map/ppermute | solution.py:360
  33.3 3.9 %collective-permute-start.8 = (bf16[1,6,16,1024]{3,2,1,0:T(8,128)(2,1)S(1)}, bf16[1,6,16,1024]{3,2,1,0:T(8,128)(2,1)S(1)}, u32[]{:S(2)}, u32[]{:S(2)}) collective-permute-start(bf16[1,6,16,1024]{3,2,1,0:T(8,128)(2,1)S(1)} %collective-permute-done.3.refs_3_.refs_7_), channel_id=1, source_target_pairs={{0,1},{1,0},{2,3},{3,2},{4,5},{5,4},{6,7},{7,6},{8,9},{9,8},{10,11... | collective-permute-start | bytes 589832 | tf_op jit(solution)/shard_map/ppermute | solution.py:360
  37.4 0.9 collective-permute-done.8.refs_8_.refs_12_
  38.3 2.0 %shard_map.38 = f32[128,256]{1,0:T(8,128)S(1)} custom-call(s32[16]{0:T(128)S(1)} %stack.67.order_ref, bf16[96,1024]{1,0:T(8,128)(2,1)S(1)} %shard_map.37.own_ref, f32[8,512]{1,0:T(8,128)S(1)} %get-tuple-element.9.cos_ref, f32[8,512]{1,0:T(8,128)S(1)} %get-tuple-element.8.sin_ref, bf16[2,6,16,1024]{3,2,1,0:T(8,128)(2,1)S(1)} %pad_maximum_fusion.refs_0_.refs_4_, ...), custom_call_target="tpu_custom_call" | custom-call | tf_op jit(solution)/shard_map/pallas_call | solution.py:329
  40.3 3.0 %collective-permute-start.10 = (f32[128,256]{1,0:T(8,128)S(1)}, f32[128,256]{1,0:T(8,128)S(1)}, u32[]{:S(2)}, u32[]{:S(2)}) collective-permute-start(f32[128,256]{1,0:T(8,128)S(1)} %shard_map.38), channel_id=1, source_target_pairs={{0,128},{16,144},{32,160},{48,176},{64,192},{80,208},{96,224},{112... | collective-permute-start | bytes 393224 | tf_op jit(solution)/shard_map/ppermute | solution.py:377
  43.3 3.5 %collective-permute-done.10 = f32[128,256]{1,0:T(8,128)S(1)} collective-permute-done((f32[128,256]{1,0:T(8,128)S(1)}, f32[128,256]{1,0:T(8,128)S(1)}, u32[]{:S(2)}, u32[]{:S(2)}) %collective-permute-start.10) | collective-permute-done | bytes 131104 | tf_op jit(solution)/shard_map/ppermute | solution.py:377
  46.8 1.7 %collective-permute-start.11 = (f32[128,256]{1,0:T(8,128)S(1)}, f32[128,256]{1,0:T(8,128)S(1)}, u32[]{:S(2)}, u32[]{:S(2)}) collective-permute-start(f32[128,256]{1,0:T(8,128)S(1)} %add.243), channel_id=1, source_target_pairs={{0,16},{16,0},{32,48},{48,32},{64,80},{80,64},{96,112},{112,96},{1... | collective-permute-start | bytes 393224 | tf_op jit(solution)/shard_map/ppermute | solution.py:377
  48.5 2.4 %collective-permute-done.11 = f32[128,256]{1,0:T(8,128)S(1)} collective-permute-done((f32[128,256]{1,0:T(8,128)S(1)}, f32[128,256]{1,0:T(8,128)S(1)}, u32[]{:S(2)}, u32[]{:S(2)}) %collective-permute-start.11) | collective-permute-done | bytes 131104 | tf_op jit(solution)/shard_map/ppermute | solution.py:377
  50.9 3.1 %collective-permute-start.12 = (f32[128,256]{1,0:T(8,128)S(1)}, f32[128,256]{1,0:T(8,128)S(1)}, u32[]{:S(2)}, u32[]{:S(2)}) collective-permute-start(f32[128,256]{1,0:T(8,128)S(1)} %add.244), channel_id=1, source_target_pairs={{0,32},{16,48},{32,0},{48,16},{64,96},{80,112},{96,64},{112,80},{1... | collective-permute-start | bytes 393224 | tf_op jit(solution)/shard_map/ppermute | solution.py:377
  54.0 4.1 %collective-permute-done.12 = f32[128,256]{1,0:T(8,128)S(1)} collective-permute-done((f32[128,256]{1,0:T(8,128)S(1)}, f32[128,256]{1,0:T(8,128)S(1)}, u32[]{:S(2)}, u32[]{:S(2)}) %collective-permute-start.12) | collective-permute-done | bytes 131104 | tf_op jit(solution)/shard_map/ppermute | solution.py:377
  58.1 5.8 %collective-permute-start.13 = (f32[128,256]{1,0:T(8,128)S(1)}, f32[128,256]{1,0:T(8,128)S(1)}, u32[]{:S(2)}, u32[]{:S(2)}) collective-permute-start(f32[128,256]{1,0:T(8,128)S(1)} %add.245), channel_id=1, source_target_pairs={{0,64},{16,80},{32,96},{48,112},{64,0},{80,16},{96,32},{112,48},{1... | collective-permute-start | bytes 393224 | tf_op jit(solution)/shard_map/ppermute | solution.py:377
  63.9 2.6 %collective-permute-done.13 = f32[128,256]{1,0:T(8,128)S(1)} collective-permute-done((f32[128,256]{1,0:T(8,128)S(1)}, f32[128,256]{1,0:T(8,128)S(1)}, u32[]{:S(2)}, u32[]{:S(2)}) %collective-permute-start.13) | collective-permute-done | bytes 131104 | tf_op jit(solution)/shard_map/ppermute | solution.py:377
  66.5 1.3 collective-permute-start.14
  67.8 2.2 %collective-permute-done.14 = f32[1,4,16,256]{3,2,1,0:T(8,128)S(1)} collective-permute-done((f32[1,4,16,256]{3,2,1,0:T(8,128)S(1)}, f32[1,4,16,256]{3,2,1,0:T(8,128)S(1)}, u32[]{:S(2)}, u32[]{:S(2)}) %collective-permute-start.14) | collective-permute-done | bytes 65568 | tf_op jit(solution)/shard_map/ppermute | solution.py:354
  70.1 1.5 %collective-permute-start.15 = (f32[2,4,16,256]{3,2,1,0:T(8,128)S(1)}, f32[2,4,16,256]{3,2,1,0:T(8,128)S(1)}, u32[]{:S(2)}, u32[]{:S(2)}) collective-permute-start(f32[2,4,16,256]{3,2,1,0:T(8,128)S(1)} %pad_maximum_fusion.1.refs_0_), channel_id=1, source_target_pairs={{0,2},{1,3},{2,4},{3,5},{4,6},{5,7},{6,0},{7,1},{8,10},{9,11},{10,... | collective-permute-start | bytes 393224 | tf_op jit(solution)/shard_map/ppermute | solution.py:355
  71.6 6.2 %collective-permute-start.19 = (f32[2,4,16,256]{3,2,1,0:T(8,128)S(1)}, f32[2,4,16,256]{3,2,1,0:T(8,128)S(1)}, u32[]{:S(2)}, u32[]{:S(2)}) collective-permute-start(f32[2,4,16,256]{3,2,1,0:T(8,128)S(1)} %pad_maximum_fusion.1.refs_0_), channel_id=1, source_target_pairs={{0,1},{1,0},{2,3},{3,2},{4,5},{5,4},{6,7},{7,6},{8,9},{9,8},{10,11... | collective-permute-start | bytes 393224 | tf_op jit(solution)/shard_map/ppermute | solution.py:360
  77.8 1.1 collective-permute-start.18
  79.4 3.4 %collective-permute-start.21 = (f32[2,4,16,256]{3,2,1,0:T(8,128)S(1)}, f32[2,4,16,256]{3,2,1,0:T(8,128)S(1)}, u32[]{:S(2)}, u32[]{:S(2)}) collective-permute-start(f32[2,4,16,256]{3,2,1,0:T(8,128)S(1)} %collective-permute-done.16.refs_2_), channel_id=1, source_target_pairs={{0,1},{1,0},{2,3},{3,2},{4,5},{5,4},{6,7},{7,6},{8,9},{9,8},{10,11... | collective-permute-start | bytes 393224 | tf_op jit(solution)/shard_map/ppermute | solution.py:360
  82.9 2.1 %collective-permute-start.23 = (f32[1,4,16,256]{3,2,1,0:T(8,128)S(1)}, f32[1,4,16,256]{3,2,1,0:T(8,128)S(1)}, u32[]{:S(2)}, u32[]{:S(2)}) collective-permute-start(f32[1,4,16,256]{3,2,1,0:T(8,128)S(1)} %collective-permute-done.18.refs_4_), channel_id=1, source_target_pairs={{0,1},{1,0},{2,3},{3,2},{4,5},{5,4},{6,7},{7,6},{8,9},{9,8},{10,11... | collective-permute-start | bytes 196616 | tf_op jit(solution)/shard_map/ppermute | solution.py:360
  85.0 2.5 %collective-permute-start.22 = (f32[1,4,16,256]{3,2,1,0:T(8,128)S(1)}, f32[1,4,16,256]{3,2,1,0:T(8,128)S(1)}, u32[]{:S(2)}, u32[]{:S(2)}) collective-permute-start(f32[1,4,16,256]{3,2,1,0:T(8,128)S(1)} %collective-permute-done.17.refs_3_), channel_id=1, source_target_pairs={{0,1},{1,0},{2,3},{3,2},{4,5},{5,4},{6,7},{7,6},{8,9},{9,8},{10,11... | collective-permute-start | bytes 196616 | tf_op jit(solution)/shard_map/ppermute | solution.py:360
  88.5 43.3 %shard_map.39.filter_ref = bf16[4,16,256]{2,1,0:T(8,128)(2,1)S(1)} custom-call(s32[16]{0:T(128)S(1)} %stack.67.order_ref, f32[4,16,256]{2,1,0:T(8,128)S(1)} %bitcast.23, f32[2,4,16,256]{3,2,1,0:T(8,128)S(1)} %pad_maximum_fusion.1.refs_0_, f32[2,4,16,256]{3,2,1,0:T(8,128)S(1)} %collective-permute-done.15.refs_1_, ...), custom_call_target="tpu_custom_call" | custom-call | tf_op jit(solution)/shard_map/pallas_call | solution.py:276
  131.8 6.0 %shard_map.40 = bf16[6,16,8192]{2,1,0:T(8,128)(2,1)} custom-call(s32[16]{0:T(128)S(1)} %stack.67.order_ref, bf16[4,16,256]{2,1,0:T(8,128)(2,1)S(1)} %shard_map.39.filter_ref, bf16[96,1024]{1,0:T(8,128)(2,1)S(1)} %shard_map.37.own_ref, f32[4,512]{1,0:T(4,128)S(1)} %slice.43.cos_ref, f32[4,512]{1,0:T(4,128)S(1)} %slice.44.sin_ref, f32[96,1]{1,0:T(8,128)S(1)} %copy-done.4, ...), custom_call_target="tpu_custom_call" | custom-call | tf_op jit(solution)/shard_map/pallas_call | solution.py:138
  (54 shorter events, 6.1 us)
Async XLA Ops:
  0.8 5.3 %copy-start.3 = (f32[96,1]{1,0:T(8,128)}, f32[96,1]{1,0:T(8,128)S(1)}, u32[]{:S(2)}) copy-start(f32[96,1]{1,0:T(8,128)S(1)} %reshape.23.live_ref) | copy-start | bytes 1156
  2.2 4.0 %copy-start.1 = (f32[32,512]{1,0:T(8,128)}, f32[32,512]{1,0:T(8,128)S(1)}, u32[]{:S(2)}) copy-start(f32[32,512]{1,0:T(8,128)S(1)} %get-tuple-element.11.cc_ref.refs_0_) | copy-start | bytes 196612
  2.2 1.4 %copy-start = (bf16[6,16,8192]{2,1,0:T(8,128)(2,1)S(1)}, bf16[6,16,8192]{2,1,0:T(8,128)(2,1)}, u32[]{:S(2)}) copy-start(bf16[6,16,8192]{2,1,0:T(8,128)(2,1)} %late_ref.1) | copy-start | bytes 4718596
  6.1 5.4 %collective-permute-start = (bf16[1,6,16,1024]{3,2,1,0:T(8,128)(2,1)S(1)}, bf16[1,6,16,1024]{3,2,1,0:T(8,128)(2,1)S(1)}, u32[]{:S(2)}, u32[]{:S(2)}) collective-permute-start(bf16[1,6,16,1024]{3,2,1,0:T(8,128)(2,1)S(1)} %bitcast.21), channel_id=1, source_target_pairs={{0,8},{1,9},{2,10},{3,11},{4,12},{5,13},{6,14},{7,15},{8,0},{9,1},... | collective-permute-start | bytes 589832 | tf_op jit(solution)/shard_map/ppermute | solution.py:354
  11.6 10.9 %collective-permute-start.2 = (bf16[2,6,16,1024]{3,2,1,0:T(8,128)(2,1)S(1)}, bf16[2,6,16,1024]{3,2,1,0:T(8,128)(2,1)S(1)}, u32[]{:S(2)}, u32[]{:S(2)}) collective-permute-start(bf16[2,6,16,1024]{3,2,1,0:T(8,128)(2,1)S(1)} %pad_maximum_fusion.refs_0_.refs_4_), channel_id=1, source_target_pairs={{0,6},{1,7},{2,0},{3,1},{4,2},{5,3},{6,4},{7,5},{8,14},{9,15},{10,... | collective-permute-start | bytes 1179656 | tf_op jit(solution)/shard_map/ppermute | solution.py:356
  15.7 11.0 %collective-permute-start.1 = (bf16[2,6,16,1024]{3,2,1,0:T(8,128)(2,1)S(1)}, bf16[2,6,16,1024]{3,2,1,0:T(8,128)(2,1)S(1)}, u32[]{:S(2)}, u32[]{:S(2)}) collective-permute-start(bf16[2,6,16,1024]{3,2,1,0:T(8,128)(2,1)S(1)} %pad_maximum_fusion.refs_0_.refs_4_), channel_id=1, source_target_pairs={{0,2},{1,3},{2,4},{3,5},{4,6},{5,7},{6,0},{7,1},{8,10},{9,11},{10,... | collective-permute-start | bytes 1179656 | tf_op jit(solution)/shard_map/ppermute | solution.py:355
  16.9 20.4 %collective-permute-start.5 = (bf16[2,6,16,1024]{3,2,1,0:T(8,128)(2,1)S(1)}, bf16[2,6,16,1024]{3,2,1,0:T(8,128)(2,1)S(1)}, u32[]{:S(2)}, u32[]{:S(2)}) collective-permute-start(bf16[2,6,16,1024]{3,2,1,0:T(8,128)(2,1)S(1)} %pad_maximum_fusion.refs_0_.refs_4_), channel_id=1, source_target_pairs={{0,1},{1,0},{2,3},{3,2},{4,5},{5,4},{6,7},{7,6},{8,9},{9,8},{10,11... | collective-permute-start | bytes 1179656 | tf_op jit(solution)/shard_map/ppermute | solution.py:360
  23.2 7.7 %collective-permute-start.4 = (bf16[1,6,16,1024]{3,2,1,0:T(8,128)(2,1)}, bf16[1,6,16,1024]{3,2,1,0:T(8,128)(2,1)S(1)}, u32[]{:S(2)}, u32[]{:S(2)}) collective-permute-start(bf16[1,6,16,1024]{3,2,1,0:T(8,128)(2,1)} %slice.38), channel_id=1, source_target_pairs={{0,6},{1,7},{2,0},{3,1},{4,2},{5,3},{6,4},{7,5},{8,14},{9,15},{10,... | collective-permute-start | bytes 589832 | tf_op jit(solution)/shard_map/ppermute | solution.py:358
  27.3 5.9 %collective-permute-start.3 = (bf16[1,6,16,1024]{3,2,1,0:T(8,128)(2,1)}, bf16[1,6,16,1024]{3,2,1,0:T(8,128)(2,1)S(1)}, u32[]{:S(2)}, u32[]{:S(2)}) collective-permute-start(bf16[1,6,16,1024]{3,2,1,0:T(8,128)(2,1)} %slice.37), channel_id=1, source_target_pairs={{0,2},{1,3},{2,4},{3,5},{4,6},{5,7},{6,0},{7,1},{8,10},{9,11},{10,... | collective-permute-start | bytes 589832 | tf_op jit(solution)/shard_map/ppermute | solution.py:357
  27.3 10.0 %collective-permute-start.7 = (bf16[2,6,16,1024]{3,2,1,0:T(8,128)(2,1)S(1)}, bf16[2,6,16,1024]{3,2,1,0:T(8,128)(2,1)S(1)}, u32[]{:S(2)}, u32[]{:S(2)}) collective-permute-start(bf16[2,6,16,1024]{3,2,1,0:T(8,128)(2,1)S(1)} %collective-permute-done.2.refs_2_.refs_6_), channel_id=1, source_target_pairs={{0,1},{1,0},{2,3},{3,2},{4,5},{5,4},{6,7},{7,6},{8,9},{9,8},{10,11... | collective-permute-start | bytes 1179656 | tf_op jit(solution)/shard_map/ppermute | solution.py:360
  30.1 8.2 %collective-permute-start.6 = (bf16[2,6,16,1024]{3,2,1,0:T(8,128)(2,1)S(1)}, bf16[2,6,16,1024]{3,2,1,0:T(8,128)(2,1)S(1)}, u32[]{:S(2)}, u32[]{:S(2)}) collective-permute-start(bf16[2,6,16,1024]{3,2,1,0:T(8,128)(2,1)S(1)} %collective-permute-done.1.refs_1_.refs_5_), channel_id=1, source_target_pairs={{0,1},{1,0},{2,3},{3,2},{4,5},{5,4},{6,7},{7,6},{8,9},{9,8},{10,11... | collective-permute-start | bytes 1179656 | tf_op jit(solution)/shard_map/ppermute | solution.py:360
  30.9 6.4 %collective-permute-start.9 = (bf16[1,6,16,1024]{3,2,1,0:T(8,128)(2,1)S(1)}, bf16[1,6,16,1024]{3,2,1,0:T(8,128)(2,1)S(1)}, u32[]{:S(2)}, u32[]{:S(2)}) collective-permute-start(bf16[1,6,16,1024]{3,2,1,0:T(8,128)(2,1)S(1)} %collective-permute-done.4.refs_4_.refs_8_), channel_id=1, source_target_pairs={{0,1},{1,0},{2,3},{3,2},{4,5},{5,4},{6,7},{7,6},{8,9},{9,8},{10,11... | collective-permute-start | bytes 589832 | tf_op jit(solution)/shard_map/ppermute | solution.py:360
  33.3 5.0 %collective-permute-start.8 = (bf16[1,6,16,1024]{3,2,1,0:T(8,128)(2,1)S(1)}, bf16[1,6,16,1024]{3,2,1,0:T(8,128)(2,1)S(1)}, u32[]{:S(2)}, u32[]{:S(2)}) collective-permute-start(bf16[1,6,16,1024]{3,2,1,0:T(8,128)(2,1)S(1)} %collective-permute-done.3.refs_3_.refs_7_), channel_id=1, source_target_pairs={{0,1},{1,0},{2,3},{3,2},{4,5},{5,4},{6,7},{7,6},{8,9},{9,8},{10,11... | collective-permute-start | bytes 589832 | tf_op jit(solution)/shard_map/ppermute | solution.py:360
  40.3 6.5 %collective-permute-start.10 = (f32[128,256]{1,0:T(8,128)S(1)}, f32[128,256]{1,0:T(8,128)S(1)}, u32[]{:S(2)}, u32[]{:S(2)}) collective-permute-start(f32[128,256]{1,0:T(8,128)S(1)} %shard_map.38), channel_id=1, source_target_pairs={{0,128},{16,144},{32,160},{48,176},{64,192},{80,208},{96,224},{112... | collective-permute-start | bytes 393224 | tf_op jit(solution)/shard_map/ppermute | solution.py:377
  46.8 85.0 %copy-start.2 = (f32[32,512]{1,0:T(8,128)S(1)}, f32[32,512]{1,0:T(8,128)}, u32[]{:S(2)}) copy-start(f32[32,512]{1,0:T(8,128)} %copy-done.1) | copy-start | bytes 196612
  46.8 85.0 %copy-start.4 = (f32[96,1]{1,0:T(8,128)S(1)}, f32[96,1]{1,0:T(8,128)}, u32[]{:S(2)}) copy-start(f32[96,1]{1,0:T(8,128)} %copy-done.3) | copy-start | bytes 1156
  46.8 4.1 %collective-permute-start.11 = (f32[128,256]{1,0:T(8,128)S(1)}, f32[128,256]{1,0:T(8,128)S(1)}, u32[]{:S(2)}, u32[]{:S(2)}) collective-permute-start(f32[128,256]{1,0:T(8,128)S(1)} %add.243), channel_id=1, source_target_pairs={{0,16},{16,0},{32,48},{48,32},{64,80},{80,64},{96,112},{112,96},{1... | collective-permute-start | bytes 393224 | tf_op jit(solution)/shard_map/ppermute | solution.py:377
  50.9 7.2 %collective-permute-start.12 = (f32[128,256]{1,0:T(8,128)S(1)}, f32[128,256]{1,0:T(8,128)S(1)}, u32[]{:S(2)}, u32[]{:S(2)}) collective-permute-start(f32[128,256]{1,0:T(8,128)S(1)} %add.244), channel_id=1, source_target_pairs={{0,32},{16,48},{32,0},{48,16},{64,96},{80,112},{96,64},{112,80},{1... | collective-permute-start | bytes 393224 | tf_op jit(solution)/shard_map/ppermute | solution.py:377
  58.1 8.4 %collective-permute-start.13 = (f32[128,256]{1,0:T(8,128)S(1)}, f32[128,256]{1,0:T(8,128)S(1)}, u32[]{:S(2)}, u32[]{:S(2)}) collective-permute-start(f32[128,256]{1,0:T(8,128)S(1)} %add.245), channel_id=1, source_target_pairs={{0,64},{16,80},{32,96},{48,112},{64,0},{80,16},{96,32},{112,48},{1... | collective-permute-start | bytes 393224 | tf_op jit(solution)/shard_map/ppermute | solution.py:377
  66.5 3.5 %collective-permute-start.14 = (f32[1,4,16,256]{3,2,1,0:T(8,128)S(1)}, f32[1,4,16,256]{3,2,1,0:T(8,128)S(1)}, u32[]{:S(2)}, u32[]{:S(2)}) collective-permute-start(f32[1,4,16,256]{3,2,1,0:T(8,128)S(1)} %bitcast.24), channel_id=1, source_target_pairs={{0,8},{1,9},{2,10},{3,11},{4,12},{5,13},{6,14},{7,15},{8,0},{9,1},... | collective-permute-start | bytes 196616 | tf_op jit(solution)/shard_map/ppermute | solution.py:354
  70.1 7.7 %collective-permute-start.16 = (f32[2,4,16,256]{3,2,1,0:T(8,128)S(1)}, f32[2,4,16,256]{3,2,1,0:T(8,128)S(1)}, u32[]{:S(2)}, u32[]{:S(2)}) collective-permute-start(f32[2,4,16,256]{3,2,1,0:T(8,128)S(1)} %pad_maximum_fusion.1.refs_0_), channel_id=1, source_target_pairs={{0,6},{1,7},{2,0},{3,1},{4,2},{5,3},{6,4},{7,5},{8,14},{9,15},{10,... | collective-permute-start | bytes 393224 | tf_op jit(solution)/shard_map/ppermute | solution.py:356
  70.1 8.8 %collective-permute-start.15 = (f32[2,4,16,256]{3,2,1,0:T(8,128)S(1)}, f32[2,4,16,256]{3,2,1,0:T(8,128)S(1)}, u32[]{:S(2)}, u32[]{:S(2)}) collective-permute-start(f32[2,4,16,256]{3,2,1,0:T(8,128)S(1)} %pad_maximum_fusion.1.refs_0_), channel_id=1, source_target_pairs={{0,2},{1,3},{2,4},{3,5},{4,6},{5,7},{6,0},{7,1},{8,10},{9,11},{10,... | collective-permute-start | bytes 393224 | tf_op jit(solution)/shard_map/ppermute | solution.py:355
  71.6 16.0 %collective-permute-start.19 = (f32[2,4,16,256]{3,2,1,0:T(8,128)S(1)}, f32[2,4,16,256]{3,2,1,0:T(8,128)S(1)}, u32[]{:S(2)}, u32[]{:S(2)}) collective-permute-start(f32[2,4,16,256]{3,2,1,0:T(8,128)S(1)} %pad_maximum_fusion.1.refs_0_), channel_id=1, source_target_pairs={{0,1},{1,0},{2,3},{3,2},{4,5},{5,4},{6,7},{7,6},{8,9},{9,8},{10,11... | collective-permute-start | bytes 393224 | tf_op jit(solution)/shard_map/ppermute | solution.py:360
  77.8 5.1 %collective-permute-start.18 = (f32[1,4,16,256]{3,2,1,0:T(8,128)S(1)}, f32[1,4,16,256]{3,2,1,0:T(8,128)S(1)}, u32[]{:S(2)}, u32[]{:S(2)}) collective-permute-start(f32[1,4,16,256]{3,2,1,0:T(8,128)S(1)} %slice.42), channel_id=1, source_target_pairs={{0,6},{1,7},{2,0},{3,1},{4,2},{5,3},{6,4},{7,5},{8,14},{9,15},{10,... | collective-permute-start | bytes 196616 | tf_op jit(solution)/shard_map/ppermute | solution.py:358
  78.9 6.1 %collective-permute-start.17 = (f32[1,4,16,256]{3,2,1,0:T(8,128)S(1)}, f32[1,4,16,256]{3,2,1,0:T(8,128)S(1)}, u32[]{:S(2)}, u32[]{:S(2)}) collective-permute-start(f32[1,4,16,256]{3,2,1,0:T(8,128)S(1)} %slice.41), channel_id=1, source_target_pairs={{0,2},{1,3},{2,4},{3,5},{4,6},{5,7},{6,0},{7,1},{8,10},{9,11},{10,... | collective-permute-start | bytes 196616 | tf_op jit(solution)/shard_map/ppermute | solution.py:357
  79.4 8.1 %collective-permute-start.21 = (f32[2,4,16,256]{3,2,1,0:T(8,128)S(1)}, f32[2,4,16,256]{3,2,1,0:T(8,128)S(1)}, u32[]{:S(2)}, u32[]{:S(2)}) collective-permute-start(f32[2,4,16,256]{3,2,1,0:T(8,128)S(1)} %collective-permute-done.16.refs_2_), channel_id=1, source_target_pairs={{0,1},{1,0},{2,3},{3,2},{4,5},{5,4},{6,7},{7,6},{8,9},{9,8},{10,11... | collective-permute-start | bytes 393224 | tf_op jit(solution)/shard_map/ppermute | solution.py:360
  82.9 5.6 %collective-permute-start.20 = (f32[2,4,16,256]{3,2,1,0:T(8,128)S(1)}, f32[2,4,16,256]{3,2,1,0:T(8,128)S(1)}, u32[]{:S(2)}, u32[]{:S(2)}) collective-permute-start(f32[2,4,16,256]{3,2,1,0:T(8,128)S(1)} %collective-permute-done.15.refs_1_), channel_id=1, source_target_pairs={{0,1},{1,0},{2,3},{3,2},{4,5},{5,4},{6,7},{7,6},{8,9},{9,8},{10,11... | collective-permute-start | bytes 393224 | tf_op jit(solution)/shard_map/ppermute | solution.py:360
  82.9 4.7 %collective-permute-start.23 = (f32[1,4,16,256]{3,2,1,0:T(8,128)S(1)}, f32[1,4,16,256]{3,2,1,0:T(8,128)S(1)}, u32[]{:S(2)}, u32[]{:S(2)}) collective-permute-start(f32[1,4,16,256]{3,2,1,0:T(8,128)S(1)} %collective-permute-done.18.refs_4_), channel_id=1, source_target_pairs={{0,1},{1,0},{2,3},{3,2},{4,5},{5,4},{6,7},{7,6},{8,9},{9,8},{10,11... | collective-permute-start | bytes 196616 | tf_op jit(solution)/shard_map/ppermute | solution.py:360
  85.0 3.4 %collective-permute-start.22 = (f32[1,4,16,256]{3,2,1,0:T(8,128)S(1)}, f32[1,4,16,256]{3,2,1,0:T(8,128)S(1)}, u32[]{:S(2)}, u32[]{:S(2)}) collective-permute-start(f32[1,4,16,256]{3,2,1,0:T(8,128)S(1)} %collective-permute-done.17.refs_3_), channel_id=1, source_target_pairs={{0,1},{1,0},{2,3},{3,2},{4,5},{5,4},{6,7},{7,6},{8,9},{9,8},{10,11... | collective-permute-start | bytes 196616 | tf_op jit(solution)/shard_map/ppermute | solution.py:360

commit v6 on v5

--- a/solution.py
+++ b/solution.py
@@ -372,10 +372,18 @@
 
 
 def sum_over_shot(value):
-    for bit in (8, 1, 2, 4):
-        pairs = [(i, i ^ bit) for i in range(16)]
-        value = value + lax.ppermute(value, "shot", pairs)
-    return value
+    half = value.shape[0] // 2
+    odd = lax.axis_index("shot") % 2 == 1
+
+    def other(part, bit):
+        return lax.ppermute(part, "shot", [(i, i ^ bit) for i in range(16)])
+
+    first, second = value[:half], value[half:]
+    held = jnp.where(odd, second, first) + other(jnp.where(odd, first, second), 1)
+    for bit in (2, 4, 8):
+        held = held + other(held, bit)
+    back = other(held, 1)
+    return jnp.where(odd, back, held), jnp.where(odd, held, back)
 
 
 def shards(traces, live_mask, gap_samples):
@@ -397,10 +405,10 @@
     channels = partial_value.shape[1]
     total_shots = shot_count * lax.axis_size("shot")
     scale = (1.0 / samples) * (1.0 / (samples * total_shots))
-    summed = sum_over_shot(partial_value) * scale
-    summed = summed.reshape(2 * LAGS, local_chan, channels)
-    correlation = gather_lag(summed[:LAGS])
-    filter_bf = solve_filter(order, correlation, summed[LAGS:])
+    shape = (LAGS, local_chan, channels)
+    system, targets = sum_over_shot(partial_value)
+    correlation = gather_lag((system * scale).reshape(shape))
+    filter_bf = solve_filter(order, correlation, (targets * scale).reshape(shape))
     return inverse(order, filter_bf, spectra, own_rows, cosine[LAGS:], sine[LAGS:], live, waves, samples)
 
 

time: 138 us -> 138 us (level)
  waiting for transfers between devices: 24 us -> 21.8 us
  starting transfers between devices: 52.5 us -> 54.6 us
    ppermute x4 -> x5, waiting for transfers between devices: 12.5 us -> 10.3 us  [other(): return lax.ppermute(part, 'shot', [(i, i ^ bit) for i in range(16)])]
    ppermute x4 -> x5, starting transfers between devices: 13.7 us -> 14.8 us  [other(): return lax.ppermute(part, 'shot', [(i, i ^ bit) for i in range(16)])]
  transfers between devices with their start and end apart: 24 -> 25, of which waited for: 10 -> 11; matrix products, arithmetic and copies ran while one was open for 2% -> 2% of each run, Pallas kernels for 0% -> 0%
where the time goes in v6:
time: 138 us
  starting transfers between devices  54.6 us (40%)
  Pallas kernels  53.8 us (39%)
  waiting for transfers between devices  21.8 us (16%)
  other arithmetic  3.51 us (3%)
  local copies, waits for them, and re-layouts  3.02 us (2%)
    pallas_call x1, Pallas kernels, solve_filter(): pl.pallas_call(solve_kernel, out_shape=jax.ShapeDtypeStruct((LAGS, chans,...  43.3 us
    ppermute x10, starting transfers between devices, gather_lag(): return near + [lax.ppermute(piece, 'lag', over_core) for piece in near]  25.9 us
    ppermute x5, starting transfers between devices, other(): return lax.ppermute(part, 'shot', [(i, i ^ bit) for i in range(16)])  14.8 us
    ppermute x5, waiting for transfers between devices, other(): return lax.ppermute(part, 'shot', [(i, i ^ bit) for i in range(16)])  10.3 us
    pallas_call x1, Pallas kernels, inverse(): pl.pallas_call(inverse_kernel, grid=(steps, 2), out_shape=jax.ShapeDtypeS...  6.01 us
    ppermute x2, waiting for transfers between devices, gather_lag(): pair = jnp.concatenate([own, lax.ppermute(own, 'lag', over_x)], axis=0)  5.47 us
    ppermute x2, starting transfers between devices, gather_lag(): far_other = lax.ppermute(above[1:], 'lag', down)  4.51 us
    ppermute x2, starting transfers between devices, gather_lag(): above = lax.ppermute(pair, 'lag', down)  4.17 us
  transfers between devices with their start and end apart: 25, of which 11 were waited for; matrix products, arithmetic and copies ran while one was open for 2% of the time, Pallas kernels for 0%

profile of v6, /device:TPU:1, one launch (start us, length us, event | category | flops | bytes accessed | tf_op | source)
XLA Modules:
  0.0 137.5 jit_solution(7769471240603087855)
XLA Ops:
  0.8 1.0 fusion.6
  2.2 1.4 %copy-done = bf16[6,16,8192]{2,1,0:T(8,128)(2,1)S(1)} copy-done((bf16[6,16,8192]{2,1,0:T(8,128)(2,1)S(1)}, bf16[6,16,8192]{2,1,0:T(8,128)(2,1)}, u32[]{:S(2)}) %copy-start) | copy-done | bytes 1572888
  3.6 2.5 %shard_map.37.own_ref = bf16[96,1024]{1,0:T(8,128)(2,1)S(1)} custom-call(bf16[6,16,8192]{2,1,0:T(8,128)(2,1)S(1)} %copy-done, bf16[6,16,8192]{2,1,0:T(8,128)(2,1)S(1)} %copy-done, f32[96,1]{1,0:T(8,128)S(1)} %reshape.23.live_ref, f32[32,512]{1,0:T(8,128)S(1)} %get-tuple-element.11.cc_ref.refs_0_, f32[32,512]{1,0:T(8,128)S(1)} %get-tuple-element.10.cs_ref.refs_1_, ...), custom_call_target="tpu_custom_call" | custom-call | tf_op jit(solution)/shard_map/pallas_call | solution.py:73
  6.1 2.1 %collective-permute-start = (bf16[1,6,16,1024]{3,2,1,0:T(8,128)(2,1)S(1)}, bf16[1,6,16,1024]{3,2,1,0:T(8,128)(2,1)S(1)}, u32[]{:S(2)}, u32[]{:S(2)}) collective-permute-start(bf16[1,6,16,1024]{3,2,1,0:T(8,128)(2,1)S(1)} %bitcast.21), channel_id=1, source_target_pairs={{0,8},{1,9},{2,10},{3,11},{4,12},{5,13},{6,14},{7,15},{8,0},{9,1},... | collective-permute-start | bytes 589832 | tf_op jit(solution)/shard_map/ppermute | solution.py:354
  8.3 3.3 %collective-permute-done = bf16[1,6,16,1024]{3,2,1,0:T(8,128)(2,1)S(1)} collective-permute-done((bf16[1,6,16,1024]{3,2,1,0:T(8,128)(2,1)S(1)}, bf16[1,6,16,1024]{3,2,1,0:T(8,128)(2,1)S(1)}, u32[]{:S(2)}, u32[]{:S(2)}) %collective-permute-start) | collective-permute-done | bytes 196640 | tf_op jit(solution)/shard_map/ppermute | solution.py:354
  11.6 4.1 %collective-permute-start.2 = (bf16[2,6,16,1024]{3,2,1,0:T(8,128)(2,1)S(1)}, bf16[2,6,16,1024]{3,2,1,0:T(8,128)(2,1)S(1)}, u32[]{:S(2)}, u32[]{:S(2)}) collective-permute-start(bf16[2,6,16,1024]{3,2,1,0:T(8,128)(2,1)S(1)} %pad_maximum_fusion.refs_0_.refs_4_), channel_id=1, source_target_pairs={{0,6},{1,7},{2,0},{3,1},{4,2},{5,3},{6,4},{7,5},{8,14},{9,15},{10,... | collective-permute-start | bytes 1179656 | tf_op jit(solution)/shard_map/ppermute | solution.py:356
  16.8 1.8 %collective-permute-start.5 = (bf16[2,6,16,1024]{3,2,1,0:T(8,128)(2,1)S(1)}, bf16[2,6,16,1024]{3,2,1,0:T(8,128)(2,1)S(1)}, u32[]{:S(2)}, u32[]{:S(2)}) collective-permute-start(bf16[2,6,16,1024]{3,2,1,0:T(8,128)(2,1)S(1)} %pad_maximum_fusion.refs_0_.refs_4_), channel_id=1, source_target_pairs={{0,1},{1,0},{2,3},{3,2},{4,5},{5,4},{6,7},{7,6},{8,9},{9,8},{10,11... | collective-permute-start | bytes 1179656 | tf_op jit(solution)/shard_map/ppermute | solution.py:360
  18.7 3.9 %collective-permute-done.2.refs_2_.refs_6_ = bf16[2,6,16,1024]{3,2,1,0:T(8,128)(2,1)S(1)} collective-permute-done((bf16[2,6,16,1024]{3,2,1,0:T(8,128)(2,1)S(1)}, bf16[2,6,16,1024]{3,2,1,0:T(8,128)(2,1)S(1)}, u32[]{:S(2)}, u32[]{:S(2)}) %collective-permute-start.2) | collective-permute-done | bytes 393248 | tf_op jit(solution)/shard_map/ppermute | solution.py:356
  23.2 3.4 %collective-permute-start.4 = (bf16[1,6,16,1024]{3,2,1,0:T(8,128)(2,1)}, bf16[1,6,16,1024]{3,2,1,0:T(8,128)(2,1)S(1)}, u32[]{:S(2)}, u32[]{:S(2)}) collective-permute-start(bf16[1,6,16,1024]{3,2,1,0:T(8,128)(2,1)} %slice.33), channel_id=1, source_target_pairs={{0,6},{1,7},{2,0},{3,1},{4,2},{5,3},{6,4},{7,5},{8,14},{9,15},{10,... | collective-permute-start | bytes 589832 | tf_op jit(solution)/shard_map/ppermute | solution.py:358
  27.3 2.7 %collective-permute-start.7 = (bf16[2,6,16,1024]{3,2,1,0:T(8,128)(2,1)S(1)}, bf16[2,6,16,1024]{3,2,1,0:T(8,128)(2,1)S(1)}, u32[]{:S(2)}, u32[]{:S(2)}) collective-permute-start(bf16[2,6,16,1024]{3,2,1,0:T(8,128)(2,1)S(1)} %collective-permute-done.2.refs_2_.refs_6_), channel_id=1, source_target_pairs={{0,1},{1,0},{2,3},{3,2},{4,5},{5,4},{6,7},{7,6},{8,9},{9,8},{10,11... | collective-permute-start | bytes 1179656 | tf_op jit(solution)/shard_map/ppermute | solution.py:360
  30.9 2.0 %collective-permute-start.9 = (bf16[1,6,16,1024]{3,2,1,0:T(8,128)(2,1)S(1)}, bf16[1,6,16,1024]{3,2,1,0:T(8,128)(2,1)S(1)}, u32[]{:S(2)}, u32[]{:S(2)}) collective-permute-start(bf16[1,6,16,1024]{3,2,1,0:T(8,128)(2,1)S(1)} %collective-permute-done.4.refs_4_.refs_8_), channel_id=1, source_target_pairs={{0,1},{1,0},{2,3},{3,2},{4,5},{5,4},{6,7},{7,6},{8,9},{9,8},{10,11... | collective-permute-start | bytes 589832 | tf_op jit(solution)/shard_map/ppermute | solution.py:360
  33.3 3.9 %collective-permute-start.8 = (bf16[1,6,16,1024]{3,2,1,0:T(8,128)(2,1)S(1)}, bf16[1,6,16,1024]{3,2,1,0:T(8,128)(2,1)S(1)}, u32[]{:S(2)}, u32[]{:S(2)}) collective-permute-start(bf16[1,6,16,1024]{3,2,1,0:T(8,128)(2,1)S(1)} %collective-permute-done.3.refs_3_.refs_7_), channel_id=1, source_target_pairs={{0,1},{1,0},{2,3},{3,2},{4,5},{5,4},{6,7},{7,6},{8,9},{9,8},{10,11... | collective-permute-start | bytes 589832 | tf_op jit(solution)/shard_map/ppermute | solution.py:360
  38.3 2.0 %shard_map.38 = f32[128,256]{1,0:T(8,128)S(1)} custom-call(s32[16]{0:T(128)S(1)} %stack.67.order_ref, bf16[96,1024]{1,0:T(8,128)(2,1)S(1)} %shard_map.37.own_ref, f32[8,512]{1,0:T(8,128)S(1)} %get-tuple-element.9.cos_ref, f32[8,512]{1,0:T(8,128)S(1)} %get-tuple-element.8.sin_ref, bf16[2,6,16,1024]{3,2,1,0:T(8,128)(2,1)S(1)} %pad_maximum_fusion.refs_0_.refs_4_, ...), custom_call_target="tpu_custom_call" | custom-call | tf_op jit(solution)/shard_map/pallas_call | solution.py:329
  40.3 1.9 %collective-permute-start.10 = (f32[64,256]{1,0:T(8,128)S(1)}, f32[64,256]{1,0:T(8,128)S(1)}, u32[]{:S(2)}, u32[]{:S(2)}) collective-permute-start(f32[64,256]{1,0:T(8,128)S(1)} %slice_select_fusion), channel_id=1, source_target_pairs={{0,16},{16,0},{32,48},{48,32},{64,80},{80,64},{96,112},{112,96},{1... | collective-permute-start | bytes 196616 | tf_op jit(solution)/shard_map/ppermute | solution.py:379
  42.2 2.0 %collective-permute-done.10 = f32[64,256]{1,0:T(8,128)S(1)} collective-permute-done((f32[64,256]{1,0:T(8,128)S(1)}, f32[64,256]{1,0:T(8,128)S(1)}, u32[]{:S(2)}, u32[]{:S(2)}) %collective-permute-start.10) | collective-permute-done | bytes 65568 | tf_op jit(solution)/shard_map/ppermute | solution.py:379
  44.3 3.1 %collective-permute-start.11 = (f32[64,256]{1,0:T(8,128)S(1)}, f32[64,256]{1,0:T(8,128)S(1)}, u32[]{:S(2)}, u32[]{:S(2)}) collective-permute-start(f32[64,256]{1,0:T(8,128)S(1)} %select_add_fusion), channel_id=1, source_target_pairs={{0,32},{16,48},{32,0},{48,16},{64,96},{80,112},{96,64},{112,80},{1... | collective-permute-start | bytes 196616 | tf_op jit(solution)/shard_map/ppermute | solution.py:379
  47.4 1.7 %collective-permute-done.11 = f32[64,256]{1,0:T(8,128)S(1)} collective-permute-done((f32[64,256]{1,0:T(8,128)S(1)}, f32[64,256]{1,0:T(8,128)S(1)}, u32[]{:S(2)}, u32[]{:S(2)}) %collective-permute-start.11) | collective-permute-done | bytes 65568 | tf_op jit(solution)/shard_map/ppermute | solution.py:379
  49.0 6.5 %collective-permute-start.12 = (f32[64,256]{1,0:T(8,128)S(1)}, f32[64,256]{1,0:T(8,128)S(1)}, u32[]{:S(2)}, u32[]{:S(2)}) collective-permute-start(f32[64,256]{1,0:T(8,128)S(1)} %add.248), channel_id=1, source_target_pairs={{0,64},{16,80},{32,96},{48,112},{64,0},{80,16},{96,32},{112,48},{1... | collective-permute-start | bytes 196616 | tf_op jit(solution)/shard_map/ppermute | solution.py:379
  55.5 1.7 %collective-permute-done.12 = f32[64,256]{1,0:T(8,128)S(1)} collective-permute-done((f32[64,256]{1,0:T(8,128)S(1)}, f32[64,256]{1,0:T(8,128)S(1)}, u32[]{:S(2)}, u32[]{:S(2)}) %collective-permute-start.12) | collective-permute-done | bytes 65568 | tf_op jit(solution)/shard_map/ppermute | solution.py:379
  57.2 2.9 %collective-permute-start.13 = (f32[64,256]{1,0:T(8,128)S(1)}, f32[64,256]{1,0:T(8,128)S(1)}, u32[]{:S(2)}, u32[]{:S(2)}) collective-permute-start(f32[64,256]{1,0:T(8,128)S(1)} %add.249), channel_id=1, source_target_pairs={{0,128},{16,144},{32,160},{48,176},{64,192},{80,208},{96,224},{112... | collective-permute-start | bytes 196616 | tf_op jit(solution)/shard_map/ppermute | solution.py:379
  60.1 1.9 %collective-permute-done.13 = f32[64,256]{1,0:T(8,128)S(1)} collective-permute-done((f32[64,256]{1,0:T(8,128)S(1)}, f32[64,256]{1,0:T(8,128)S(1)}, u32[]{:S(2)}, u32[]{:S(2)}) %collective-permute-start.13) | collective-permute-done | bytes 65568 | tf_op jit(solution)/shard_map/ppermute | solution.py:379
  62.4 3.0 %collective-permute-done.14 = f32[64,256]{1,0:T(8,128)S(1)} collective-permute-done((f32[64,256]{1,0:T(8,128)S(1)}, f32[64,256]{1,0:T(8,128)S(1)}, u32[]{:S(2)}, u32[]{:S(2)}) %collective-permute-start.14) | collective-permute-done | bytes 65568 | tf_op jit(solution)/shard_map/ppermute | solution.py:379
  65.5 1.0 collective-permute-start.15
  66.5 2.2 %collective-permute-done.15 = f32[1,4,16,256]{3,2,1,0:T(8,128)S(1)} collective-permute-done((f32[1,4,16,256]{3,2,1,0:T(8,128)S(1)}, f32[1,4,16,256]{3,2,1,0:T(8,128)S(1)}, u32[]{:S(2)}, u32[]{:S(2)}) %collective-permute-start.15) | collective-permute-done | bytes 65568 | tf_op jit(solution)/shard_map/ppermute | solution.py:354
  68.8 1.5 %collective-permute-start.16 = (f32[2,4,16,256]{3,2,1,0:T(8,128)S(1)}, f32[2,4,16,256]{3,2,1,0:T(8,128)S(1)}, u32[]{:S(2)}, u32[]{:S(2)}) collective-permute-start(f32[2,4,16,256]{3,2,1,0:T(8,128)S(1)} %pad_maximum_fusion.1.refs_0_), channel_id=1, source_target_pairs={{0,2},{1,3},{2,4},{3,5},{4,6},{5,7},{6,0},{7,1},{8,10},{9,11},{10,... | collective-permute-start | bytes 393224 | tf_op jit(solution)/shard_map/ppermute | solution.py:355
  70.2 7.3 %collective-permute-start.20 = (f32[2,4,16,256]{3,2,1,0:T(8,128)S(1)}, f32[2,4,16,256]{3,2,1,0:T(8,128)S(1)}, u32[]{:S(2)}, u32[]{:S(2)}) collective-permute-start(f32[2,4,16,256]{3,2,1,0:T(8,128)S(1)} %pad_maximum_fusion.1.refs_0_), channel_id=1, source_target_pairs={{0,1},{1,0},{2,3},{3,2},{4,5},{5,4},{6,7},{7,6},{8,9},{9,8},{10,11... | collective-permute-start | bytes 393224 | tf_op jit(solution)/shard_map/ppermute | solution.py:360
  77.6 1.1 collective-permute-start.19
  79.2 3.4 %collective-permute-start.22 = (f32[2,4,16,256]{3,2,1,0:T(8,128)S(1)}, f32[2,4,16,256]{3,2,1,0:T(8,128)S(1)}, u32[]{:S(2)}, u32[]{:S(2)}) collective-permute-start(f32[2,4,16,256]{3,2,1,0:T(8,128)S(1)} %collective-permute-done.17.refs_2_), channel_id=1, source_target_pairs={{0,1},{1,0},{2,3},{3,2},{4,5},{5,4},{6,7},{7,6},{8,9},{9,8},{10,11... | collective-permute-start | bytes 393224 | tf_op jit(solution)/shard_map/ppermute | solution.py:360
  82.6 2.1 %collective-permute-start.24 = (f32[1,4,16,256]{3,2,1,0:T(8,128)S(1)}, f32[1,4,16,256]{3,2,1,0:T(8,128)S(1)}, u32[]{:S(2)}, u32[]{:S(2)}) collective-permute-start(f32[1,4,16,256]{3,2,1,0:T(8,128)S(1)} %collective-permute-done.19.refs_4_), channel_id=1, source_target_pairs={{0,1},{1,0},{2,3},{3,2},{4,5},{5,4},{6,7},{7,6},{8,9},{9,8},{10,11... | collective-permute-start | bytes 196616 | tf_op jit(solution)/shard_map/ppermute | solution.py:360
  84.8 2.5 %collective-permute-start.23 = (f32[1,4,16,256]{3,2,1,0:T(8,128)S(1)}, f32[1,4,16,256]{3,2,1,0:T(8,128)S(1)}, u32[]{:S(2)}, u32[]{:S(2)}) collective-permute-start(f32[1,4,16,256]{3,2,1,0:T(8,128)S(1)} %collective-permute-done.18.refs_3_), channel_id=1, source_target_pairs={{0,1},{1,0},{2,3},{3,2},{4,5},{5,4},{6,7},{7,6},{8,9},{9,8},{10,11... | collective-permute-start | bytes 196616 | tf_op jit(solution)/shard_map/ppermute | solution.py:360
  88.2 43.3 %shard_map.39.filter_ref = bf16[4,16,256]{2,1,0:T(8,128)(2,1)S(1)} custom-call(s32[16]{0:T(128)S(1)} %stack.67.order_ref, f32[4,16,256]{2,1,0:T(8,128)S(1)} %bitcast.23, f32[2,4,16,256]{3,2,1,0:T(8,128)S(1)} %pad_maximum_fusion.1.refs_0_, f32[2,4,16,256]{3,2,1,0:T(8,128)S(1)} %collective-permute-done.16.refs_1_, ...), custom_call_target="tpu_custom_call" | custom-call | tf_op jit(solution)/shard_map/pallas_call | solution.py:276
  131.5 6.0 %shard_map.40 = bf16[6,16,8192]{2,1,0:T(8,128)(2,1)} custom-call(s32[16]{0:T(128)S(1)} %stack.67.order_ref, bf16[4,16,256]{2,1,0:T(8,128)(2,1)S(1)} %shard_map.39.filter_ref, bf16[96,1024]{1,0:T(8,128)(2,1)S(1)} %shard_map.37.own_ref, f32[4,512]{1,0:T(4,128)S(1)} %slice.38.cos_ref, f32[4,512]{1,0:T(4,128)S(1)} %slice.39.sin_ref, f32[96,1]{1,0:T(8,128)S(1)} %copy-done.4, ...), custom_call_target="tpu_custom_call" | custom-call | tf_op jit(solution)/shard_map/pallas_call | solution.py:138
  (57 shorter events, 7.4 us)
Async XLA Ops:
  0.8 5.3 %copy-start.3 = (f32[96,1]{1,0:T(8,128)}, f32[96,1]{1,0:T(8,128)S(1)}, u32[]{:S(2)}) copy-start(f32[96,1]{1,0:T(8,128)S(1)} %reshape.23.live_ref) | copy-start | bytes 1156
  2.2 4.0 %copy-start.1 = (f32[32,512]{1,0:T(8,128)}, f32[32,512]{1,0:T(8,128)S(1)}, u32[]{:S(2)}) copy-start(f32[32,512]{1,0:T(8,128)S(1)} %get-tuple-element.11.cc_ref.refs_0_) | copy-start | bytes 196612
  2.2 1.4 %copy-start = (bf16[6,16,8192]{2,1,0:T(8,128)(2,1)S(1)}, bf16[6,16,8192]{2,1,0:T(8,128)(2,1)}, u32[]{:S(2)}) copy-start(bf16[6,16,8192]{2,1,0:T(8,128)(2,1)} %late_ref.1) | copy-start | bytes 4718596
  6.1 5.4 %collective-permute-start = (bf16[1,6,16,1024]{3,2,1,0:T(8,128)(2,1)S(1)}, bf16[1,6,16,1024]{3,2,1,0:T(8,128)(2,1)S(1)}, u32[]{:S(2)}, u32[]{:S(2)}) collective-permute-start(bf16[1,6,16,1024]{3,2,1,0:T(8,128)(2,1)S(1)} %bitcast.21), channel_id=1, source_target_pairs={{0,8},{1,9},{2,10},{3,11},{4,12},{5,13},{6,14},{7,15},{8,0},{9,1},... | collective-permute-start | bytes 589832 | tf_op jit(solution)/shard_map/ppermute | solution.py:354
  11.6 10.9 %collective-permute-start.2 = (bf16[2,6,16,1024]{3,2,1,0:T(8,128)(2,1)S(1)}, bf16[2,6,16,1024]{3,2,1,0:T(8,128)(2,1)S(1)}, u32[]{:S(2)}, u32[]{:S(2)}) collective-permute-start(bf16[2,6,16,1024]{3,2,1,0:T(8,128)(2,1)S(1)} %pad_maximum_fusion.refs_0_.refs_4_), channel_id=1, source_target_pairs={{0,6},{1,7},{2,0},{3,1},{4,2},{5,3},{6,4},{7,5},{8,14},{9,15},{10,... | collective-permute-start | bytes 1179656 | tf_op jit(solution)/shard_map/ppermute | solution.py:356
  15.7 11.0 %collective-permute-start.1 = (bf16[2,6,16,1024]{3,2,1,0:T(8,128)(2,1)S(1)}, bf16[2,6,16,1024]{3,2,1,0:T(8,128)(2,1)S(1)}, u32[]{:S(2)}, u32[]{:S(2)}) collective-permute-start(bf16[2,6,16,1024]{3,2,1,0:T(8,128)(2,1)S(1)} %pad_maximum_fusion.refs_0_.refs_4_), channel_id=1, source_target_pairs={{0,2},{1,3},{2,4},{3,5},{4,6},{5,7},{6,0},{7,1},{8,10},{9,11},{10,... | collective-permute-start | bytes 1179656 | tf_op jit(solution)/shard_map/ppermute | solution.py:355
  16.8 20.5 %collective-permute-start.5 = (bf16[2,6,16,1024]{3,2,1,0:T(8,128)(2,1)S(1)}, bf16[2,6,16,1024]{3,2,1,0:T(8,128)(2,1)S(1)}, u32[]{:S(2)}, u32[]{:S(2)}) collective-permute-start(bf16[2,6,16,1024]{3,2,1,0:T(8,128)(2,1)S(1)} %pad_maximum_fusion.refs_0_.refs_4_), channel_id=1, source_target_pairs={{0,1},{1,0},{2,3},{3,2},{4,5},{5,4},{6,7},{7,6},{8,9},{9,8},{10,11... | collective-permute-start | bytes 1179656 | tf_op jit(solution)/shard_map/ppermute | solution.py:360
  23.2 7.6 %collective-permute-start.4 = (bf16[1,6,16,1024]{3,2,1,0:T(8,128)(2,1)}, bf16[1,6,16,1024]{3,2,1,0:T(8,128)(2,1)S(1)}, u32[]{:S(2)}, u32[]{:S(2)}) collective-permute-start(bf16[1,6,16,1024]{3,2,1,0:T(8,128)(2,1)} %slice.33), channel_id=1, source_target_pairs={{0,6},{1,7},{2,0},{3,1},{4,2},{5,3},{6,4},{7,5},{8,14},{9,15},{10,... | collective-permute-start | bytes 589832 | tf_op jit(solution)/shard_map/ppermute | solution.py:358
  27.3 5.9 %collective-permute-start.3 = (bf16[1,6,16,1024]{3,2,1,0:T(8,128)(2,1)}, bf16[1,6,16,1024]{3,2,1,0:T(8,128)(2,1)S(1)}, u32[]{:S(2)}, u32[]{:S(2)}) collective-permute-start(bf16[1,6,16,1024]{3,2,1,0:T(8,128)(2,1)} %slice.32), channel_id=1, source_target_pairs={{0,2},{1,3},{2,4},{3,5},{4,6},{5,7},{6,0},{7,1},{8,10},{9,11},{10,... | collective-permute-start | bytes 589832 | tf_op jit(solution)/shard_map/ppermute | solution.py:357
  27.3 10.0 %collective-permute-start.7 = (bf16[2,6,16,1024]{3,2,1,0:T(8,128)(2,1)S(1)}, bf16[2,6,16,1024]{3,2,1,0:T(8,128)(2,1)S(1)}, u32[]{:S(2)}, u32[]{:S(2)}) collective-permute-start(bf16[2,6,16,1024]{3,2,1,0:T(8,128)(2,1)S(1)} %collective-permute-done.2.refs_2_.refs_6_), channel_id=1, source_target_pairs={{0,1},{1,0},{2,3},{3,2},{4,5},{5,4},{6,7},{7,6},{8,9},{9,8},{10,11... | collective-permute-start | bytes 1179656 | tf_op jit(solution)/shard_map/ppermute | solution.py:360
  30.1 8.2 %collective-permute-start.6 = (bf16[2,6,16,1024]{3,2,1,0:T(8,128)(2,1)S(1)}, bf16[2,6,16,1024]{3,2,1,0:T(8,128)(2,1)S(1)}, u32[]{:S(2)}, u32[]{:S(2)}) collective-permute-start(bf16[2,6,16,1024]{3,2,1,0:T(8,128)(2,1)S(1)} %collective-permute-done.1.refs_1_.refs_5_), channel_id=1, source_target_pairs={{0,1},{1,0},{2,3},{3,2},{4,5},{5,4},{6,7},{7,6},{8,9},{9,8},{10,11... | collective-permute-start | bytes 1179656 | tf_op jit(solution)/shard_map/ppermute | solution.py:360
  30.9 6.5 %collective-permute-start.9 = (bf16[1,6,16,1024]{3,2,1,0:T(8,128)(2,1)S(1)}, bf16[1,6,16,1024]{3,2,1,0:T(8,128)(2,1)S(1)}, u32[]{:S(2)}, u32[]{:S(2)}) collective-permute-start(bf16[1,6,16,1024]{3,2,1,0:T(8,128)(2,1)S(1)} %collective-permute-done.4.refs_4_.refs_8_), channel_id=1, source_target_pairs={{0,1},{1,0},{2,3},{3,2},{4,5},{5,4},{6,7},{7,6},{8,9},{9,8},{10,11... | collective-permute-start | bytes 589832 | tf_op jit(solution)/shard_map/ppermute | solution.py:360
  33.3 5.0 %collective-permute-start.8 = (bf16[1,6,16,1024]{3,2,1,0:T(8,128)(2,1)S(1)}, bf16[1,6,16,1024]{3,2,1,0:T(8,128)(2,1)S(1)}, u32[]{:S(2)}, u32[]{:S(2)}) collective-permute-start(bf16[1,6,16,1024]{3,2,1,0:T(8,128)(2,1)S(1)} %collective-permute-done.3.refs_3_.refs_7_), channel_id=1, source_target_pairs={{0,1},{1,0},{2,3},{3,2},{4,5},{5,4},{6,7},{7,6},{8,9},{9,8},{10,11... | collective-permute-start | bytes 589832 | tf_op jit(solution)/shard_map/ppermute | solution.py:360
  40.3 91.2 %copy-start.2 = (f32[32,512]{1,0:T(8,128)S(1)}, f32[32,512]{1,0:T(8,128)}, u32[]{:S(2)}) copy-start(f32[32,512]{1,0:T(8,128)} %copy-done.1) | copy-start | bytes 196612
  40.3 91.2 %copy-start.4 = (f32[96,1]{1,0:T(8,128)S(1)}, f32[96,1]{1,0:T(8,128)}, u32[]{:S(2)}) copy-start(f32[96,1]{1,0:T(8,128)} %copy-done.3) | copy-start | bytes 1156
  40.3 4.0 %collective-permute-start.10 = (f32[64,256]{1,0:T(8,128)S(1)}, f32[64,256]{1,0:T(8,128)S(1)}, u32[]{:S(2)}, u32[]{:S(2)}) collective-permute-start(f32[64,256]{1,0:T(8,128)S(1)} %slice_select_fusion), channel_id=1, source_target_pairs={{0,16},{16,0},{32,48},{48,32},{64,80},{80,64},{96,112},{112,96},{1... | collective-permute-start | bytes 196616 | tf_op jit(solution)/shard_map/ppermute | solution.py:379
  44.3 4.7 %collective-permute-start.11 = (f32[64,256]{1,0:T(8,128)S(1)}, f32[64,256]{1,0:T(8,128)S(1)}, u32[]{:S(2)}, u32[]{:S(2)}) collective-permute-start(f32[64,256]{1,0:T(8,128)S(1)} %select_add_fusion), channel_id=1, source_target_pairs={{0,32},{16,48},{32,0},{48,16},{64,96},{80,112},{96,64},{112,80},{1... | collective-permute-start | bytes 196616 | tf_op jit(solution)/shard_map/ppermute | solution.py:379
  49.0 8.2 %collective-permute-start.12 = (f32[64,256]{1,0:T(8,128)S(1)}, f32[64,256]{1,0:T(8,128)S(1)}, u32[]{:S(2)}, u32[]{:S(2)}) collective-permute-start(f32[64,256]{1,0:T(8,128)S(1)} %add.248), channel_id=1, source_target_pairs={{0,64},{16,80},{32,96},{48,112},{64,0},{80,16},{96,32},{112,48},{1... | collective-permute-start | bytes 196616 | tf_op jit(solution)/shard_map/ppermute | solution.py:379
  57.2 4.7 %collective-permute-start.13 = (f32[64,256]{1,0:T(8,128)S(1)}, f32[64,256]{1,0:T(8,128)S(1)}, u32[]{:S(2)}, u32[]{:S(2)}) collective-permute-start(f32[64,256]{1,0:T(8,128)S(1)} %add.249), channel_id=1, source_target_pairs={{0,128},{16,144},{32,160},{48,176},{64,192},{80,208},{96,224},{112... | collective-permute-start | bytes 196616 | tf_op jit(solution)/shard_map/ppermute | solution.py:379
  62.0 3.5 %collective-permute-start.14 = (f32[64,256]{1,0:T(8,128)S(1)}, f32[64,256]{1,0:T(8,128)S(1)}, u32[]{:S(2)}, u32[]{:S(2)}) collective-permute-start(f32[64,256]{1,0:T(8,128)S(1)} %add.250), channel_id=1, source_target_pairs={{0,16},{16,0},{32,48},{48,32},{64,80},{80,64},{96,112},{112,96},{1... | collective-permute-start | bytes 196616 | tf_op jit(solution)/shard_map/ppermute | solution.py:379
  65.5 3.2 %collective-permute-start.15 = (f32[1,4,16,256]{3,2,1,0:T(8,128)S(1)}, f32[1,4,16,256]{3,2,1,0:T(8,128)S(1)}, u32[]{:S(2)}, u32[]{:S(2)}) collective-permute-start(f32[1,4,16,256]{3,2,1,0:T(8,128)S(1)} %bitcast.24), channel_id=1, source_target_pairs={{0,8},{1,9},{2,10},{3,11},{4,12},{5,13},{6,14},{7,15},{8,0},{9,1},... | collective-permute-start | bytes 196616 | tf_op jit(solution)/shard_map/ppermute | solution.py:354
  68.7 8.9 %collective-permute-start.17 = (f32[2,4,16,256]{3,2,1,0:T(8,128)S(1)}, f32[2,4,16,256]{3,2,1,0:T(8,128)S(1)}, u32[]{:S(2)}, u32[]{:S(2)}) collective-permute-start(f32[2,4,16,256]{3,2,1,0:T(8,128)S(1)} %pad_maximum_fusion.1.refs_0_), channel_id=1, source_target_pairs={{0,6},{1,7},{2,0},{3,1},{4,2},{5,3},{6,4},{7,5},{8,14},{9,15},{10,... | collective-permute-start | bytes 393224 | tf_op jit(solution)/shard_map/ppermute | solution.py:356
  68.8 9.9 %collective-permute-start.16 = (f32[2,4,16,256]{3,2,1,0:T(8,128)S(1)}, f32[2,4,16,256]{3,2,1,0:T(8,128)S(1)}, u32[]{:S(2)}, u32[]{:S(2)}) collective-permute-start(f32[2,4,16,256]{3,2,1,0:T(8,128)S(1)} %pad_maximum_fusion.1.refs_0_), channel_id=1, source_target_pairs={{0,2},{1,3},{2,4},{3,5},{4,6},{5,7},{6,0},{7,1},{8,10},{9,11},{10,... | collective-permute-start | bytes 393224 | tf_op jit(solution)/shard_map/ppermute | solution.py:355
  70.2 17.1 %collective-permute-start.20 = (f32[2,4,16,256]{3,2,1,0:T(8,128)S(1)}, f32[2,4,16,256]{3,2,1,0:T(8,128)S(1)}, u32[]{:S(2)}, u32[]{:S(2)}) collective-permute-start(f32[2,4,16,256]{3,2,1,0:T(8,128)S(1)} %pad_maximum_fusion.1.refs_0_), channel_id=1, source_target_pairs={{0,1},{1,0},{2,3},{3,2},{4,5},{5,4},{6,7},{7,6},{8,9},{9,8},{10,11... | collective-permute-start | bytes 393224 | tf_op jit(solution)/shard_map/ppermute | solution.py:360
  77.6 5.1 %collective-permute-start.19 = (f32[1,4,16,256]{3,2,1,0:T(8,128)S(1)}, f32[1,4,16,256]{3,2,1,0:T(8,128)S(1)}, u32[]{:S(2)}, u32[]{:S(2)}) collective-permute-start(f32[1,4,16,256]{3,2,1,0:T(8,128)S(1)} %slice.37), channel_id=1, source_target_pairs={{0,6},{1,7},{2,0},{3,1},{4,2},{5,3},{6,4},{7,5},{8,14},{9,15},{10,... | collective-permute-start | bytes 196616 | tf_op jit(solution)/shard_map/ppermute | solution.py:358
  78.7 6.1 %collective-permute-start.18 = (f32[1,4,16,256]{3,2,1,0:T(8,128)S(1)}, f32[1,4,16,256]{3,2,1,0:T(8,128)S(1)}, u32[]{:S(2)}, u32[]{:S(2)}) collective-permute-start(f32[1,4,16,256]{3,2,1,0:T(8,128)S(1)} %slice.36), channel_id=1, source_target_pairs={{0,2},{1,3},{2,4},{3,5},{4,6},{5,7},{6,0},{7,1},{8,10},{9,11},{10,... | collective-permute-start | bytes 196616 | tf_op jit(solution)/shard_map/ppermute | solution.py:357
  79.2 8.1 %collective-permute-start.22 = (f32[2,4,16,256]{3,2,1,0:T(8,128)S(1)}, f32[2,4,16,256]{3,2,1,0:T(8,128)S(1)}, u32[]{:S(2)}, u32[]{:S(2)}) collective-permute-start(f32[2,4,16,256]{3,2,1,0:T(8,128)S(1)} %collective-permute-done.17.refs_2_), channel_id=1, source_target_pairs={{0,1},{1,0},{2,3},{3,2},{4,5},{5,4},{6,7},{7,6},{8,9},{9,8},{10,11... | collective-permute-start | bytes 393224 | tf_op jit(solution)/shard_map/ppermute | solution.py:360
  82.6 5.6 %collective-permute-start.21 = (f32[2,4,16,256]{3,2,1,0:T(8,128)S(1)}, f32[2,4,16,256]{3,2,1,0:T(8,128)S(1)}, u32[]{:S(2)}, u32[]{:S(2)}) collective-permute-start(f32[2,4,16,256]{3,2,1,0:T(8,128)S(1)} %collective-permute-done.16.refs_1_), channel_id=1, source_target_pairs={{0,1},{1,0},{2,3},{3,2},{4,5},{5,4},{6,7},{7,6},{8,9},{9,8},{10,11... | collective-permute-start | bytes 393224 | tf_op jit(solution)/shard_map/ppermute | solution.py:360
  82.6 4.7 %collective-permute-start.24 = (f32[1,4,16,256]{3,2,1,0:T(8,128)S(1)}, f32[1,4,16,256]{3,2,1,0:T(8,128)S(1)}, u32[]{:S(2)}, u32[]{:S(2)}) collective-permute-start(f32[1,4,16,256]{3,2,1,0:T(8,128)S(1)} %collective-permute-done.19.refs_4_), channel_id=1, source_target_pairs={{0,1},{1,0},{2,3},{3,2},{4,5},{5,4},{6,7},{7,6},{8,9},{9,8},{10,11... | collective-permute-start | bytes 196616 | tf_op jit(solution)/shard_map/ppermute | solution.py:360
  84.8 3.4 %collective-permute-start.23 = (f32[1,4,16,256]{3,2,1,0:T(8,128)S(1)}, f32[1,4,16,256]{3,2,1,0:T(8,128)S(1)}, u32[]{:S(2)}, u32[]{:S(2)}) collective-permute-start(f32[1,4,16,256]{3,2,1,0:T(8,128)S(1)} %collective-permute-done.18.refs_3_), channel_id=1, source_target_pairs={{0,1},{1,0},{2,3},{3,2},{4,5},{5,4},{6,7},{7,6},{8,9},{9,8},{10,11... | collective-permute-start | bytes 196616 | tf_op jit(solution)/shard_map/ppermute | solution.py:360

commit v7 on v6

--- a/solution.py
+++ b/solution.py
@@ -8,7 +8,7 @@
 LAGS = 4
 CHUNK = 4096
 BACK_CHUNK = 4096
-FINE = 128
+FINE = 64
 f32 = jnp.float32
 bf = jnp.bfloat16
 VM = pl.BlockSpec(memory_space=pltpu.VMEM)
@@ -81,7 +81,7 @@
         + [VM] * 5,
         out_specs=pl.BlockSpec((rows, 2 * band), lambda i: (0, 0)),
         scratch_shapes=[pltpu.VMEM((2 * rows, 2 * band), f32), pltpu.VMEM((CHUNK, 2 * band), bf)],
-        compiler_params=pltpu.CompilerParams(vmem_limit_bytes=40 * 2**20),
+        compiler_params=pltpu.CompilerParams(vmem_limit_bytes=60 * 2**20),
     )(traces, traces, live.reshape(rows, 1), *waves)
 
 

time: 138 us -> 139 us (level)
  Pallas kernels: 53.8 us -> 56 us
  local copies, waits for them, and re-layouts: 3.02 us -> 0.87 us
    pallas_call x1, Pallas kernels: 2.5 us -> 4.69 us  [forward(): pl.pallas_call(forward_kernel, grid=(steps,), out_shape=jax.ShapeDtypeStr...]
    unnamed x10 -> x12, local copies, waits for them, and re-layouts: 1.45 us -> 0.03 us
  transfers between devices with their start and end apart: 25 -> 25, of which waited for: 11 -> 10; matrix products, arithmetic and copies ran while one was open for 2% -> 0% of each run, Pallas kernels for 0% -> 0%
where the time goes in v7:
time: 139 us
  Pallas kernels  56 us (40%)
  starting transfers between devices  55.4 us (40%)
  waiting for transfers between devices  22.2 us (16%)
  other arithmetic  3.84 us (3%)
    pallas_call x1, Pallas kernels, solve_filter(): pl.pallas_call(solve_kernel, out_shape=jax.ShapeDtypeStruct((LAGS, chans,...  43.3 us
    ppermute x10, starting transfers between devices, gather_lag(): return near + [lax.ppermute(piece, 'lag', over_core) for piece in near]  26.9 us
    ppermute x5, starting transfers between devices, other(): return lax.ppermute(part, 'shot', [(i, i ^ bit) for i in range(16)])  14.7 us
    ppermute x5, waiting for transfers between devices, other(): return lax.ppermute(part, 'shot', [(i, i ^ bit) for i in range(16)])  10.3 us
    pallas_call x1, Pallas kernels, inverse(): pl.pallas_call(inverse_kernel, grid=(steps, 2), out_shape=jax.ShapeDtypeS...  6.09 us
    ppermute x2, waiting for transfers between devices, gather_lag(): pair = jnp.concatenate([own, lax.ppermute(own, 'lag', over_x)], axis=0)  5.78 us
    pallas_call x1, Pallas kernels, forward(): pl.pallas_call(forward_kernel, grid=(steps,), out_shape=jax.ShapeDtypeStr...  4.69 us
    ppermute x2, starting transfers between devices, gather_lag(): far_other = lax.ppermute(above[1:], 'lag', down)  4.67 us
  transfers between devices with their start and end apart: 25, of which 10 were waited for; matrix products, arithmetic and copies ran while one was open for 0% of the time, Pallas kernels for 0%

profile of v7, /device:TPU:1, one launch (start us, length us, event | category | flops | bytes accessed | tf_op | source)
XLA Modules:
  0.0 139.3 jit_solution(12538830743244887520)
XLA Ops:
  1.4 1.9 %fusion.11 = (f32[64,512]{1,0:T(8,128)}, f32[64,512]{1,0:T(8,128)}, f32[64,512]{1,0:T(8,128)}, f32[64,512]{1,0:T(8,128)}) fusion(s32[512]{0:T(512)S(1)} %iota_add_fusion, s32[64]{0:T(128)S(1)} %iota_multiply_fusion.1), kind=kLoop, calls=%fused_computation.24 | loop fusion | flops 917504 | bytes 526592 | tf_op jit(solution)/shard_map/sin | solution.py:21
  3.3 4.7 %shard_map.37.own_ref = bf16[96,1024]{1,0:T(8,128)(2,1)} custom-call(bf16[6,16,8192]{2,1,0:T(8,128)(2,1)} %late_ref.1, bf16[6,16,8192]{2,1,0:T(8,128)(2,1)} %late_ref.1, f32[96,1]{1,0:T(8,128)} %reshape.23.live_ref, f32[64,512]{1,0:T(8,128)} %get-tuple-element.11.cc_ref.refs_0_, f32[64,512]{1,0:T(8,128)} %get-tuple-element.10.cs_ref.refs_1_, ...), custom_call_target="tpu_custom_call" | custom-call | tf_op jit(solution)/shard_map/pallas_call | solution.py:73
  8.0 2.0 %collective-permute-start = (bf16[1,6,16,1024]{3,2,1,0:T(8,128)(2,1)}, bf16[1,6,16,1024]{3,2,1,0:T(8,128)(2,1)S(1)}, u32[]{:S(2)}, u32[]{:S(2)}) collective-permute-start(bf16[1,6,16,1024]{3,2,1,0:T(8,128)(2,1)} %bitcast.21), channel_id=1, source_target_pairs={{0,8},{1,9},{2,10},{3,11},{4,12},{5,13},{6,14},{7,15},{8,0},{9,1},... | collective-permute-start | bytes 589832 | tf_op jit(solution)/shard_map/ppermute | solution.py:354
  10.0 3.5 %collective-permute-done = bf16[1,6,16,1024]{3,2,1,0:T(8,128)(2,1)S(1)} collective-permute-done((bf16[1,6,16,1024]{3,2,1,0:T(8,128)(2,1)}, bf16[1,6,16,1024]{3,2,1,0:T(8,128)(2,1)S(1)}, u32[]{:S(2)}, u32[]{:S(2)}) %collective-permute-start) | collective-permute-done | bytes 196640 | tf_op jit(solution)/shard_map/ppermute | solution.py:354
  13.5 1.0 pad_maximum_fusion.refs_0_.refs_4_
  14.5 4.1 %collective-permute-start.2 = (bf16[2,6,16,1024]{3,2,1,0:T(8,128)(2,1)S(1)}, bf16[2,6,16,1024]{3,2,1,0:T(8,128)(2,1)S(1)}, u32[]{:S(2)}, u32[]{:S(2)}) collective-permute-start(bf16[2,6,16,1024]{3,2,1,0:T(8,128)(2,1)S(1)} %pad_maximum_fusion.refs_0_.refs_4_), channel_id=1, source_target_pairs={{0,6},{1,7},{2,0},{3,1},{4,2},{5,3},{6,4},{7,5},{8,14},{9,15},{10,... | collective-permute-start | bytes 1179656 | tf_op jit(solution)/shard_map/ppermute | solution.py:356
  19.2 1.9 %collective-permute-start.5 = (bf16[2,6,16,1024]{3,2,1,0:T(8,128)(2,1)S(1)}, bf16[2,6,16,1024]{3,2,1,0:T(8,128)(2,1)S(1)}, u32[]{:S(2)}, u32[]{:S(2)}) collective-permute-start(bf16[2,6,16,1024]{3,2,1,0:T(8,128)(2,1)S(1)} %pad_maximum_fusion.refs_0_.refs_4_), channel_id=1, source_target_pairs={{0,1},{1,0},{2,3},{3,2},{4,5},{5,4},{6,7},{7,6},{8,9},{9,8},{10,11... | collective-permute-start | bytes 1179656 | tf_op jit(solution)/shard_map/ppermute | solution.py:360
  21.1 4.3 %collective-permute-done.2.refs_2_.refs_6_ = bf16[2,6,16,1024]{3,2,1,0:T(8,128)(2,1)S(1)} collective-permute-done((bf16[2,6,16,1024]{3,2,1,0:T(8,128)(2,1)S(1)}, bf16[2,6,16,1024]{3,2,1,0:T(8,128)(2,1)S(1)}, u32[]{:S(2)}, u32[]{:S(2)}) %collective-permute-start.2) | collective-permute-done | bytes 393248 | tf_op jit(solution)/shard_map/ppermute | solution.py:356
  25.4 3.5 %collective-permute-start.4 = (bf16[1,6,16,1024]{3,2,1,0:T(8,128)(2,1)S(1)}, bf16[1,6,16,1024]{3,2,1,0:T(8,128)(2,1)S(1)}, u32[]{:S(2)}, u32[]{:S(2)}) collective-permute-start(bf16[1,6,16,1024]{3,2,1,0:T(8,128)(2,1)S(1)} %slice.33), channel_id=1, source_target_pairs={{0,6},{1,7},{2,0},{3,1},{4,2},{5,3},{6,4},{7,5},{8,14},{9,15},{10,... | collective-permute-start | bytes 589832 | tf_op jit(solution)/shard_map/ppermute | solution.py:358
  29.0 2.8 %collective-permute-start.7 = (bf16[2,6,16,1024]{3,2,1,0:T(8,128)(2,1)S(1)}, bf16[2,6,16,1024]{3,2,1,0:T(8,128)(2,1)S(1)}, u32[]{:S(2)}, u32[]{:S(2)}) collective-permute-start(bf16[2,6,16,1024]{3,2,1,0:T(8,128)(2,1)S(1)} %collective-permute-done.2.refs_2_.refs_6_), channel_id=1, source_target_pairs={{0,1},{1,0},{2,3},{3,2},{4,5},{5,4},{6,7},{7,6},{8,9},{9,8},{10,11... | collective-permute-start | bytes 1179656 | tf_op jit(solution)/shard_map/ppermute | solution.py:360
  32.2 2.7 %collective-permute-start.9 = (bf16[1,6,16,1024]{3,2,1,0:T(8,128)(2,1)S(1)}, bf16[1,6,16,1024]{3,2,1,0:T(8,128)(2,1)S(1)}, u32[]{:S(2)}, u32[]{:S(2)}) collective-permute-start(bf16[1,6,16,1024]{3,2,1,0:T(8,128)(2,1)S(1)} %collective-permute-done.4.refs_4_.refs_8_), channel_id=1, source_target_pairs={{0,1},{1,0},{2,3},{3,2},{4,5},{5,4},{6,7},{7,6},{8,9},{9,8},{10,11... | collective-permute-start | bytes 589832 | tf_op jit(solution)/shard_map/ppermute | solution.py:360
  34.9 3.8 %collective-permute-start.8 = (bf16[1,6,16,1024]{3,2,1,0:T(8,128)(2,1)S(1)}, bf16[1,6,16,1024]{3,2,1,0:T(8,128)(2,1)S(1)}, u32[]{:S(2)}, u32[]{:S(2)}) collective-permute-start(bf16[1,6,16,1024]{3,2,1,0:T(8,128)(2,1)S(1)} %collective-permute-done.3.refs_3_.refs_7_), channel_id=1, source_target_pairs={{0,1},{1,0},{2,3},{3,2},{4,5},{5,4},{6,7},{7,6},{8,9},{9,8},{10,11... | collective-permute-start | bytes 589832 | tf_op jit(solution)/shard_map/ppermute | solution.py:360
  39.7 2.0 %shard_map.38 = f32[128,256]{1,0:T(8,128)S(1)} custom-call(s32[16]{0:T(128)S(1)} %stack.67.order_ref, bf16[96,1024]{1,0:T(8,128)(2,1)S(1)} %copy-done, f32[8,512]{1,0:T(8,128)S(1)} %get-tuple-element.9.cos_ref, f32[8,512]{1,0:T(8,128)S(1)} %get-tuple-element.8.sin_ref, bf16[2,6,16,1024]{3,2,1,0:T(8,128)(2,1)S(1)} %pad_maximum_fusion.refs_0_.refs_4_, ...), custom_call_target="tpu_custom_call" | custom-call | tf_op jit(solution)/shard_map/pallas_call | solution.py:329
  41.8 1.7 %collective-permute-start.10 = (f32[64,256]{1,0:T(8,128)S(1)}, f32[64,256]{1,0:T(8,128)S(1)}, u32[]{:S(2)}, u32[]{:S(2)}) collective-permute-start(f32[64,256]{1,0:T(8,128)S(1)} %slice_select_fusion), channel_id=1, source_target_pairs={{0,16},{16,0},{32,48},{48,32},{64,80},{80,64},{96,112},{112,96},{1... | collective-permute-start | bytes 196616 | tf_op jit(solution)/shard_map/ppermute | solution.py:379
  43.5 2.0 %collective-permute-done.10 = f32[64,256]{1,0:T(8,128)S(1)} collective-permute-done((f32[64,256]{1,0:T(8,128)S(1)}, f32[64,256]{1,0:T(8,128)S(1)}, u32[]{:S(2)}, u32[]{:S(2)}) %collective-permute-start.10) | collective-permute-done | bytes 65568 | tf_op jit(solution)/shard_map/ppermute | solution.py:379
  45.5 3.3 %collective-permute-start.11 = (f32[64,256]{1,0:T(8,128)S(1)}, f32[64,256]{1,0:T(8,128)S(1)}, u32[]{:S(2)}, u32[]{:S(2)}) collective-permute-start(f32[64,256]{1,0:T(8,128)S(1)} %select_add_fusion), channel_id=1, source_target_pairs={{0,32},{16,48},{32,0},{48,16},{64,96},{80,112},{96,64},{112,80},{1... | collective-permute-start | bytes 196616 | tf_op jit(solution)/shard_map/ppermute | solution.py:379
  48.8 1.7 %collective-permute-done.11 = f32[64,256]{1,0:T(8,128)S(1)} collective-permute-done((f32[64,256]{1,0:T(8,128)S(1)}, f32[64,256]{1,0:T(8,128)S(1)}, u32[]{:S(2)}, u32[]{:S(2)}) %collective-permute-start.11) | collective-permute-done | bytes 65568 | tf_op jit(solution)/shard_map/ppermute | solution.py:379
  50.5 6.5 %collective-permute-start.12 = (f32[64,256]{1,0:T(8,128)S(1)}, f32[64,256]{1,0:T(8,128)S(1)}, u32[]{:S(2)}, u32[]{:S(2)}) collective-permute-start(f32[64,256]{1,0:T(8,128)S(1)} %add.246), channel_id=1, source_target_pairs={{0,64},{16,80},{32,96},{48,112},{64,0},{80,16},{96,32},{112,48},{1... | collective-permute-start | bytes 196616 | tf_op jit(solution)/shard_map/ppermute | solution.py:379
  57.0 1.7 %collective-permute-done.12 = f32[64,256]{1,0:T(8,128)S(1)} collective-permute-done((f32[64,256]{1,0:T(8,128)S(1)}, f32[64,256]{1,0:T(8,128)S(1)}, u32[]{:S(2)}, u32[]{:S(2)}) %collective-permute-start.12) | collective-permute-done | bytes 65568 | tf_op jit(solution)/shard_map/ppermute | solution.py:379
  58.7 2.8 %collective-permute-start.13 = (f32[64,256]{1,0:T(8,128)S(1)}, f32[64,256]{1,0:T(8,128)S(1)}, u32[]{:S(2)}, u32[]{:S(2)}) collective-permute-start(f32[64,256]{1,0:T(8,128)S(1)} %add.247), channel_id=1, source_target_pairs={{0,128},{16,144},{32,160},{48,176},{64,192},{80,208},{96,224},{112... | collective-permute-start | bytes 196616 | tf_op jit(solution)/shard_map/ppermute | solution.py:379
  61.5 1.9 %collective-permute-done.13 = f32[64,256]{1,0:T(8,128)S(1)} collective-permute-done((f32[64,256]{1,0:T(8,128)S(1)}, f32[64,256]{1,0:T(8,128)S(1)}, u32[]{:S(2)}, u32[]{:S(2)}) %collective-permute-start.13) | collective-permute-done | bytes 65568 | tf_op jit(solution)/shard_map/ppermute | solution.py:379
  63.9 3.1 %collective-permute-done.14 = f32[64,256]{1,0:T(8,128)S(1)} collective-permute-done((f32[64,256]{1,0:T(8,128)S(1)}, f32[64,256]{1,0:T(8,128)S(1)}, u32[]{:S(2)}, u32[]{:S(2)}) %collective-permute-start.14) | collective-permute-done | bytes 65568 | tf_op jit(solution)/shard_map/ppermute | solution.py:379
  66.9 1.0 collective-permute-start.15
  67.9 2.3 %collective-permute-done.15 = f32[1,4,16,256]{3,2,1,0:T(8,128)S(1)} collective-permute-done((f32[1,4,16,256]{3,2,1,0:T(8,128)S(1)}, f32[1,4,16,256]{3,2,1,0:T(8,128)S(1)}, u32[]{:S(2)}, u32[]{:S(2)}) %collective-permute-start.15) | collective-permute-done | bytes 65568 | tf_op jit(solution)/shard_map/ppermute | solution.py:354
  70.3 1.4 %collective-permute-start.16 = (f32[2,4,16,256]{3,2,1,0:T(8,128)S(1)}, f32[2,4,16,256]{3,2,1,0:T(8,128)S(1)}, u32[]{:S(2)}, u32[]{:S(2)}) collective-permute-start(f32[2,4,16,256]{3,2,1,0:T(8,128)S(1)} %pad_maximum_fusion.1.refs_0_), channel_id=1, source_target_pairs={{0,2},{1,3},{2,4},{3,5},{4,6},{5,7},{6,0},{7,1},{8,10},{9,11},{10,... | collective-permute-start | bytes 393224 | tf_op jit(solution)/shard_map/ppermute | solution.py:355
  71.7 7.3 %collective-permute-start.20 = (f32[2,4,16,256]{3,2,1,0:T(8,128)S(1)}, f32[2,4,16,256]{3,2,1,0:T(8,128)S(1)}, u32[]{:S(2)}, u32[]{:S(2)}) collective-permute-start(f32[2,4,16,256]{3,2,1,0:T(8,128)S(1)} %pad_maximum_fusion.1.refs_0_), channel_id=1, source_target_pairs={{0,1},{1,0},{2,3},{3,2},{4,5},{5,4},{6,7},{7,6},{8,9},{9,8},{10,11... | collective-permute-start | bytes 393224 | tf_op jit(solution)/shard_map/ppermute | solution.py:360
  79.0 1.2 collective-permute-start.19
  80.7 3.4 %collective-permute-start.22 = (f32[2,4,16,256]{3,2,1,0:T(8,128)S(1)}, f32[2,4,16,256]{3,2,1,0:T(8,128)S(1)}, u32[]{:S(2)}, u32[]{:S(2)}) collective-permute-start(f32[2,4,16,256]{3,2,1,0:T(8,128)S(1)} %collective-permute-done.17.refs_2_), channel_id=1, source_target_pairs={{0,1},{1,0},{2,3},{3,2},{4,5},{5,4},{6,7},{7,6},{8,9},{9,8},{10,11... | collective-permute-start | bytes 393224 | tf_op jit(solution)/shard_map/ppermute | solution.py:360
  84.1 2.1 %collective-permute-start.24 = (f32[1,4,16,256]{3,2,1,0:T(8,128)S(1)}, f32[1,4,16,256]{3,2,1,0:T(8,128)S(1)}, u32[]{:S(2)}, u32[]{:S(2)}) collective-permute-start(f32[1,4,16,256]{3,2,1,0:T(8,128)S(1)} %collective-permute-done.19.refs_4_), channel_id=1, source_target_pairs={{0,1},{1,0},{2,3},{3,2},{4,5},{5,4},{6,7},{7,6},{8,9},{9,8},{10,11... | collective-permute-start | bytes 196616 | tf_op jit(solution)/shard_map/ppermute | solution.py:360
  86.2 2.7 %collective-permute-start.23 = (f32[1,4,16,256]{3,2,1,0:T(8,128)S(1)}, f32[1,4,16,256]{3,2,1,0:T(8,128)S(1)}, u32[]{:S(2)}, u32[]{:S(2)}) collective-permute-start(f32[1,4,16,256]{3,2,1,0:T(8,128)S(1)} %collective-permute-done.18.refs_3_), channel_id=1, source_target_pairs={{0,1},{1,0},{2,3},{3,2},{4,5},{5,4},{6,7},{7,6},{8,9},{9,8},{10,11... | collective-permute-start | bytes 196616 | tf_op jit(solution)/shard_map/ppermute | solution.py:360
  89.8 43.3 %shard_map.39.filter_ref = bf16[4,16,256]{2,1,0:T(8,128)(2,1)S(1)} custom-call(s32[16]{0:T(128)S(1)} %stack.67.order_ref, f32[4,16,256]{2,1,0:T(8,128)S(1)} %bitcast.23, f32[2,4,16,256]{3,2,1,0:T(8,128)S(1)} %pad_maximum_fusion.1.refs_0_, f32[2,4,16,256]{3,2,1,0:T(8,128)S(1)} %collective-permute-done.16.refs_1_, ...), custom_call_target="tpu_custom_call" | custom-call | tf_op jit(solution)/shard_map/pallas_call | solution.py:276
  133.2 6.1 %shard_map.40 = bf16[6,16,8192]{2,1,0:T(8,128)(2,1)} custom-call(s32[16]{0:T(128)S(1)} %stack.67.order_ref, bf16[4,16,256]{2,1,0:T(8,128)(2,1)S(1)} %shard_map.39.filter_ref, bf16[96,1024]{1,0:T(8,128)(2,1)S(1)} %copy-done, f32[4,512]{1,0:T(4,128)S(1)} %slice.38.cos_ref, f32[4,512]{1,0:T(4,128)S(1)} %slice.39.sin_ref, f32[96,1]{1,0:T(8,128)S(1)} %copy-done.5, ...), custom_call_target="tpu_custom_call" | custom-call | tf_op jit(solution)/shard_map/pallas_call | solution.py:138
  (58 shorter events, 4.8 us)
Async XLA Ops:
  8.0 31.8 %copy-start = (bf16[96,1024]{1,0:T(8,128)(2,1)S(1)}, bf16[96,1024]{1,0:T(8,128)(2,1)}, u32[]{:S(2)}) copy-start(bf16[96,1024]{1,0:T(8,128)(2,1)} %shard_map.37.own_ref) | copy-start | bytes 589828
  8.0 5.6 %collective-permute-start = (bf16[1,6,16,1024]{3,2,1,0:T(8,128)(2,1)}, bf16[1,6,16,1024]{3,2,1,0:T(8,128)(2,1)S(1)}, u32[]{:S(2)}, u32[]{:S(2)}) collective-permute-start(bf16[1,6,16,1024]{3,2,1,0:T(8,128)(2,1)} %bitcast.21), channel_id=1, source_target_pairs={{0,8},{1,9},{2,10},{3,11},{4,12},{5,13},{6,14},{7,15},{8,0},{9,1},... | collective-permute-start | bytes 589832 | tf_op jit(solution)/shard_map/ppermute | solution.py:354
  14.5 10.9 %collective-permute-start.2 = (bf16[2,6,16,1024]{3,2,1,0:T(8,128)(2,1)S(1)}, bf16[2,6,16,1024]{3,2,1,0:T(8,128)(2,1)S(1)}, u32[]{:S(2)}, u32[]{:S(2)}) collective-permute-start(bf16[2,6,16,1024]{3,2,1,0:T(8,128)(2,1)S(1)} %pad_maximum_fusion.refs_0_.refs_4_), channel_id=1, source_target_pairs={{0,6},{1,7},{2,0},{3,1},{4,2},{5,3},{6,4},{7,5},{8,14},{9,15},{10,... | collective-permute-start | bytes 1179656 | tf_op jit(solution)/shard_map/ppermute | solution.py:356
  18.6 10.4 %collective-permute-start.1 = (bf16[2,6,16,1024]{3,2,1,0:T(8,128)(2,1)S(1)}, bf16[2,6,16,1024]{3,2,1,0:T(8,128)(2,1)S(1)}, u32[]{:S(2)}, u32[]{:S(2)}) collective-permute-start(bf16[2,6,16,1024]{3,2,1,0:T(8,128)(2,1)S(1)} %pad_maximum_fusion.refs_0_.refs_4_), channel_id=1, source_target_pairs={{0,2},{1,3},{2,4},{3,5},{4,6},{5,7},{6,0},{7,1},{8,10},{9,11},{10,... | collective-permute-start | bytes 1179656 | tf_op jit(solution)/shard_map/ppermute | solution.py:355
  19.2 19.6 %collective-permute-start.5 = (bf16[2,6,16,1024]{3,2,1,0:T(8,128)(2,1)S(1)}, bf16[2,6,16,1024]{3,2,1,0:T(8,128)(2,1)S(1)}, u32[]{:S(2)}, u32[]{:S(2)}) collective-permute-start(bf16[2,6,16,1024]{3,2,1,0:T(8,128)(2,1)S(1)} %pad_maximum_fusion.refs_0_.refs_4_), channel_id=1, source_target_pairs={{0,1},{1,0},{2,3},{3,2},{4,5},{5,4},{6,7},{7,6},{8,9},{9,8},{10,11... | collective-permute-start | bytes 1179656 | tf_op jit(solution)/shard_map/ppermute | solution.py:360
  25.4 6.7 %collective-permute-start.4 = (bf16[1,6,16,1024]{3,2,1,0:T(8,128)(2,1)S(1)}, bf16[1,6,16,1024]{3,2,1,0:T(8,128)(2,1)S(1)}, u32[]{:S(2)}, u32[]{:S(2)}) collective-permute-start(bf16[1,6,16,1024]{3,2,1,0:T(8,128)(2,1)S(1)} %slice.33), channel_id=1, source_target_pairs={{0,6},{1,7},{2,0},{3,1},{4,2},{5,3},{6,4},{7,5},{8,14},{9,15},{10,... | collective-permute-start | bytes 589832 | tf_op jit(solution)/shard_map/ppermute | solution.py:358
  29.0 5.9 %collective-permute-start.3 = (bf16[1,6,16,1024]{3,2,1,0:T(8,128)(2,1)S(1)}, bf16[1,6,16,1024]{3,2,1,0:T(8,128)(2,1)S(1)}, u32[]{:S(2)}, u32[]{:S(2)}) collective-permute-start(bf16[1,6,16,1024]{3,2,1,0:T(8,128)(2,1)S(1)} %slice.32), channel_id=1, source_target_pairs={{0,2},{1,3},{2,4},{3,5},{4,6},{5,7},{6,0},{7,1},{8,10},{9,11},{10,... | collective-permute-start | bytes 589832 | tf_op jit(solution)/shard_map/ppermute | solution.py:357
  29.0 9.8 %collective-permute-start.7 = (bf16[2,6,16,1024]{3,2,1,0:T(8,128)(2,1)S(1)}, bf16[2,6,16,1024]{3,2,1,0:T(8,128)(2,1)S(1)}, u32[]{:S(2)}, u32[]{:S(2)}) collective-permute-start(bf16[2,6,16,1024]{3,2,1,0:T(8,128)(2,1)S(1)} %collective-permute-done.2.refs_2_.refs_6_), channel_id=1, source_target_pairs={{0,1},{1,0},{2,3},{3,2},{4,5},{5,4},{6,7},{7,6},{8,9},{9,8},{10,11... | collective-permute-start | bytes 1179656 | tf_op jit(solution)/shard_map/ppermute | solution.py:360
  31.9 7.9 %collective-permute-start.6 = (bf16[2,6,16,1024]{3,2,1,0:T(8,128)(2,1)S(1)}, bf16[2,6,16,1024]{3,2,1,0:T(8,128)(2,1)S(1)}, u32[]{:S(2)}, u32[]{:S(2)}) collective-permute-start(bf16[2,6,16,1024]{3,2,1,0:T(8,128)(2,1)S(1)} %collective-permute-done.1.refs_1_.refs_5_), channel_id=1, source_target_pairs={{0,1},{1,0},{2,3},{3,2},{4,5},{5,4},{6,7},{7,6},{8,9},{9,8},{10,11... | collective-permute-start | bytes 1179656 | tf_op jit(solution)/shard_map/ppermute | solution.py:360
  32.2 6.7 %collective-permute-start.9 = (bf16[1,6,16,1024]{3,2,1,0:T(8,128)(2,1)S(1)}, bf16[1,6,16,1024]{3,2,1,0:T(8,128)(2,1)S(1)}, u32[]{:S(2)}, u32[]{:S(2)}) collective-permute-start(bf16[1,6,16,1024]{3,2,1,0:T(8,128)(2,1)S(1)} %collective-permute-done.4.refs_4_.refs_8_), channel_id=1, source_target_pairs={{0,1},{1,0},{2,3},{3,2},{4,5},{5,4},{6,7},{7,6},{8,9},{9,8},{10,11... | collective-permute-start | bytes 589832 | tf_op jit(solution)/shard_map/ppermute | solution.py:360
  34.9 4.9 %collective-permute-start.8 = (bf16[1,6,16,1024]{3,2,1,0:T(8,128)(2,1)S(1)}, bf16[1,6,16,1024]{3,2,1,0:T(8,128)(2,1)S(1)}, u32[]{:S(2)}, u32[]{:S(2)}) collective-permute-start(bf16[1,6,16,1024]{3,2,1,0:T(8,128)(2,1)S(1)} %collective-permute-done.3.refs_3_.refs_7_), channel_id=1, source_target_pairs={{0,1},{1,0},{2,3},{3,2},{4,5},{5,4},{6,7},{7,6},{8,9},{9,8},{10,11... | collective-permute-start | bytes 589832 | tf_op jit(solution)/shard_map/ppermute | solution.py:360
  41.7 91.4 %copy-start.1 = (f32[64,512]{1,0:T(8,128)S(1)}, f32[64,512]{1,0:T(8,128)}, u32[]{:S(2)}) copy-start(f32[64,512]{1,0:T(8,128)} %get-tuple-element.10.cs_ref.refs_1_) | copy-start | bytes 393220
  41.7 91.4 %copy-start.2 = (f32[64,512]{1,0:T(8,128)S(1)}, f32[64,512]{1,0:T(8,128)}, u32[]{:S(2)}) copy-start(f32[64,512]{1,0:T(8,128)} %get-tuple-element.11.cc_ref.refs_0_) | copy-start | bytes 393220
  41.7 91.4 %copy-start.3 = (f32[64,512]{1,0:T(8,128)S(1)}, f32[64,512]{1,0:T(8,128)}, u32[]{:S(2)}) copy-start(f32[64,512]{1,0:T(8,128)} %get-tuple-element.12.fs_ref.refs_3_) | copy-start | bytes 393220
  41.7 91.4 %copy-start.4 = (f32[64,512]{1,0:T(8,128)S(1)}, f32[64,512]{1,0:T(8,128)}, u32[]{:S(2)}) copy-start(f32[64,512]{1,0:T(8,128)} %get-tuple-element.13.fc_ref.refs_2_) | copy-start | bytes 393220
  41.8 91.4 %copy-start.5 = (f32[96,1]{1,0:T(8,128)S(1)}, f32[96,1]{1,0:T(8,128)}, u32[]{:S(2)}) copy-start(f32[96,1]{1,0:T(8,128)} %reshape.23.live_ref) | copy-start | bytes 1156
  41.8 3.7 %collective-permute-start.10 = (f32[64,256]{1,0:T(8,128)S(1)}, f32[64,256]{1,0:T(8,128)S(1)}, u32[]{:S(2)}, u32[]{:S(2)}) collective-permute-start(f32[64,256]{1,0:T(8,128)S(1)} %slice_select_fusion), channel_id=1, source_target_pairs={{0,16},{16,0},{32,48},{48,32},{64,80},{80,64},{96,112},{112,96},{1... | collective-permute-start | bytes 196616 | tf_op jit(solution)/shard_map/ppermute | solution.py:379
  45.5 5.0 %collective-permute-start.11 = (f32[64,256]{1,0:T(8,128)S(1)}, f32[64,256]{1,0:T(8,128)S(1)}, u32[]{:S(2)}, u32[]{:S(2)}) collective-permute-start(f32[64,256]{1,0:T(8,128)S(1)} %select_add_fusion), channel_id=1, source_target_pairs={{0,32},{16,48},{32,0},{48,16},{64,96},{80,112},{96,64},{112,80},{1... | collective-permute-start | bytes 196616 | tf_op jit(solution)/shard_map/ppermute | solution.py:379
  50.5 8.2 %collective-permute-start.12 = (f32[64,256]{1,0:T(8,128)S(1)}, f32[64,256]{1,0:T(8,128)S(1)}, u32[]{:S(2)}, u32[]{:S(2)}) collective-permute-start(f32[64,256]{1,0:T(8,128)S(1)} %add.246), channel_id=1, source_target_pairs={{0,64},{16,80},{32,96},{48,112},{64,0},{80,16},{96,32},{112,48},{1... | collective-permute-start | bytes 196616 | tf_op jit(solution)/shard_map/ppermute | solution.py:379
  58.7 4.7 %collective-permute-start.13 = (f32[64,256]{1,0:T(8,128)S(1)}, f32[64,256]{1,0:T(8,128)S(1)}, u32[]{:S(2)}, u32[]{:S(2)}) collective-permute-start(f32[64,256]{1,0:T(8,128)S(1)} %add.247), channel_id=1, source_target_pairs={{0,128},{16,144},{32,160},{48,176},{64,192},{80,208},{96,224},{112... | collective-permute-start | bytes 196616 | tf_op jit(solution)/shard_map/ppermute | solution.py:379
  63.4 3.5 %collective-permute-start.14 = (f32[64,256]{1,0:T(8,128)S(1)}, f32[64,256]{1,0:T(8,128)S(1)}, u32[]{:S(2)}, u32[]{:S(2)}) collective-permute-start(f32[64,256]{1,0:T(8,128)S(1)} %add.248), channel_id=1, source_target_pairs={{0,16},{16,0},{32,48},{48,32},{64,80},{80,64},{96,112},{112,96},{1... | collective-permute-start | bytes 196616 | tf_op jit(solution)/shard_map/ppermute | solution.py:379
  66.9 3.2 %collective-permute-start.15 = (f32[1,4,16,256]{3,2,1,0:T(8,128)S(1)}, f32[1,4,16,256]{3,2,1,0:T(8,128)S(1)}, u32[]{:S(2)}, u32[]{:S(2)}) collective-permute-start(f32[1,4,16,256]{3,2,1,0:T(8,128)S(1)} %bitcast.24), channel_id=1, source_target_pairs={{0,8},{1,9},{2,10},{3,11},{4,12},{5,13},{6,14},{7,15},{8,0},{9,1},... | collective-permute-start | bytes 196616 | tf_op jit(solution)/shard_map/ppermute | solution.py:354
  70.2 8.8 %collective-permute-start.17 = (f32[2,4,16,256]{3,2,1,0:T(8,128)S(1)}, f32[2,4,16,256]{3,2,1,0:T(8,128)S(1)}, u32[]{:S(2)}, u32[]{:S(2)}) collective-permute-start(f32[2,4,16,256]{3,2,1,0:T(8,128)S(1)} %pad_maximum_fusion.1.refs_0_), channel_id=1, source_target_pairs={{0,6},{1,7},{2,0},{3,1},{4,2},{5,3},{6,4},{7,5},{8,14},{9,15},{10,... | collective-permute-start | bytes 393224 | tf_op jit(solution)/shard_map/ppermute | solution.py:356
  70.3 9.9 %collective-permute-start.16 = (f32[2,4,16,256]{3,2,1,0:T(8,128)S(1)}, f32[2,4,16,256]{3,2,1,0:T(8,128)S(1)}, u32[]{:S(2)}, u32[]{:S(2)}) collective-permute-start(f32[2,4,16,256]{3,2,1,0:T(8,128)S(1)} %pad_maximum_fusion.1.refs_0_), channel_id=1, source_target_pairs={{0,2},{1,3},{2,4},{3,5},{4,6},{5,7},{6,0},{7,1},{8,10},{9,11},{10,... | collective-permute-start | bytes 393224 | tf_op jit(solution)/shard_map/ppermute | solution.py:355
  71.7 17.2 %collective-permute-start.20 = (f32[2,4,16,256]{3,2,1,0:T(8,128)S(1)}, f32[2,4,16,256]{3,2,1,0:T(8,128)S(1)}, u32[]{:S(2)}, u32[]{:S(2)}) collective-permute-start(f32[2,4,16,256]{3,2,1,0:T(8,128)S(1)} %pad_maximum_fusion.1.refs_0_), channel_id=1, source_target_pairs={{0,1},{1,0},{2,3},{3,2},{4,5},{5,4},{6,7},{7,6},{8,9},{9,8},{10,11... | collective-permute-start | bytes 393224 | tf_op jit(solution)/shard_map/ppermute | solution.py:360
  79.0 5.1 %collective-permute-start.19 = (f32[1,4,16,256]{3,2,1,0:T(8,128)S(1)}, f32[1,4,16,256]{3,2,1,0:T(8,128)S(1)}, u32[]{:S(2)}, u32[]{:S(2)}) collective-permute-start(f32[1,4,16,256]{3,2,1,0:T(8,128)S(1)} %slice.37), channel_id=1, source_target_pairs={{0,6},{1,7},{2,0},{3,1},{4,2},{5,3},{6,4},{7,5},{8,14},{9,15},{10,... | collective-permute-start | bytes 196616 | tf_op jit(solution)/shard_map/ppermute | solution.py:358
  80.2 6.0 %collective-permute-start.18 = (f32[1,4,16,256]{3,2,1,0:T(8,128)S(1)}, f32[1,4,16,256]{3,2,1,0:T(8,128)S(1)}, u32[]{:S(2)}, u32[]{:S(2)}) collective-permute-start(f32[1,4,16,256]{3,2,1,0:T(8,128)S(1)} %slice.36), channel_id=1, source_target_pairs={{0,2},{1,3},{2,4},{3,5},{4,6},{5,7},{6,0},{7,1},{8,10},{9,11},{10,... | collective-permute-start | bytes 196616 | tf_op jit(solution)/shard_map/ppermute | solution.py:357
  80.7 8.3 %collective-permute-start.22 = (f32[2,4,16,256]{3,2,1,0:T(8,128)S(1)}, f32[2,4,16,256]{3,2,1,0:T(8,128)S(1)}, u32[]{:S(2)}, u32[]{:S(2)}) collective-permute-start(f32[2,4,16,256]{3,2,1,0:T(8,128)S(1)} %collective-permute-done.17.refs_2_), channel_id=1, source_target_pairs={{0,1},{1,0},{2,3},{3,2},{4,5},{5,4},{6,7},{7,6},{8,9},{9,8},{10,11... | collective-permute-start | bytes 393224 | tf_op jit(solution)/shard_map/ppermute | solution.py:360
  84.1 5.7 %collective-permute-start.21 = (f32[2,4,16,256]{3,2,1,0:T(8,128)S(1)}, f32[2,4,16,256]{3,2,1,0:T(8,128)S(1)}, u32[]{:S(2)}, u32[]{:S(2)}) collective-permute-start(f32[2,4,16,256]{3,2,1,0:T(8,128)S(1)} %collective-permute-done.16.refs_1_), channel_id=1, source_target_pairs={{0,1},{1,0},{2,3},{3,2},{4,5},{5,4},{6,7},{7,6},{8,9},{9,8},{10,11... | collective-permute-start | bytes 393224 | tf_op jit(solution)/shard_map/ppermute | solution.py:360
  84.1 4.9 %collective-permute-start.24 = (f32[1,4,16,256]{3,2,1,0:T(8,128)S(1)}, f32[1,4,16,256]{3,2,1,0:T(8,128)S(1)}, u32[]{:S(2)}, u32[]{:S(2)}) collective-permute-start(f32[1,4,16,256]{3,2,1,0:T(8,128)S(1)} %collective-permute-done.19.refs_4_), channel_id=1, source_target_pairs={{0,1},{1,0},{2,3},{3,2},{4,5},{5,4},{6,7},{7,6},{8,9},{9,8},{10,11... | collective-permute-start | bytes 196616 | tf_op jit(solution)/shard_map/ppermute | solution.py:360
  86.2 3.6 %collective-permute-start.23 = (f32[1,4,16,256]{3,2,1,0:T(8,128)S(1)}, f32[1,4,16,256]{3,2,1,0:T(8,128)S(1)}, u32[]{:S(2)}, u32[]{:S(2)}) collective-permute-start(f32[1,4,16,256]{3,2,1,0:T(8,128)S(1)} %collective-permute-done.18.refs_3_), channel_id=1, source_target_pairs={{0,1},{1,0},{2,3},{3,2},{4,5},{5,4},{6,7},{7,6},{8,9},{9,8},{10,11... | collective-permute-start | bytes 196616 | tf_op jit(solution)/shard_map/ppermute | solution.py:360
